TPU v7x, 32 devices: a whole 2x2x4 slice. The times are simulated.
32 devices in a mesh: row: 8 (over y, x, core), col: 4 (over z).
Axes of the slice: x: 2, y: 2, z: 4, core: 2. Of those that a mesh axis runs over, the one named last changes fastest.
Arguments:
- multispectral: bfloat16 [2, 16384, 2048], P(None, 'row', 'col'), may hold values from -6 to 6
- hyperspectral: bfloat16 [96, 4096, 512], P(None, 'row', 'col'), may hold values from -6 to 6
- row_start: float32 [16384, 128], P(('row', 'col')), may hold values from -6 to 6
- col_factor: bfloat16 [2048, 128], P('col', 'row'), may hold values from -0.125 to 0.125
- band_factor: float32 [96, 128], replicated, may hold values from -2 to 2
- response: float32 [2, 96], replicated, may hold values from 0.2 to 1
- blur_taps: float32 [9], replicated, may hold values from 0.2 to 1
- offsets: int32 [9], replicated, may hold values from -8 to 8, as said below
Outputs:
- row_factor: float32 [16384, 128], P(('row', 'col'))
- residual: float32 [16384, 128], P(('row', 'col'))
Inputs may be any that keep to these rules, and one draw needn't show every extreme that they name: 9 distinct offsets; -8 and 8 are always among them.
All inputs are finite; a program needn't handle non-finite values.
Results may differ from a plain program's by a relative error of at most 0.0023.
Values may be sent and summed in bfloat16 or wider, within the bound.
No kernel may reach another device: no remote copies, remote signals or barrier semaphores. Data moves between devices by JAX's collectives and lax.ppermute only.
A program may use at most 128 MiB of HBM per device.

v0:
```python
import jax
import jax.numpy as jnp
from jax import lax
from jax.sharding import PartitionSpec as P

DEC = 4
W = 8
ITERS = 4


RIDGE_TERM = 0.1
FULL_PRECISION = lax.Precision.HIGHEST


def extended(cells, sides, width):
    for axis, dim in sides:
        count = lax.axis_size(axis)
        head = lax.slice_in_dim(cells, 0, width, axis=dim)
        tail = lax.slice_in_dim(cells, cells.shape[dim] - width, cells.shape[dim], axis=dim)
        cells = jnp.concatenate(
            [
                lax.ppermute(tail, axis, [(i, (i + 1) % count) for i in range(count)]),
                cells,
                lax.ppermute(head, axis, [((i + 1) % count, i) for i in range(count)]),
            ],
            axis=dim,
        )
    return cells


def down_matrix(weights, offsets, rows_out, rows_in):
    outer = lax.broadcasted_iota(jnp.int32, (rows_out, rows_in), 0)
    inner = lax.broadcasted_iota(jnp.int32, (rows_out, rows_in), 1)
    total = jnp.zeros((rows_out, rows_in), jnp.float32)
    for number in range(weights.shape[0]):
        target = DEC * outer + offsets[number] + W
        total = total + jnp.where(inner == target, weights[number], jnp.float32(0.0))
    return total


def up_matrix(weights, offsets, rows_in, low_margin):
    rows_out = (rows_in - 2 * low_margin) * DEC
    outer = lax.broadcasted_iota(jnp.int32, (rows_out, rows_in), 0)
    inner = lax.broadcasted_iota(jnp.int32, (rows_out, rows_in), 1)
    total = jnp.zeros((rows_out, rows_in), jnp.float32)
    for number in range(weights.shape[0]):
        target = outer + DEC * low_margin - offsets[number]
        total = total + jnp.where(DEC * inner == target, weights[number], jnp.float32(0.0))
    return total


def apply_band(matrix, values):
    return jnp.dot(matrix, values.astype(jnp.float32), precision=FULL_PRECISION)


def body(
    multispectral, hyperspectral, row_start, col_factor, band_factor, response, blur_taps, offsets
):
    low_reach = (W + DEC - 1) // DEC
    columns = lax.all_gather(col_factor, "row", axis=1, tiled=True)
    column_wide = extended(columns, (("col", 0),), W)
    column_down = down_matrix(blur_taps, offsets, columns.shape[0] // DEC, column_wide.shape[0])
    coarse_columns = apply_band(column_down, column_wide)
    merged = jnp.dot(response, band_factor, precision=FULL_PRECISION)
    multi_pairs = (merged[:, None, :] * columns.astype(jnp.float32)[None, :, :]).astype(
        jnp.bfloat16
    )
    hyper_pairs = (band_factor[:, None, :] * coarse_columns[None, :, :]).astype(jnp.bfloat16)
    multi_part = jnp.einsum(
        "kij,kjr->ir", multispectral, multi_pairs, preferred_element_type=jnp.float32
    )
    hyper_part = jnp.einsum(
        "kij,kjr->ir", hyperspectral, hyper_pairs, preferred_element_type=jnp.float32
    )
    column_part = jnp.einsum("jr,js->rs", columns, columns, preferred_element_type=jnp.float32)
    coarse_part = jnp.einsum("jr,js->rs", coarse_columns, coarse_columns, precision=FULL_PRECISION)
    column_gram, coarse_gram = lax.psum((column_part, coarse_part), "col")
    band_gram = jnp.dot(band_factor.T, band_factor, precision=FULL_PRECISION)
    merged_gram = jnp.dot(merged.T, merged, precision=FULL_PRECISION)
    hyper_gram = coarse_gram * band_gram
    multi_gram = column_gram * merged_gram
    multi_sums, hyper_sums = lax.psum((multi_part, hyper_part), "col")
    start_rows = lax.all_gather(row_start, "col", axis=0, tiled=True)

    def fine_rim(values, breadth):
        return extended(values, (("row", 0),), breadth)

    def inner_sum(first_field, second_field):
        return lax.psum(jnp.sum(first_field * second_field), "row")

    fine_rows = start_rows.shape[0]
    coarse_rows = fine_rows // DEC
    lifting = up_matrix(blur_taps, offsets, coarse_rows + 2 * low_reach, low_reach)
    lowering = down_matrix(
        blur_taps, offsets, coarse_rows + 2 * low_reach, fine_rows + 2 * (W + DEC * low_reach)
    )

    def operate(values):
        fine_wide = fine_rim(values, W + DEC * low_reach)
        coarse_wide = apply_band(lowering, fine_wide)
        restored = apply_band(lifting, coarse_wide)
        return (
            jnp.dot(restored, hyper_gram, precision=FULL_PRECISION)
            + jnp.dot(values, multi_gram, precision=FULL_PRECISION)
            + RIDGE_TERM * values
        )

    right_side = apply_band(lifting, extended(hyper_sums, (("row", 0),), low_reach)) + multi_sums
    solution = start_rows
    residual = right_side - operate(solution)
    direction = residual
    norm_now = inner_sum(residual, residual)
    for iteration in range(ITERS):
        mapped = operate(direction)
        step_size = norm_now / inner_sum(direction, mapped)
        solution = solution + step_size * direction
        residual = residual - step_size * mapped
        norm_next = inner_sum(residual, residual)
        direction = residual + norm_next / norm_now * direction
        norm_now = norm_next
    portion = solution.shape[0] // lax.axis_size("col")
    corner = lax.axis_index("col") * portion
    solution = lax.dynamic_slice_in_dim(solution, corner, portion, 0)
    residual = lax.dynamic_slice_in_dim(residual, corner, portion, 0)
    return (solution, residual)


def solution(mesh):
    in_specs = (
        P(None, "row", "col"),
        P(None, "row", "col"),
        P(("row", "col"), None),
        P("col", "row"),
        P(),
        P(),
        P(),
        P(),
    )
    out_specs = (P(("row", "col"), None), P(("row", "col"), None))
    return jax.shard_map(body, mesh=mesh, in_specs=in_specs, out_specs=out_specs, check_vma=False)
```

profile of v0, /device:TPU:0, one launch (start us, length us, event | category | flops | bytes accessed | tf_op | source)
XLA Modules:
  0.0 479.1 jit_solution(14813871930401068489)
XLA Ops:
  7.2 10.8 %all_gather.7 = bf16[512,128]{0,1:T(8,128)(2,1)S(1)} all-gather(bf16[512,16]{0,1:T(8,128)(2,1)} %param.11), channel_id=1, replica_groups=mesh['row'=8,'col'=4] {'row'}, dimensions={1}, use_global_device_ids=true | all-gather | bytes 147456 | tf_op jit(solution)/shard_map/all_gather | solution.py:60
  32.0 4.5 convolution_bitcast_fusion.1
  37.1 6.4 %fusion.50 = f32[128,128]{1,0:T(8,128)S(1)} fusion(bf16[8,128]{0,1:T(8,128)(2,1)S(1)} %collective-permute-done.1, bf16[512,128]{0,1:T(8,128)(2,1)S(1)} %all_gather.7, bf16[8,128]{0,1:T(8,128)(2,1)S(1)} %collective-permute-done, f32[]{:T(128)} %bitcast.17, s32[128]{0:T(128)S(1)} %get-tuple-element.69, f32[]{:T(128)} %bitcast.15, ...), kind=kOutput, calls=%fused_computation.87 | convolution fusion | flops 105971712 | bytes 205348 | tf_op jit(solution)/shard_map/dot_general | solution.py:53
  44.5 8.2 %fusion.14 = f32[512,128]{0,1:T(8,128)} fusion(bf16[96,512,128]{2,1,0:T(8,128)(2,1)} %param.9, f32[128,128]{0,1:T(8,128)S(1)} %copy.10, f32[96,128]{1,0:T(8,128)S(1)} %copy-done.4), kind=kOutput, calls=%fused_computation.33 | convolution fusion | flops 1613758464 | bytes 12959744 | tf_op jit(solution)/shard_map/kij,kjr->ir/dot_general | solution.py:72
  64.4 52.8 %all-reduce.4.cloned.1.call-done = (f32[128,128]{1,0:T(8,128)}, f32[128,128]{1,0:T(8,128)}, f32[2048,128]{1,0:T(8,128)}, f32[512,128]{0,1:T(8,128)}) async-done(((f32[128,128]{1,0:T(8,128)}, f32[128,128]{1,0:T(8,128)}, f32[2048,128]{1,0:T(8,128)}, f32[512,128]{0,1:T(8,128)}), (f32[128,128]{1,0:T(8,128)}, f32[128,128]{1,0:T(8,128)}, f32[2048,128]{1,0:T(8,128)}, ...) | async-done | bytes 1441808 | tf_op jit(solution)/shard_map/psum | solution.py:77
  119.3 26.5 %all-gather.2.cloned.1.call-done = f32[2048,128]{1,0:T(8,128)} async-done(((f32[512,128]{1,0:T(8,128)}), f32[2048,128]{1,0:T(8,128)}) %all-gather.2.cloned.1.call-update) | async-done | bytes 1048592 | tf_op jit(solution)/shard_map/all_gather | solution.py:83
  146.5 2.6 collective-permute-start.5
  150.3 2.8 collective-permute-start.3
  153.1 15.5 %fusion.13 = f32[516,128]{1,0:T(8,128)S(1)} fusion(f32[]{:T(128)} %bitcast.17, s32[516]{0:T(1024)S(1)} %get-tuple-element.53, f32[]{:T(128)} %bitcast.15, s32[516]{0:T(1024)S(1)} %get-tuple-element.54, f32[]{:T(128)} %bitcast.13, s32[516]{0:T(1024)S(1)} %get-tuple-element.55, f32[]{:T(128)} %bitcast.11, s32[516]{0:T(1024)S(1)} %get-tuple-element.56, ...), kind=kOutput, calls=%fused_computation.32 | convolution fusion | flops 1676995840 | bytes 1347764 | tf_op jit(solution)/shard_map/dot_general | solution.py:53
  168.7 15.3 %fusion.19 = f32[2048,128]{1,0:T(8,128)S(1)} fusion(f32[516,128]{1,0:T(8,128)S(1)} %fusion.13, f32[]{:T(128)} %bitcast.17, f32[]{:T(128)} %bitcast.15, f32[]{:T(128)} %bitcast.13, f32[]{:T(128)} %bitcast.11, f32[]{:T(128)} %bitcast.9, f32[]{:T(128)} %bitcast.7, f32[]{:T(128)} %bitcast.5, f32[]{:T(128)} %bitcast.3, f32[]{:T(128)} %bitcast.1, ...), kind=kOutput, calls=%fused_computation.40 | convolution fusion | flops 1650671616 | bytes 1388596 | tf_op jit(solution)/shard_map/dot_general | solution.py:53
  186.1 15.0 %fusion.3 = f32[2048,128]{1,0:T(8,128)S(1)} fusion(f32[2048,128]{1,0:T(8,128)S(1)} %fusion.5, f32[2048,128]{1,0:T(8,128)S(1)} %copy-done.6, f32[]{:T(128)} %bitcast.17, f32[]{:T(128)} %bitcast.15, f32[]{:T(128)} %bitcast.13, f32[]{:T(128)} %bitcast.11, f32[]{:T(128)} %bitcast.9, f32[]{:T(128)} %bitcast.7, f32[]{:T(128)} %bitcast.5, f32[]{:T(128)} %bitcast.3, ...), kind=kOutput, calls=%fused_computation.18 | convolution fusion | flops 1651328000 | bytes 3485748 | tf_op jit(solution)/shard_map/dot_general | solution.py:53
  205.2 14.3 %fusion.12 = f32[516,128]{1,0:T(8,128)S(1)} fusion(f32[]{:T(128)} %bitcast.17, s32[516]{0:T(1024)S(1)} %get-tuple-element.53, f32[]{:T(128)} %bitcast.15, s32[516]{0:T(1024)S(1)} %get-tuple-element.54, f32[]{:T(128)} %bitcast.13, s32[516]{0:T(1024)S(1)} %get-tuple-element.55, f32[]{:T(128)} %bitcast.11, s32[516]{0:T(1024)S(1)} %get-tuple-element.56, ...), kind=kOutput, calls=%fused_computation.31 | convolution fusion | flops 1676995840 | bytes 1347764 | tf_op jit(solution)/shard_map/dot_general | solution.py:53
  219.5 15.2 %fusion.18 = f32[2048,128]{1,0:T(8,128)S(1)} fusion(f32[516,128]{1,0:T(8,128)S(1)} %fusion.12, f32[]{:T(128)} %bitcast.17, f32[]{:T(128)} %bitcast.15, f32[]{:T(128)} %bitcast.13, f32[]{:T(128)} %bitcast.11, f32[]{:T(128)} %bitcast.9, f32[]{:T(128)} %bitcast.7, f32[]{:T(128)} %bitcast.5, f32[]{:T(128)} %bitcast.3, f32[]{:T(128)} %bitcast.1, ...), kind=kOutput, calls=%fused_computation.39 | convolution fusion | flops 1650671616 | bytes 1388596 | tf_op jit(solution)/shard_map/dot_general | solution.py:53
  237.4 15.0 %all-reduce = (f32[]{:T(128)}, f32[]{:T(128)}) all-reduce(f32[]{:T(128)} %get-tuple-element.3, f32[]{:T(128)} %get-tuple-element.2), channel_id=1, replica_groups=mesh['row'=8,'col'=4] {'row'}, use_global_device_ids=true, to_apply=%region_5.6 | all-reduce | flops 2 | bytes 16 | tf_op jit(solution)/shard_map/psum | solution.py:89
  254.6 12.4 %psum.90 = f32[]{:T(128)} all-reduce(f32[]{:T(128)} %multiply_reduce_fusion.5), channel_id=1, replica_groups=mesh['row'=8,'col'=4] {'row'}, use_global_device_ids=true, to_apply=%region_9.10 | all-reduce | flops 1 | bytes 8 | tf_op jit(solution)/shard_map/psum | solution.py:89
  268.6 2.8 collective-permute-start.9
  272.8 14.3 %fusion.11 = f32[516,128]{1,0:T(8,128)S(1)} fusion(f32[]{:T(128)} %bitcast.17, s32[516]{0:T(1024)S(1)} %get-tuple-element.53, f32[]{:T(128)} %bitcast.15, s32[516]{0:T(1024)S(1)} %get-tuple-element.54, f32[]{:T(128)} %bitcast.13, s32[516]{0:T(1024)S(1)} %get-tuple-element.55, f32[]{:T(128)} %bitcast.11, s32[516]{0:T(1024)S(1)} %get-tuple-element.56, ...), kind=kOutput, calls=%fused_computation.30 | convolution fusion | flops 1676995840 | bytes 1347764 | tf_op jit(solution)/shard_map/dot_general | solution.py:53
  287.1 15.0 %fusion.17 = f32[2048,128]{1,0:T(8,128)S(1)} fusion(f32[516,128]{1,0:T(8,128)S(1)} %fusion.11, f32[]{:T(128)} %bitcast.17, f32[]{:T(128)} %bitcast.15, f32[]{:T(128)} %bitcast.13, f32[]{:T(128)} %bitcast.11, f32[]{:T(128)} %bitcast.9, f32[]{:T(128)} %bitcast.7, f32[]{:T(128)} %bitcast.5, f32[]{:T(128)} %bitcast.3, f32[]{:T(128)} %bitcast.1, ...), kind=kOutput, calls=%fused_computation.38 | convolution fusion | flops 1650671616 | bytes 1388596 | tf_op jit(solution)/shard_map/dot_general | solution.py:53
  303.1 2.7 multiply_reduce_fusion.4
  305.7 15.0 %psum.91 = f32[]{:T(128)} all-reduce(f32[]{:T(128)} %get-tuple-element.47), channel_id=1, replica_groups=mesh['row'=8,'col'=4] {'row'}, use_global_device_ids=true, to_apply=%region_11.12 | all-reduce | flops 1 | bytes 8 | tf_op jit(solution)/shard_map/psum | solution.py:89
  322.1 3.1 multiply_reduce_fusion.3
  325.2 12.4 %psum.92 = f32[]{:T(128)} all-reduce(f32[]{:T(128)} %get-tuple-element.12), channel_id=1, replica_groups=mesh['row'=8,'col'=4] {'row'}, use_global_device_ids=true, to_apply=%region_13.14 | all-reduce | flops 1 | bytes 8 | tf_op jit(solution)/shard_map/psum | solution.py:89
  340.4 3.0 collective-permute-start.11
  344.8 14.3 %fusion.10 = f32[516,128]{1,0:T(8,128)S(1)} fusion(f32[]{:T(128)} %bitcast.17, s32[516]{0:T(1024)S(1)} %get-tuple-element.53, f32[]{:T(128)} %bitcast.15, s32[516]{0:T(1024)S(1)} %get-tuple-element.54, f32[]{:T(128)} %bitcast.13, s32[516]{0:T(1024)S(1)} %get-tuple-element.55, f32[]{:T(128)} %bitcast.11, s32[516]{0:T(1024)S(1)} %get-tuple-element.56, ...), kind=kOutput, calls=%fused_computation.29 | convolution fusion | flops 1676995840 | bytes 1347764 | tf_op jit(solution)/shard_map/dot_general | solution.py:53
  359.1 14.9 %fusion.16 = f32[2048,128]{1,0:T(8,128)S(1)} fusion(f32[516,128]{1,0:T(8,128)S(1)} %fusion.10, f32[]{:T(128)} %bitcast.17, f32[]{:T(128)} %bitcast.15, f32[]{:T(128)} %bitcast.13, f32[]{:T(128)} %bitcast.11, f32[]{:T(128)} %bitcast.9, f32[]{:T(128)} %bitcast.7, f32[]{:T(128)} %bitcast.5, f32[]{:T(128)} %bitcast.3, f32[]{:T(128)} %bitcast.1, ...), kind=kOutput, calls=%fused_computation.37 | convolution fusion | flops 1650671616 | bytes 1388596 | tf_op jit(solution)/shard_map/dot_general | solution.py:53
  377.7 15.0 %psum.93 = f32[]{:T(128)} all-reduce(f32[]{:T(128)} %get-tuple-element.49), channel_id=1, replica_groups=mesh['row'=8,'col'=4] {'row'}, use_global_device_ids=true, to_apply=%region_15.16 | all-reduce | flops 1 | bytes 8 | tf_op jit(solution)/shard_map/psum | solution.py:89
  394.0 3.4 multiply_reduce_fusion.1
  397.4 12.4 %psum.94 = f32[]{:T(128)} all-reduce(f32[]{:T(128)} %get-tuple-element.10), channel_id=1, replica_groups=mesh['row'=8,'col'=4] {'row'}, use_global_device_ids=true, to_apply=%region_17.18 | all-reduce | flops 1 | bytes 8 | tf_op jit(solution)/shard_map/psum | solution.py:89
  413.5 2.8 collective-permute-start.13
  417.7 15.5 %fusion.9 = f32[516,128]{1,0:T(8,128)S(1)} fusion(f32[]{:T(128)} %bitcast.17, s32[516]{0:T(1024)S(1)} %get-tuple-element.53, f32[]{:T(128)} %bitcast.15, s32[516]{0:T(1024)S(1)} %get-tuple-element.54, f32[]{:T(128)} %bitcast.13, s32[516]{0:T(1024)S(1)} %get-tuple-element.55, f32[]{:T(128)} %bitcast.11, s32[516]{0:T(1024)S(1)} %get-tuple-element.56, ...), kind=kOutput, calls=%fused_computation.28 | convolution fusion | flops 1676995840 | bytes 1347764 | tf_op jit(solution)/shard_map/dot_general | solution.py:53
  433.3 15.1 %fusion.15 = f32[2048,128]{1,0:T(8,128)S(1)} fusion(f32[516,128]{1,0:T(8,128)S(1)} %fusion.9, f32[]{:T(128)} %bitcast.17, f32[]{:T(128)} %bitcast.15, f32[]{:T(128)} %bitcast.13, f32[]{:T(128)} %bitcast.11, f32[]{:T(128)} %bitcast.9, f32[]{:T(128)} %bitcast.7, f32[]{:T(128)} %bitcast.5, f32[]{:T(128)} %bitcast.3, f32[]{:T(128)} %bitcast.1, ...), kind=kOutput, calls=%fused_computation.36 | convolution fusion | flops 1650671616 | bytes 1388596 | tf_op jit(solution)/shard_map/dot_general | solution.py:53
  452.0 15.0 %psum.95 = f32[]{:T(128)} all-reduce(f32[]{:T(128)} %get-tuple-element.51), channel_id=1, replica_groups=mesh['row'=8,'col'=4] {'row'}, use_global_device_ids=true, to_apply=%region_19.20 | all-reduce | flops 1 | bytes 8 | tf_op jit(solution)/shard_map/psum | solution.py:89
  (88 shorter events, 60.8 us)
Async XLA Ops:
  7.2 23.9 %copy-start = (f32[2,96]{1,0:T(2,128)S(1)}, f32[2,96]{1,0:T(2,128)}, u32[]{:S(2)}) copy-start(f32[2,96]{1,0:T(2,128)} %param.13) | copy-start | bytes 2308
  7.2 110.0 %all-reduce.4.cloned.1.call-start = ((), (), s32[]{:S(2)}) async-start(), calls=%async_computation.1 | async-start | bytes 2883584 | tf_op jit(solution)/shard_map/psum | solution.py:77
  18.2 18.9 %collective-permute-start = (bf16[8,128]{0,1:T(8,128)(2,1)S(1)}, bf16[8,128]{0,1:T(8,128)(2,1)S(1)}, u32[]{:S(2)}, u32[]{:S(2)}) collective-permute-start(bf16[8,128]{0,1:T(8,128)(2,1)S(1)} %get-tuple-element.26), channel_id=1, source_target_pairs={{0,1},{1,2},{2,3},{3,0},{4,5},{5,6},{6,7},{7,4},{8,9},{9,10},{10,1... | collective-permute-start | bytes 6152 | tf_op jit(solution)/shard_map/ppermute | solution.py:22
  19.7 17.4 %collective-permute-start.1 = (bf16[8,128]{0,1:T(8,128)(2,1)S(1)}, bf16[8,128]{0,1:T(8,128)(2,1)S(1)}, u32[]{:S(2)}, u32[]{:S(2)}) collective-permute-start(bf16[8,128]{0,1:T(8,128)(2,1)S(1)} %get-tuple-element.27), channel_id=1, source_target_pairs={{1,0},{2,1},{3,2},{0,3},{5,4},{6,5},{7,6},{4,7},{9,8},{10,9},{11,1... | collective-permute-start | bytes 6152 | tf_op jit(solution)/shard_map/ppermute | solution.py:24
  32.0 12.5 %copy-start.4 = (f32[96,128]{1,0:T(8,128)S(1)}, f32[96,128]{1,0:T(8,128)}, u32[]{:S(2)}) copy-start(f32[96,128]{1,0:T(8,128)} %param.12) | copy-start | bytes 147460
  52.7 93.1 %all-gather.2.cloned.1.call-start = ((), (), s32[]{:S(2)}) async-start(), calls=%async_computation | async-start | bytes 1310720 | tf_op jit(solution)/shard_map/all_gather | solution.py:83
  146.5 6.6 %collective-permute-start.4 = (f32[16,128]{1,0:T(8,128)S(1)}, f32[16,128]{1,0:T(8,128)S(1)}, u32[]{:S(2)}, u32[]{:S(2)}) collective-permute-start(f32[16,128]{1,0:T(8,128)S(1)} %get-tuple-element.22), channel_id=1, source_target_pairs={{0,4},{4,8},{8,12},{12,16},{16,20},{20,24},{24,28},{28,0},{1,5},{5... | collective-permute-start | bytes 24584 | tf_op jit(solution)/shard_map/ppermute | solution.py:22
  146.5 6.6 %collective-permute-start.5 = (f32[16,128]{1,0:T(8,128)S(1)}, f32[16,128]{1,0:T(8,128)S(1)}, u32[]{:S(2)}, u32[]{:S(2)}) collective-permute-start(f32[16,128]{1,0:T(8,128)S(1)} %get-tuple-element.23), channel_id=1, source_target_pairs={{4,0},{8,4},{12,8},{16,12},{20,16},{24,20},{28,24},{0,28},{5,1},{9... | collective-permute-start | bytes 24584 | tf_op jit(solution)/shard_map/ppermute | solution.py:24
  150.3 35.7 %collective-permute-start.2 = (f32[2,128]{0,1:T(8,128)S(1)}, f32[2,128]{0,1:T(8,128)S(1)}, u32[]{:S(2)}, u32[]{:S(2)}) collective-permute-start(f32[2,128]{0,1:T(8,128)S(1)} %get-tuple-element.24), channel_id=1, source_target_pairs={{0,4},{4,8},{8,12},{12,16},{16,20},{20,24},{24,28},{28,0},{1,5},{5... | collective-permute-start | bytes 3080 | tf_op jit(solution)/shard_map/ppermute | solution.py:22
  150.3 35.7 %collective-permute-start.3 = (f32[2,128]{0,1:T(8,128)S(1)}, f32[2,128]{0,1:T(8,128)S(1)}, u32[]{:S(2)}, u32[]{:S(2)}) collective-permute-start(f32[2,128]{0,1:T(8,128)S(1)} %get-tuple-element.25), channel_id=1, source_target_pairs={{4,0},{8,4},{12,8},{16,12},{20,16},{24,20},{28,24},{0,28},{5,1},{9... | collective-permute-start | bytes 3080 | tf_op jit(solution)/shard_map/ppermute | solution.py:24
  168.7 16.3 %copy-start.3 = (f32[2048,128]{1,0:T(8,128)S(1)}, f32[2048,128]{1,0:T(8,128)}, u32[]{:S(2)}) copy-start(f32[2048,128]{1,0:T(8,128)} %all-gather.2.cloned.1.call-done) | copy-start | bytes 3145732
  183.9 2.1 copy-start.5
  183.9 2.1 copy-start.6
  201.1 4.1 collective-permute-start.6
  201.2 4.0 collective-permute-start.7
  268.6 4.0 collective-permute-start.8
  268.6 4.1 collective-permute-start.9
  340.4 4.0 collective-permute-start.10
  340.4 4.4 collective-permute-start.11
  412.6 1.0 copy-start.1
  413.5 4.0 collective-permute-start.12
  413.5 4.2 collective-permute-start.13
  433.3 16.1 %copy-start.2 = (f32[2048,128]{1,0:T(8,128)S(1)}, f32[2048,128]{1,0:T(8,128)}, u32[]{:S(2)}) copy-start(f32[2048,128]{1,0:T(8,128)} %copy-done.1) | copy-start | bytes 3145732
Sparse Core Ops, SparseCore 0:
  52.8 64.3 all-reduce.3
  118.8 26.9 all-gather.1
where the time goes:
time: 485 us; the launch traced here: 479 us
  matrix products  204 us (42%)
  blocking collectives  108 us (22%)
  waiting for transfers between devices  85.5 us (18%)
  other arithmetic  30.3 us (6%)
  between operations  24.1 us (5%)
  starting transfers between devices  20.8 us (4%)
  local copies, waits for them, and re-layouts  6.18 us (1%)
    dot_general x12, matrix products, apply_band(): return jnp.dot(matrix, values.astype(jnp.float32), precision=FULL_PRECISION)  171 us
    psum x7, blocking collectives, inner_sum(): return lax.psum(jnp.sum(first_field * second_field), 'row')  97.3 us
    psum x1, waiting for transfers between devices, body(): column_gram, coarse_gram = lax.psum((column_part, coarse_part), 'col')  52.8 us
    all_gather x1, waiting for transfers between devices, body(): start_rows = lax.all_gather(row_start, 'col', axis=0, tiled=True)  26.5 us
    ppermute x7, starting transfers between devices, extended(): lax.ppermute(head, axis, [((i + 1) % count, i) for i in range(count)])  18.9 us
    add x10, other arithmetic, down_matrix(): target = DEC * outer + offsets[number] + W  10.8 us
    all_gather x1, blocking collectives, body(): columns = lax.all_gather(col_factor, 'row', axis=1, tiled=True)  10.8 us
    dot_general x5, matrix products, operate(): jnp.dot(values, multi_gram, precision=FULL_PRECISION)  10.7 us
  transfers between devices with their start and end apart: 16, of which 9 were waited for; matrix products, arithmetic and copies ran while one was open for 13% of the time, Pallas kernels for 0%

commit v1 on v0

v1 whole, which is shorter than its diff:
```python
import functools

import jax
import jax.numpy as jnp
from jax import lax
from jax.experimental import pallas as pl
from jax.experimental.pallas import tpu as pltpu
from jax.sharding import PartitionSpec as P

DEC = 4
W = 8
REACH = W // DEC
ITERS = 4
RIDGE_TERM = 0.1
FULL_PRECISION = lax.Precision.HIGHEST
BOTH = ("row", "col")
ROWS_A = 256
BANDS_B = 16
RIM = 24
RIM_MULTI = 16
PAIRS = [(i, j) for i in range(ITERS + 1) for j in range(i, ITERS + 1)]
TRUST = 2.0e4
VMEM_LIMIT = 48 * 1024 * 1024


def params():
    return pltpu.CompilerParams(vmem_limit_bytes=VMEM_LIMIT)


def whole(shape):
    return pl.BlockSpec(shape, lambda *_: (0,) * len(shape))


SMEM = pl.BlockSpec(memory_space=pltpu.SMEM)


def multi_kernel(columns, band, response, image, out, gram, pairs):
    depth = columns.shape[0]

    @pl.when(pl.program_id(0) == 0)
    def _():
        wide = columns[...].astype(jnp.float32)
        merged = jnp.dot(
            response[...], band[...], precision=FULL_PRECISION, preferred_element_type=jnp.float32
        )
        for k in range(2):
            pairs[k * depth : (k + 1) * depth, :] = (merged[k : k + 1, :] * wide).astype(jnp.bfloat16)
        gram[...] = lax.dot_general(
            columns[...], columns[...], (((0,), (0,)), ((), ())), preferred_element_type=jnp.float32
        )

    total = jnp.dot(image[0], pairs[:depth, :], preferred_element_type=jnp.float32)
    total += jnp.dot(image[1], pairs[depth:, :], preferred_element_type=jnp.float32)
    out[...] = total.astype(jnp.bfloat16)


def contract_multi(columns, band, response, image):
    bands, rows, depth = image.shape
    rank = columns.shape[1]
    return pl.pallas_call(
        multi_kernel,
        grid=(rows // ROWS_A,),
        in_specs=[
            whole(columns.shape),
            whole(band.shape),
            whole(response.shape),
            pl.BlockSpec((bands, ROWS_A, depth), lambda i: (0, i, 0)),
        ],
        out_specs=[pl.BlockSpec((ROWS_A, rank), lambda i: (i, 0)), whole((rank, rank))],
        out_shape=[
            jax.ShapeDtypeStruct((rows, rank), jnp.bfloat16),
            jax.ShapeDtypeStruct((rank, rank), jnp.float32),
        ],
        scratch_shapes=[pltpu.VMEM((bands * depth, rank), jnp.bfloat16)],
        compiler_params=params(),
        name="contract_multi",
    )(columns, band, response, image)


def coarse_kernel(taps, columns, before, after, coarse, gram, wide):
    edge = before.shape[0]
    size = columns.shape[0]
    wide[:edge, :] = before[...].astype(jnp.float32)
    wide[edge : edge + size, :] = columns[...].astype(jnp.float32)
    wide[edge + size :, :] = after[...].astype(jnp.float32)
    total = jnp.zeros(coarse.shape, jnp.float32)
    for offset in range(-W, W + 1):
        total += taps[offset + W] * wide[pl.ds(edge + offset, size // DEC, stride=DEC), :]
    coarse[...] = total
    gram[...] = lax.dot_general(
        total, total, (((0,), (0,)), ((), ())), precision=FULL_PRECISION,
        preferred_element_type=jnp.float32,
    )


def coarsen(taps, columns, before, after):
    size, rank = columns.shape
    return pl.pallas_call(
        coarse_kernel,
        in_specs=[SMEM] + [whole(a.shape) for a in (columns, before, after)],
        out_specs=[whole((size // DEC, rank)), whole((rank, rank))],
        out_shape=[
            jax.ShapeDtypeStruct((size // DEC, rank), jnp.float32),
            jax.ShapeDtypeStruct((rank, rank), jnp.float32),
        ],
        scratch_shapes=[pltpu.VMEM((size + 2 * before.shape[0], rank), jnp.float32)],
        compiler_params=params(),
        name="coarsen",
    )(taps, columns, before, after)


def hyper_kernel(coarse, band, image, out, total):
    step = pl.program_id(0)
    field = coarse[...]
    pairs = jnp.concatenate(
        [(band[k : k + 1, :] * field).astype(jnp.bfloat16) for k in range(BANDS_B)], axis=0
    )
    pixels = jnp.concatenate([image[k] for k in range(BANDS_B)], axis=1)
    part = jnp.dot(pixels, pairs, preferred_element_type=jnp.float32)

    @pl.when(step == 0)
    def _():
        total[...] = part

    @pl.when(step > 0)
    def _():
        total[...] += part

    @pl.when(step == pl.num_programs(0) - 1)
    def _():
        out[...] = total[...].astype(jnp.bfloat16)


def contract_hyper(coarse, band, image):
    bands, rows, depth = image.shape
    rank = coarse.shape[1]
    return pl.pallas_call(
        hyper_kernel,
        grid=(bands // BANDS_B,),
        in_specs=[
            whole(coarse.shape),
            pl.BlockSpec((BANDS_B, rank), lambda i: (i, 0)),
            pl.BlockSpec((BANDS_B, rows, depth), lambda i: (i, 0, 0)),
        ],
        out_specs=whole((rows, rank)),
        out_shape=jax.ShapeDtypeStruct((rows, rank), jnp.bfloat16),
        scratch_shapes=[pltpu.VMEM((rows, rank), jnp.float32)],
        compiler_params=params(),
        name="contract_hyper",
    )(coarse, band, image)


def two_halves(matrix):
    high = matrix.astype(jnp.bfloat16)
    low = (matrix - high.astype(jnp.float32)).astype(jnp.bfloat16)
    return high, low


def operator_kernel(
    taps, band, response, column_gram, coarse_gram, hyper_out, multi_out, hyper_w, multi_w, bound
):
    rank = band.shape[1]

    def gram_of(values):
        return lax.dot_general(
            values, values, (((0,), (0,)), ((), ())), precision=FULL_PRECISION,
            preferred_element_type=jnp.float32,
        )

    merged = jnp.dot(
        response[...], band[...], precision=FULL_PRECISION, preferred_element_type=jnp.float32
    )
    merged_gram = gram_of(merged)
    hyper = coarse_gram[...] * gram_of(band[...])
    multi = column_gram[...] * merged_gram
    eye = (
        lax.broadcasted_iota(jnp.int32, (rank, rank), 0)
        == lax.broadcasted_iota(jnp.int32, (rank, rank), 1)
    ).astype(jnp.float32)
    multi = multi + RIDGE_TERM * eye
    hyper_out[...] = hyper
    multi_out[...] = multi
    squared = jnp.float32(0.0)
    for phase in range(DEC):
        in_phase = jnp.float32(0.0)
        for offset in range(-W, W + 1):
            if offset % DEC == phase:
                in_phase = in_phase + taps[offset + W]
        squared = squared + in_phase * in_phase
    largest = squared * hyper + multi

    def trace(values):
        return jnp.sum(jnp.sum(values * eye, axis=1, keepdims=True), axis=0, keepdims=True)

    power = largest / trace(largest)
    for _ in range(4):
        power = jnp.dot(power, power, preferred_element_type=jnp.float32)
        power = power / trace(power)
    value = jnp.sum(jnp.sum(power * largest, axis=1, keepdims=True), axis=0, keepdims=True)
    top = 1.1 * value
    bound[...] = jnp.broadcast_to(top, bound.shape)
    for matrix, weights in ((hyper, hyper_w), (multi, multi_w)):
        high, low = two_halves(matrix * (4.0 / top))
        weights[:rank, :rank] = high
        weights[:rank, rank:] = low
        weights[rank:, :rank] = high
        weights[rank:, rank:] = jnp.zeros_like(high)


def make_operator(taps, band, response, column_gram, coarse_gram):
    rank = band.shape[1]
    square = jax.ShapeDtypeStruct((rank, rank), jnp.float32)
    weights = jax.ShapeDtypeStruct((2 * rank, 2 * rank), jnp.bfloat16)
    bound = jax.ShapeDtypeStruct((8, rank), jnp.float32)
    outs = [square, square, weights, weights, bound]
    return pl.pallas_call(
        operator_kernel,
        in_specs=[SMEM] + [whole(a.shape) for a in (band, response, column_gram, coarse_gram)],
        out_specs=[whole(o.shape) for o in outs],
        out_shape=outs,
        compiler_params=params(),
        name="make_operator",
    )(taps, band, response, column_gram, coarse_gram)


def times(values, weights):
    rank = values.shape[1]
    both = jnp.dot(
        jnp.concatenate(two_halves(values), axis=1), weights, preferred_element_type=jnp.float32
    )
    return both[:, :rank] + both[:, rank:]


def shifted(values, by):
    size = values.shape[0]
    return values if by == 0 else pltpu.roll(values, by % size, 0)


def blur_down(taps, field):
    total = None
    for block in range(-REACH, REACH + 1):
        term = None
        for phase in range(DEC):
            offset = DEC * block + phase
            if offset <= W:
                more = taps[offset + W] * field(phase)
                term = more if term is None else term + more
        term = shifted(term, -block)
        total = term if total is None else total + term
    return total


def blur_up(taps, values, phase):
    total = None
    for block in range(-REACH, REACH + 1):
        offset = DEC * block + phase
        if offset <= W:
            term = taps[offset + W] * shifted(values, block)
            total = term if total is None else total + term
    return total


def sums_kernel(count, place, *refs):
    del place
    own = refs[:2]
    arrived = refs[2 : 2 + 2 * count]
    start = refs[2 + 2 * count]
    multi, hyper, low, high = refs[3 + 2 * count :]
    for which, out in ((0, multi), (1, hyper)):
        total = own[which][...].astype(jnp.float32)
        for number in range(count):
            total += arrived[2 * number + which][...].astype(jnp.float32)
        out[...] = total
    first, second = DEC * RIM_MULTI, DEC * RIM_MULTI + RIM
    for pack, top in ((low, True), (high, False)):
        for source, begin, size in (
            (multi, 0, first),
            (hyper, first, RIM),
            (start, second, DEC * RIM),
        ):
            rows = source.shape[0]
            at = 0 if top else rows - size
            pack[begin : begin + size, :] = source[at : at + size, :]


def add_sums(place, multi_part, hyper_part, arrived, start):
    fine, rank = start.shape
    coarse = fine // DEC
    count = len(arrived) // 2
    pack = jax.ShapeDtypeStruct((DEC * RIM_MULTI + RIM + DEC * RIM, rank), jnp.float32)
    outs = [
        jax.ShapeDtypeStruct((fine, rank), jnp.float32),
        jax.ShapeDtypeStruct((coarse, rank), jnp.float32),
        pack,
        pack,
    ]
    return pl.pallas_call(
        functools.partial(sums_kernel, count),
        grid_spec=pltpu.PrefetchScalarGridSpec(
            num_scalar_prefetch=1,
            grid=(1,),
            in_specs=[
                pl.BlockSpec((fine, rank), lambda i, place: (place[0], 0)),
                pl.BlockSpec((coarse, rank), lambda i, place: (place[0], 0)),
            ]
            + [whole(a.shape) for a in arrived]
            + [whole(start.shape)],
            out_specs=[whole(o.shape) for o in outs],
        ),
        out_shape=outs,
        compiler_params=params(),
        name="add_sums",
    )(place, multi_part, hyper_part, *arrived, start)


def basis_kernel(
    devices, taps, multi, hyper, start, before, after, hyper_w, multi_w, bound, basis, products,
    natural, lifted, held,
):
    fine = multi.shape[0]
    coarse = fine // DEC
    wide = coarse + 2 * RIM
    first, second = DEC * RIM_MULTI, DEC * RIM_MULTI + RIM
    own = slice(RIM, RIM + coarse)

    def apply(field):
        lowered = times(blur_down(taps, field), hyper_w[...])
        return [blur_up(taps, lowered, phase) + times(field(phase), multi_w[...]) for phase in range(DEC)]

    natural[: DEC * RIM, :] = before[second:, :]
    natural[DEC * RIM : DEC * RIM + fine, :] = start[...]
    natural[DEC * RIM + fine :, :] = after[second:, :]
    for phase in range(DEC):
        held[1, phase] = natural[pl.ds(phase, wide, stride=DEC), :]
    mapped = apply(lambda phase: held[1, phase])

    lifted[:RIM, :] = before[first:second, :]
    lifted[own, :] = hyper[...]
    lifted[RIM + coarse :, :] = after[first:second, :]
    margin = DEC * (RIM - RIM_MULTI)
    none = jnp.zeros((margin, multi.shape[1]), jnp.float32)
    natural[:margin, :] = none
    natural[margin : DEC * RIM, :] = before[:first, :]
    natural[DEC * RIM : DEC * RIM + fine, :] = multi[...]
    natural[DEC * RIM + fine : 2 * DEC * RIM + fine - margin, :] = after[:first, :]
    natural[2 * DEC * RIM + fine - margin :, :] = none
    quarter = bound[0:1, :] * 0.25
    sums = lifted[...]
    for phase in range(DEC):
        right = natural[pl.ds(phase, wide, stride=DEC), :] + blur_up(taps, sums, phase)
        held[0, phase] = right - quarter * mapped[phase]

    for step in range(ITERS):
        now = step % 2
        mapped = apply(lambda phase: held[now, phase])
        for phase in range(DEC):
            basis[step, phase] = held[now, phase, own, :]
            if step == 0:
                result = 0.5 * mapped[phase] - held[now, phase]
            else:
                result = mapped[phase] - 2.0 * held[now, phase] - held[1 - now, phase]
            if step < ITERS - 1:
                held[1 - now, phase] = result
            else:
                basis[ITERS, phase] = result[own, :]
    rows = []
    for i, j in PAIRS:
        total = jnp.zeros((coarse, multi.shape[1]), jnp.float32)
        for phase in range(DEC):
            total += basis[i, phase] * basis[j, phase]
        rows.append(jnp.sum(total, axis=0, keepdims=True))
    rows.append(jnp.zeros_like(rows[0]))
    block = jnp.concatenate(rows, axis=0)
    for device in range(devices):
        products[device] = block


def make_basis(devices, taps, multi, hyper, start, before, after, hyper_w, multi_w, bound):
    fine, rank = multi.shape
    coarse = fine // DEC
    wide = coarse + 2 * RIM
    arrays = (multi, hyper, start, before, after, hyper_w, multi_w, bound)
    outs = [
        jax.ShapeDtypeStruct((ITERS + 1, DEC, coarse, rank), jnp.float32),
        jax.ShapeDtypeStruct((devices, len(PAIRS) + 1, rank), jnp.float32),
    ]
    return pl.pallas_call(
        functools.partial(basis_kernel, devices),
        in_specs=[SMEM] + [whole(a.shape) for a in arrays],
        out_specs=[whole(o.shape) for o in outs],
        out_shape=outs,
        scratch_shapes=[
            pltpu.VMEM((DEC * wide, rank), jnp.float32),
            pltpu.VMEM((wide, rank), jnp.float32),
            pltpu.VMEM((2, DEC, wide, rank), jnp.float32),
        ],
        compiler_params=params(),
        name="make_basis",
    )(taps, *arrays)


def advance_kernel(products, basis, start, bound, solution, residual, amplified):
    count = ITERS + 1
    sums = jnp.sum(products[...], axis=0)
    sums = jnp.sum(sums, axis=1, keepdims=True)
    inner = {}
    for number, (i, j) in enumerate(PAIRS):
        inner[i, j] = inner[j, i] = sums[number : number + 1, :]
    zero = jnp.zeros((1, 1), jnp.float32)
    one = jnp.ones((1, 1), jnp.float32)

    def mapped_of(coefficients):
        result = [2.0 * c for c in coefficients] + [zero] * (count - len(coefficients))
        for j, c in enumerate(coefficients):
            if j + 1 < count:
                result[j + 1] = result[j + 1] + (2.0 * c if j == 0 else c)
            if j > 0:
                result[j - 1] = result[j - 1] + c
        return result

    def product(first, second):
        total = spread = zero
        for i, a in enumerate(first):
            if a is zero:
                continue
            for j, b in enumerate(second):
                if b is zero:
                    continue
                term = a * b * inner[i, j]
                total = total + term
                spread = spread + jnp.abs(term)
        return total, spread / jnp.abs(total)

    walked = [zero] * ITERS
    rest = [one] + [zero] * ITERS
    heading = [one]
    norm = inner[0, 0]
    worst = zero
    for iteration in range(ITERS):
        mapped = mapped_of(heading)
        mapped = mapped[: iteration + 2]
        curved, spread = product(heading, mapped)
        worst = jnp.maximum(worst, spread)
        step = norm / curved
        for j, c in enumerate(heading):
            walked[j] = walked[j] + step * c
        for j, c in enumerate(mapped):
            rest[j] = rest[j] - step * c
        if iteration < ITERS - 1:
            active = rest[: iteration + 2]
            following, spread = product(active, active)
            worst = jnp.maximum(worst, spread)
            ratio = following / norm
            heading = [
                c + ratio * heading[j] if j < len(heading) else c for j, c in enumerate(active)
            ]
            norm = following
    amplified[...] = jnp.broadcast_to(worst, amplified.shape)
    scale = 4.0 / bound[0:1, 0:1]
    walked = [c * scale for c in walked]
    coarse = basis.shape[2]
    for phase in range(DEC):
        rows = pl.ds(phase, coarse, stride=DEC)
        total = start[rows, :]
        for j in range(ITERS):
            total += walked[j] * basis[j, phase]
        solution[rows, :] = total
        total = rest[0] * basis[0, phase]
        for j in range(1, count):
            total += rest[j] * basis[j, phase]
        residual[rows, :] = total


def advance(products, basis, start, bound):
    rank = start.shape[1]
    outs = [
        jax.ShapeDtypeStruct(start.shape, jnp.float32),
        jax.ShapeDtypeStruct(start.shape, jnp.float32),
        jax.ShapeDtypeStruct((8, rank), jnp.float32),
    ]
    arrays = (products, basis, start, bound)
    return pl.pallas_call(
        advance_kernel,
        in_specs=[whole(a.shape) for a in arrays],
        out_specs=[whole(o.shape) for o in outs],
        out_shape=outs,
        compiler_params=params(),
        name="advance",
    )(*arrays)


def to_next(values, axis, count):
    return lax.ppermute(values, axis, [(i, (i + 1) % count) for i in range(count)])


def to_previous(values, axis, count):
    return lax.ppermute(values, axis, [((i + 1) % count, i) for i in range(count)])


def step_by_step(taps, multi, hyper, start, hyper_gram, multi_gram, devices):
    def widened(values, breadth):
        return jnp.concatenate(
            [
                to_next(values[-breadth:], BOTH, devices),
                values,
                to_previous(values[:breadth], BOTH, devices),
            ]
        )

    def down(values):
        rows = values.shape[0] // DEC
        parts = values.reshape(rows, DEC, -1)
        size = rows - 2 * REACH
        total = 0.0
        for offset in range(-W, W + 1):
            block, phase = divmod(offset, DEC)
            total = total + taps[offset + W] * lax.slice_in_dim(
                parts[:, phase], REACH + block, REACH + block + size, axis=0
            )
        return total

    def up(values):
        size = values.shape[0] - 2 * REACH
        phases = []
        for phase in range(DEC):
            total = 0.0
            for block in range(-REACH, REACH + 1):
                offset = DEC * block + phase
                if offset <= W:
                    total = total + taps[offset + W] * lax.slice_in_dim(
                        values, REACH - block, REACH - block + size, axis=0
                    )
            phases.append(total)
        return jnp.stack(phases, axis=1).reshape(DEC * size, -1)

    def operate(values):
        lowered = jnp.dot(down(widened(values, 2 * W)), hyper_gram, precision=FULL_PRECISION)
        return up(lowered) + jnp.dot(values, multi_gram, precision=FULL_PRECISION)

    def inner_sum(first, second):
        return lax.psum(jnp.sum(first * second), BOTH)

    solution = start
    residual = up(widened(hyper, REACH)) + multi - operate(solution)
    direction = residual
    norm = inner_sum(residual, residual)

    def iterate(_, state):
        solution, residual, direction, norm = state
        mapped = operate(direction)
        step = norm / inner_sum(direction, mapped)
        solution = solution + step * direction
        residual = residual - step * mapped
        following = inner_sum(residual, residual)
        return solution, residual, residual + following / norm * direction, following

    solution, residual, _, _ = lax.fori_loop(0, ITERS, iterate, (solution, residual, direction, norm))
    return solution, residual


def body(
    multispectral, hyperspectral, row_start, col_factor, band_factor, response, blur_taps, offsets
):
    across = lax.axis_size("col")
    devices = across * lax.axis_size("row")
    place = lax.axis_index("col")
    spread = jnp.arange(-W, W + 1, dtype=jnp.int32)
    taps = jnp.sum(
        jnp.where(offsets[:, None] == spread[None, :], blur_taps[:, None], jnp.float32(0.0)), axis=0
    )
    columns = lax.all_gather(col_factor.T, "row", axis=0, tiled=True).T
    edge = 2 * W
    before = to_next(columns[-edge:], "col", across)
    after = to_previous(columns[:edge], "col", across)
    multi_part, column_part = contract_multi(columns, band_factor, response, multispectral)

    fine = row_start.shape[0]

    def exchange(values, size):
        arrived = []
        for distance in range(1, across):
            piece = lax.dynamic_slice_in_dim(values, (place + distance) % across * size, size, 0)
            arrived.append(
                lax.ppermute(piece, "col", [(i, (i + distance) % across) for i in range(across)])
            )
        return arrived

    multi_arrived = exchange(multi_part, fine)
    coarse, coarse_part = coarsen(taps, columns, before, after)
    column_gram, coarse_gram = lax.psum((column_part, coarse_part), "col")
    hyper_part = contract_hyper(coarse, band_factor, hyperspectral)
    hyper_arrived = exchange(hyper_part, fine // DEC)
    hyper_gram, multi_gram, hyper_w, multi_w, bound = make_operator(
        taps, band_factor, response, column_gram, coarse_gram
    )
    arrived = [a for pair in zip(multi_arrived, hyper_arrived) for a in pair]
    multi, hyper, low, high = add_sums(place[None], multi_part, hyper_part, arrived, row_start)
    before_rows = to_next(high, BOTH, devices)
    after_rows = to_previous(low, BOTH, devices)
    basis, products = make_basis(
        devices, taps, multi, hyper, row_start, before_rows, after_rows, hyper_w, multi_w, bound
    )
    products = lax.all_to_all(products, BOTH, 0, 0, tiled=True)
    solution, residual, amplified = advance(products, basis, row_start, bound)
    return lax.cond(
        amplified[0, 0] < TRUST,
        lambda: (solution, residual),
        lambda: step_by_step(taps, multi, hyper, row_start, hyper_gram, multi_gram, devices),
    )


def solution(mesh):
    in_specs = (
        P(None, "row", "col"),
        P(None, "row", "col"),
        P(("row", "col"), None),
        P("col", "row"),
        P(),
        P(),
        P(),
        P(),
    )
    out_specs = (P(("row", "col"), None), P(("row", "col"), None))
    return jax.shard_map(body, mesh=mesh, in_specs=in_specs, out_specs=out_specs, check_vma=False)
```

time: 485 us -> 114 us (0.24); the launches traced: 479 us -> 113 us
  matrix products: 204 us -> 0 us
  blocking collectives: 108 us -> 10.8 us
  waiting for transfers between devices: 85.5 us -> 34.6 us
  other arithmetic: 30.3 us -> 0.09 us
  Pallas kernels: 0 us -> 20.2 us
  between operations: 24.1 us -> 14.9 us
    dot_general x29 -> x0, matrix products: 204 us -> none  [the longest x12 171 us: apply_band(): return jnp.dot(matrix, values.astype(jnp.float32), precision=FULL_PRECISION)]
    psum x7 -> x0, blocking collectives: 97.3 us -> none  [inner_sum(): return lax.psum(jnp.sum(first_field * second_field), 'row')]
    psum x1, waiting for transfers between devices: 52.8 us -> 19.6 us  [body(): column_gram, coarse_gram = lax.psum((column_part, coarse_part), 'col')]
    all_gather x1 -> x0, waiting for transfers between devices: 26.5 us -> none  [body(): start_rows = lax.all_gather(row_start, 'col', axis=0, tiled=True)]
    pallas_call x0 -> x7, Pallas kernels: none -> 20.2 us  [the longest x1 8.09 us: contract_hyper(): pl.pallas_call(hyper_kernel, grid=(bands // BANDS_B,), in_specs=[whole(co...]
    add x14 -> x1, other arithmetic: 15.7 us -> 0.01 us  [body(): spread = jnp.arange(-W, W + 1, dtype=jnp.int32)]
    all_to_all x0 -> x1, waiting for transfers between devices: none -> 10.2 us  [body(): products = lax.all_to_all(products, BOTH, 0, 0, tiled=True)]
    reduce_sum x3 -> x1, other arithmetic: 7.36 us -> 0.09 us  [body(): jnp.sum(jnp.where(offsets[:, None] == spread[None, :], blur_taps[:, None]...]
  transfers between devices with their start and end apart: 16 -> 12, of which waited for: 9 -> 5; matrix products, arithmetic and copies ran while one was open for 13% -> 0% of each run, Pallas kernels for 0% -> 14%
where the time goes in v1:
time: 114 us; the launch traced here: 113 us
  waiting for transfers between devices  34.6 us (30%)
  starting transfers between devices  24.5 us (21%)
  Pallas kernels  20.2 us (18%)
  between operations  14.9 us (13%)
  blocking collectives  10.8 us (9%)
  local copies, waits for them, and re-layouts  7.7 us (7%)
    psum x1, waiting for transfers between devices, body(): column_gram, coarse_gram = lax.psum((column_part, coarse_part), 'col')  19.6 us
    ppermute x6, starting transfers between devices, exchange(): lax.ppermute(piece, 'col', [(i, (i + distance) % across) for i in range(a...  11.1 us
    all_gather x1, blocking collectives, body(): columns = lax.all_gather(col_factor.T, 'row', axis=0, tiled=True).T  10.8 us
    all_to_all x1, waiting for transfers between devices, body(): products = lax.all_to_all(products, BOTH, 0, 0, tiled=True)  10.2 us
    ppermute x2, starting transfers between devices, to_previous(): lax.ppermute(values, axis, [((i + 1) % count, i) for i in range(count)])  8.98 us
    pallas_call x1, Pallas kernels, contract_hyper(): pl.pallas_call(hyper_kernel, grid=(bands // BANDS_B,), in_specs=[whole(co...  8.09 us
    unnamed x21, local copies, waits for them, and re-layouts  6.32 us
    ppermute x6, waiting for transfers between devices, exchange(): lax.ppermute(piece, 'col', [(i, (i + distance) % across) for i in range(a...  4.8 us
  transfers between devices with their start and end apart: 12, of which 5 were waited for; matrix products, arithmetic and copies ran while one was open for 0% of the time, Pallas kernels for 14%

profile of v1, /device:TPU:0, one launch (start us, length us, event | category | flops | bytes accessed | tf_op | source)
XLA Modules:
  0.0 113.1 jit_solution(17889109702345073071)
XLA Ops:
  7.2 1.0 copy.446.refs_8_.start
  8.2 10.8 %all_gather.3 = bf16[128,512]{1,0:T(8,128)(2,1)S(1)} all-gather(bf16[16,512]{1,0:T(8,128)(2,1)} %bitcast.153), channel_id=1, replica_groups=mesh['row'=8,'col'=4] {'row'}, dimensions={0}, use_global_device_ids=true | all-gather | bytes 147456 | tf_op jit(solution)/shard_map/all_gather | solution.py:571
  19.0 0.1 copy.150
  19.2 3.7 %collective-permute-start.7 = (bf16[16,128]{1,0:T(8,128)(2,1)S(1)}, bf16[16,128]{1,0:T(8,128)(2,1)S(1)}, u32[]{:S(2)}, u32[]{:S(2)}) collective-permute-start(bf16[16,128]{1,0:T(8,128)(2,1)S(1)} %get-tuple-element.221), channel_id=1, source_target_pairs={{1,0},{2,1},{3,2},{0,3},{5,4},{6,5},{7,6},{4,7},{9,8},{10,9},{11,1... | collective-permute-start | bytes 12296 | tf_op jit(solution)/shard_map/ppermute | solution.py:497
  22.8 2.2 %copy-done = bf16[2,2048,512]{2,1,0:T(8,128)(2,1)S(1)} copy-done((bf16[2,2048,512]{2,1,0:T(8,128)(2,1)S(1)}, bf16[2,2048,512]{2,1,0:T(8,128)(2,1)}, u32[]{:S(2)}) %copy-start) | copy-done | bytes 4194328
  25.0 0.8 copy-done.1
  25.8 0.7 copy-done.5
  26.5 3.4 %contract_multi.1 = (bf16[2048,128]{1,0:T(8,128)(2,1)S(1)}, f32[128,128]{1,0:T(8,128)}) custom-call(bf16[512,128]{1,0:T(8,128)(2,1)S(1)} %bitcast.146, f32[96,128]{1,0:T(8,128)S(1)} %copy-done.1, f32[2,96]{1,0:T(2,128)S(1)} %copy-done.5, bf16[2,2048,512]{2,1,0:T(8,128)(2,1)S(1)} %copy-done), custom_call_target="tpu_custom_call" | custom-call | tf_op jit(solution)/shard_map/contract_multi/pallas_call | solution.py:60
  30.0 3.9 %collective-permute-start.12 = (bf16[512,128]{1,0:T(8,128)(2,1)S(1)}, bf16[512,128]{1,0:T(8,128)(2,1)S(1)}, u32[]{:S(2)}, u32[]{:S(2)}) collective-permute-start(bf16[512,128]{1,0:T(8,128)(2,1)S(1)} %get-tuple-element.215), channel_id=1, source_target_pairs={{0,3},{1,0},{2,1},{3,2},{4,7},{5,4},{6,5},{7,6},{8,11},{9,8},{10,9... | collective-permute-start | bytes 393224 | tf_op jit(solution)/shard_map/ppermute | solution.py:584
  33.8 0.6 collective-permute-start.8
  34.5 0.1 select_reduce_fusion.taps
  34.6 1.5 %coarsen.1 = (f32[128,128]{1,0:T(8,128)S(1)}, f32[128,128]{1,0:T(8,128)}) custom-call(f32[17]{0:T(128)S(1)} %select_reduce_fusion.taps, bf16[512,128]{1,0:T(8,128)(2,1)S(1)} %bitcast.147, bf16[16,128]{1,0:T(8,128)(2,1)S(1)} %collective-permute-done.6.before, bf16[16,128]{1,0:T(8,128)(2,1)S(1)} %collective-permute-done.7.after), custom_call_target="tpu_custom_call" | custom-call | tf_op jit(solution)/shard_map/coarsen/pallas_call | solution.py:98
  36.1 8.1 %contract_hyper.1.refs_1_ = bf16[512,128]{1,0:T(8,128)(2,1)S(1)} custom-call(f32[128,128]{1,0:T(8,128)S(1)} %get-tuple-element.86.coarse, f32[96,128]{1,0:T(8,128)S(1)} %copy-done.2, bf16[96,512,128]{2,1,0:T(8,128)(2,1)} %image.3), custom_call_target="tpu_custom_call" | custom-call | tf_op jit(solution)/shard_map/contract_hyper/pallas_call | solution.py:137
  44.2 3.2 %collective-permute-start.13 = (bf16[128,128]{1,0:T(8,128)(2,1)S(1)}, bf16[128,128]{1,0:T(8,128)(2,1)S(1)}, u32[]{:S(2)}, u32[]{:S(2)}) collective-permute-start(bf16[128,128]{1,0:T(8,128)(2,1)S(1)} %get-tuple-element.218), channel_id=1, source_target_pairs={{0,3},{1,0},{2,1},{3,2},{4,7},{5,4},{6,5},{7,6},{8,11},{9,8},{10,9... | collective-permute-start | bytes 98312 | tf_op jit(solution)/shard_map/ppermute | solution.py:584
  47.5 1.2 %collective-permute-start.11 = (bf16[128,128]{1,0:T(8,128)(2,1)S(1)}, bf16[128,128]{1,0:T(8,128)(2,1)S(1)}, u32[]{:S(2)}, u32[]{:S(2)}) collective-permute-start(bf16[128,128]{1,0:T(8,128)(2,1)S(1)} %get-tuple-element.219), channel_id=1, source_target_pairs={{0,2},{1,3},{2,0},{3,1},{4,6},{5,7},{6,4},{7,5},{8,10},{9,11},{10,... | collective-permute-start | bytes 98312 | tf_op jit(solution)/shard_map/ppermute | solution.py:584
  48.7 0.4 collective-permute-done.13.refs_7_
  49.1 2.2 %collective-permute-start.9 = (bf16[128,128]{1,0:T(8,128)(2,1)S(1)}, bf16[128,128]{1,0:T(8,128)(2,1)S(1)}, u32[]{:S(2)}, u32[]{:S(2)}) collective-permute-start(bf16[128,128]{1,0:T(8,128)(2,1)S(1)} %get-tuple-element.220), channel_id=1, source_target_pairs={{0,1},{1,2},{2,3},{3,0},{4,5},{5,6},{6,7},{7,4},{8,9},{9,10},{10,1... | collective-permute-start | bytes 98312 | tf_op jit(solution)/shard_map/ppermute | solution.py:584
  51.3 1.5 %collective-permute-done.11.refs_5_ = bf16[128,128]{1,0:T(8,128)(2,1)S(1)} collective-permute-done((bf16[128,128]{1,0:T(8,128)(2,1)S(1)}, bf16[128,128]{1,0:T(8,128)(2,1)S(1)}, u32[]{:S(2)}, u32[]{:S(2)}) %collective-permute-start.11) | collective-permute-done | bytes 32800 | tf_op jit(solution)/shard_map/ppermute | solution.py:584
  52.7 3.0 %collective-permute-done.9.refs_3_ = bf16[128,128]{1,0:T(8,128)(2,1)S(1)} collective-permute-done((bf16[128,128]{1,0:T(8,128)(2,1)S(1)}, bf16[128,128]{1,0:T(8,128)(2,1)S(1)}, u32[]{:S(2)}, u32[]{:S(2)}) %collective-permute-start.9) | collective-permute-done | bytes 32800 | tf_op jit(solution)/shard_map/ppermute | solution.py:584
  55.7 0.1 add_sums.1
  55.9 5.3 %collective-permute-start.15 = (f32[184,128]{1,0:T(8,128)S(1)}, f32[184,128]{1,0:T(8,128)S(1)}, u32[]{:S(2)}, u32[]{:S(2)}) collective-permute-start(f32[184,128]{1,0:T(8,128)S(1)} %get-tuple-element.90), channel_id=1, source_target_pairs={{1,0},{2,1},{3,2},{4,3},{5,4},{6,5},{7,6},{8,7},{9,8},{10,9},{11,1... | collective-permute-start | bytes 282632 | tf_op jit(solution)/shard_map/ppermute | solution.py:497
  61.2 19.6 %all-reduce.3.cloned.1.call-done = (f32[128,128]{1,0:T(8,128)}, f32[128,128]{1,0:T(8,128)}) async-done(((f32[128,128]{1,0:T(8,128)}, f32[128,128]{1,0:T(8,128)}), (f32[128,128]{1,0:T(8,128)}, f32[128,128]{1,0:T(8,128)})) %all-reduce.3.cloned.1.call-update) | async-done | bytes 131088 | tf_op jit(solution)/shard_map/psum | solution.py:590
  80.8 0.8 copy-done.3
  81.6 0.8 copy-done.4
  82.5 2.3 %make_operator.1 = (f32[128,128]{1,0:T(8,128)S(1)}, f32[128,128]{1,0:T(8,128)S(1)}, bf16[256,256]{1,0:T(8,128)(2,1)S(1)}, bf16[256,256]{1,0:T(8,128)(2,1)S(1)}, f32[8,128]{1,0:T(8,128)S(1)}) custom-call(f32[17]{0:T(128)S(1)} %select_reduce_fusion.taps, f32[96,128]{1,0:T(8,128)S(1)} %copy-done.2, f32[2,96]{1,0:T(2,128)S(1)} %copy-done.6, ...), custom_call_target="tpu_custom_call" | custom-call | tf_op jit(solution)/shard_map/make_operator/pallas_call | solution.py:216
  84.8 3.6 %make_basis.1 = (f32[5,4,128,128]{3,2,1,0:T(8,128)S(1)}, f32[32,16,128]{2,1,0:T(8,128)}) custom-call(f32[17]{0:T(128)S(1)} %select_reduce_fusion.taps, f32[512,128]{1,0:T(8,128)S(1)} %get-tuple-element.87.multi, f32[128,128]{1,0:T(8,128)S(1)} %get-tuple-element.88.hyper, f32[512,128]{1,0:T(8,128)S(1)} %copy.446.refs_8_.start, ...), custom_call_target="tpu_custom_call" | custom-call | tf_op jit(solution)/shard_map/make_basis/pallas_call | solution.py:387
  88.4 4.3 %all-to-all-start = ((f32[32,16,128]{2,1,0:T(8,128)}), f32[32,16,128]{2,1,0:T(8,128)S(1)}, u32[]{:S(2)}, u32[]{:S(2)}) async-start(f32[32,16,128]{2,1,0:T(8,128)} %get-tuple-element.96), calls=%async_computation | async-start | bytes 524288 | tf_op jit(solution)/shard_map/all_to_all | solution.py:603
  92.7 10.2 %all-to-all-done.products = f32[32,16,128]{2,1,0:T(8,128)S(1)} async-done(((f32[32,16,128]{2,1,0:T(8,128)}), f32[32,16,128]{2,1,0:T(8,128)S(1)}, u32[]{:S(2)}, u32[]{:S(2)}) %all-to-all-start) | async-done | bytes 262176 | tf_op jit(solution)/shard_map/all_to_all | solution.py:603
  102.9 1.2 %advance.1 = (f32[512,128]{1,0:T(8,128)S(1)}, f32[512,128]{1,0:T(8,128)}, f32[8,128]{1,0:T(8,128)S(1)}) custom-call(f32[32,16,128]{2,1,0:T(8,128)S(1)} %all-to-all-done.products, f32[5,4,128,128]{3,2,1,0:T(8,128)S(1)} %get-tuple-element.97.basis, f32[512,128]{1,0:T(8,128)S(1)} %copy.446.refs_8_.start, f32[8,128]{1,0:T(8,128)S(1)} %get-tuple-element.95.bound), custom_call_target="tpu_custom_call" | custom-call | tf_op jit(solution)/shard_map/advance/pallas_call | solution.py:482
  104.1 0.5 slice.465
  105.3 0.9 conditional.1
  105.5 0.7 copy.441
  (31 shorter events, 0.2 us)
Async XLA Ops:
  7.2 28.9 %copy-start.2 = (f32[96,128]{1,0:T(8,128)S(1)}, f32[96,128]{1,0:T(8,128)}, u32[]{:S(2)}) copy-start(f32[96,128]{1,0:T(8,128)} %band.5) | copy-start | bytes 147460
  7.2 27.3 %copy-start.12 = (s32[9]{0:T(128)S(1)}, s32[9]{0:T(128)}, u32[]{:S(2)}) copy-start(s32[9]{0:T(128)} %param.19) | copy-start | bytes 112
  7.2 27.3 %copy-start.11 = (f32[9]{0:T(128)S(1)}, f32[9]{0:T(128)}, u32[]{:S(2)}) copy-start(f32[9]{0:T(128)} %param.18) | copy-start | bytes 112
  7.2 73.6 %all-reduce.3.cloned.1.call-start = ((), (), s32[]{:S(2)}) async-start(), calls=%async_computation.1 | async-start | bytes 262144 | tf_op jit(solution)/shard_map/psum | solution.py:590
  8.2 97.1 %copy-start.7 = (f32[512,128]{1,0:T(8,128)}, f32[512,128]{1,0:T(8,128)S(1)}, u32[]{:S(2)}) copy-start(f32[512,128]{1,0:T(8,128)S(1)} %copy.446.refs_8_.start) | copy-start | bytes 786436
  19.2 15.4 %collective-permute-start.7 = (bf16[16,128]{1,0:T(8,128)(2,1)S(1)}, bf16[16,128]{1,0:T(8,128)(2,1)S(1)}, u32[]{:S(2)}, u32[]{:S(2)}) collective-permute-start(bf16[16,128]{1,0:T(8,128)(2,1)S(1)} %get-tuple-element.221), channel_id=1, source_target_pairs={{1,0},{2,1},{3,2},{0,3},{5,4},{6,5},{7,6},{4,7},{9,8},{10,9},{11,1... | collective-permute-start | bytes 12296 | tf_op jit(solution)/shard_map/ppermute | solution.py:497
  22.8 11.8 %collective-permute-start.6 = (bf16[16,128]{1,0:T(8,128)(2,1)S(1)}, bf16[16,128]{1,0:T(8,128)(2,1)S(1)}, u32[]{:S(2)}, u32[]{:S(2)}) collective-permute-start(bf16[16,128]{1,0:T(8,128)(2,1)S(1)} %get-tuple-element.222), channel_id=1, source_target_pairs={{0,1},{1,2},{2,3},{3,0},{4,5},{5,6},{6,7},{7,4},{8,9},{9,10},{10,1... | collective-permute-start | bytes 12296 | tf_op jit(solution)/shard_map/ppermute | solution.py:493
  22.8 2.2 %copy-start = (bf16[2,2048,512]{2,1,0:T(8,128)(2,1)S(1)}, bf16[2,2048,512]{2,1,0:T(8,128)(2,1)}, u32[]{:S(2)}) copy-start(bf16[2,2048,512]{2,1,0:T(8,128)(2,1)} %image.2) | copy-start | bytes 12582916
  25.0 0.8 copy-start.1
  25.8 0.7 copy-start.5
  30.0 25.7 %collective-permute-start.12 = (bf16[512,128]{1,0:T(8,128)(2,1)S(1)}, bf16[512,128]{1,0:T(8,128)(2,1)S(1)}, u32[]{:S(2)}, u32[]{:S(2)}) collective-permute-start(bf16[512,128]{1,0:T(8,128)(2,1)S(1)} %get-tuple-element.215), channel_id=1, source_target_pairs={{0,3},{1,0},{2,1},{3,2},{4,7},{5,4},{6,5},{7,6},{8,11},{9,8},{10,9... | collective-permute-start | bytes 393224 | tf_op jit(solution)/shard_map/ppermute | solution.py:584
  33.8 21.9 %collective-permute-start.10 = (bf16[512,128]{1,0:T(8,128)(2,1)S(1)}, bf16[512,128]{1,0:T(8,128)(2,1)S(1)}, u32[]{:S(2)}, u32[]{:S(2)}) collective-permute-start(bf16[512,128]{1,0:T(8,128)(2,1)S(1)} %get-tuple-element.216), channel_id=1, source_target_pairs={{0,2},{1,3},{2,0},{3,1},{4,6},{5,7},{6,4},{7,5},{8,10},{9,11},{10,... | collective-permute-start | bytes 393224 | tf_op jit(solution)/shard_map/ppermute | solution.py:584
  33.8 21.9 %collective-permute-start.8 = (bf16[512,128]{1,0:T(8,128)(2,1)S(1)}, bf16[512,128]{1,0:T(8,128)(2,1)S(1)}, u32[]{:S(2)}, u32[]{:S(2)}) collective-permute-start(bf16[512,128]{1,0:T(8,128)(2,1)S(1)} %get-tuple-element.217), channel_id=1, source_target_pairs={{0,1},{1,2},{2,3},{3,0},{4,5},{5,6},{6,7},{7,4},{8,9},{9,10},{10,1... | collective-permute-start | bytes 393224 | tf_op jit(solution)/shard_map/ppermute | solution.py:584
  36.1 44.7 %copy-start.6 = (f32[2,96]{1,0:T(2,128)S(1)}, f32[2,96]{1,0:T(2,128)}, u32[]{:S(2)}) copy-start(f32[2,96]{1,0:T(2,128)} %response.3) | copy-start | bytes 2308
  44.2 4.8 %collective-permute-start.13 = (bf16[128,128]{1,0:T(8,128)(2,1)S(1)}, bf16[128,128]{1,0:T(8,128)(2,1)S(1)}, u32[]{:S(2)}, u32[]{:S(2)}) collective-permute-start(bf16[128,128]{1,0:T(8,128)(2,1)S(1)} %get-tuple-element.218), channel_id=1, source_target_pairs={{0,3},{1,0},{2,1},{3,2},{4,7},{5,4},{6,5},{7,6},{8,11},{9,8},{10,9... | collective-permute-start | bytes 98312 | tf_op jit(solution)/shard_map/ppermute | solution.py:584
  47.5 5.2 %collective-permute-start.11 = (bf16[128,128]{1,0:T(8,128)(2,1)S(1)}, bf16[128,128]{1,0:T(8,128)(2,1)S(1)}, u32[]{:S(2)}, u32[]{:S(2)}) collective-permute-start(bf16[128,128]{1,0:T(8,128)(2,1)S(1)} %get-tuple-element.219), channel_id=1, source_target_pairs={{0,2},{1,3},{2,0},{3,1},{4,6},{5,7},{6,4},{7,5},{8,10},{9,11},{10,... | collective-permute-start | bytes 98312 | tf_op jit(solution)/shard_map/ppermute | solution.py:584
  49.1 6.6 %collective-permute-start.9 = (bf16[128,128]{1,0:T(8,128)(2,1)S(1)}, bf16[128,128]{1,0:T(8,128)(2,1)S(1)}, u32[]{:S(2)}, u32[]{:S(2)}) collective-permute-start(bf16[128,128]{1,0:T(8,128)(2,1)S(1)} %get-tuple-element.220), channel_id=1, source_target_pairs={{0,1},{1,2},{2,3},{3,0},{4,5},{5,6},{6,7},{7,4},{8,9},{9,10},{10,1... | collective-permute-start | bytes 98312 | tf_op jit(solution)/shard_map/ppermute | solution.py:584
  55.8 29.0 %collective-permute-start.14 = (f32[184,128]{1,0:T(8,128)S(1)}, f32[184,128]{1,0:T(8,128)S(1)}, u32[]{:S(2)}, u32[]{:S(2)}) collective-permute-start(f32[184,128]{1,0:T(8,128)S(1)} %get-tuple-element.89), channel_id=1, source_target_pairs={{0,1},{1,2},{2,3},{3,4},{4,5},{5,6},{6,7},{7,8},{8,9},{9,10},{10,1... | collective-permute-start | bytes 282632 | tf_op jit(solution)/shard_map/ppermute | solution.py:493
  55.9 28.9 %collective-permute-start.15 = (f32[184,128]{1,0:T(8,128)S(1)}, f32[184,128]{1,0:T(8,128)S(1)}, u32[]{:S(2)}, u32[]{:S(2)}) collective-permute-start(f32[184,128]{1,0:T(8,128)S(1)} %get-tuple-element.90), channel_id=1, source_target_pairs={{1,0},{2,1},{3,2},{4,3},{5,4},{6,5},{7,6},{8,7},{9,8},{10,9},{11,1... | collective-permute-start | bytes 282632 | tf_op jit(solution)/shard_map/ppermute | solution.py:497
  80.8 0.8 copy-start.3
  81.6 0.8 copy-start.4
  88.4 14.5 %all-to-all-start = ((f32[32,16,128]{2,1,0:T(8,128)}), f32[32,16,128]{2,1,0:T(8,128)S(1)}, u32[]{:S(2)}, u32[]{:S(2)}) async-start(f32[32,16,128]{2,1,0:T(8,128)} %get-tuple-element.96), calls=%async_computation | async-start | bytes 524288 | tf_op jit(solution)/shard_map/all_to_all | solution.py:603
Sparse Core Ops, SparseCore 0:
  47.6 33.1 all-reduce.2

commit v2 on v1

--- a/solution.py
+++ b/solution.py
@@ -20,6 +20,7 @@
 RIM_MULTI = 16
 PAIRS = [(i, j) for i in range(ITERS + 1) for j in range(i, ITERS + 1)]
 TRUST = 2.0e4
+EDGE = 16
 VMEM_LIMIT = 48 * 1024 * 1024
 
 
@@ -34,79 +35,92 @@
 SMEM = pl.BlockSpec(memory_space=pltpu.SMEM)
 
 
-def multi_kernel(columns, band, response, image, out, gram, pairs):
-    depth = columns.shape[0]
+def in_hbm(values):
+    return pltpu.with_memory_space_constraint(values, pltpu.HBM)
+
+
+def two_halves(matrix):
+    high = matrix.astype(jnp.bfloat16)
+    low = (matrix - high.astype(jnp.float32)).astype(jnp.bfloat16)
+    return high, low
+
+
+def gram_of(values):
+    return lax.dot_general(
+        values, values, (((0,), (0,)), ((), ())), precision=FULL_PRECISION,
+        preferred_element_type=jnp.float32,
+    )
+
+
+def multi_kernel(
+    share, taps, place, gathered, band, response, image, out, coarse, gram, pairs, wide, grams
+):
+    depth = image.shape[2]
+    rank = out.shape[1]
+    edge = EDGE
 
     @pl.when(pl.program_id(0) == 0)
     def _():
-        wide = columns[...].astype(jnp.float32)
+        for start in range(0, depth, rank):
+            square = gathered[:, start : start + rank].astype(jnp.float32)
+            wide[edge + start : edge + start + rank, :] = square.T
+        edges = gathered[:, depth : depth + rank].astype(jnp.float32).T
+        wide[:edge, :] = edges[:edge, :]
+        wide[edge + depth :, :] = edges[edge : 2 * edge, :]
+        columns = wide[edge : edge + depth, :]
         merged = jnp.dot(
             response[...], band[...], precision=FULL_PRECISION, preferred_element_type=jnp.float32
         )
         for k in range(2):
-            pairs[k * depth : (k + 1) * depth, :] = (merged[k : k + 1, :] * wide).astype(jnp.bfloat16)
-        gram[...] = lax.dot_general(
-            columns[...], columns[...], (((0,), (0,)), ((), ())), preferred_element_type=jnp.float32
+            pairs[k * depth : (k + 1) * depth, :] = (merged[k : k + 1, :] * columns).astype(
+                jnp.bfloat16
+            )
+        total = jnp.zeros(coarse.shape, jnp.float32)
+        for offset in range(-W, W + 1):
+            total += taps[offset + W] * wide[pl.ds(edge + offset, depth // DEC, stride=DEC), :]
+        coarse[...] = total
+        exact = columns.astype(jnp.bfloat16)
+        grams[0] = lax.dot_general(
+            exact, exact, (((0,), (0,)), ((), ())), preferred_element_type=jnp.float32
         )
+        grams[1] = gram_of(total)
+        first = pl.multiple_of(place[0] * share, share)
+        halves = two_halves(
+            jnp.concatenate([grams[0, pl.ds(first, share), :], grams[1, pl.ds(first, share), :]])
+        )
+        gram[: 2 * share, :] = halves[0]
+        gram[2 * share :, :] = halves[1]
 
     total = jnp.dot(image[0], pairs[:depth, :], preferred_element_type=jnp.float32)
     total += jnp.dot(image[1], pairs[depth:, :], preferred_element_type=jnp.float32)
     out[...] = total.astype(jnp.bfloat16)
 
 
-def contract_multi(columns, band, response, image):
+def contract_multi(share, taps, place, gathered, band, response, image):
     bands, rows, depth = image.shape
-    rank = columns.shape[1]
+    rank = band.shape[1]
+    outs = [
+        jax.ShapeDtypeStruct((rows, rank), jnp.bfloat16),
+        jax.ShapeDtypeStruct((depth // DEC, rank), jnp.float32),
+        jax.ShapeDtypeStruct((4 * share, rank), jnp.bfloat16),
+    ]
     return pl.pallas_call(
-        multi_kernel,
+        functools.partial(multi_kernel, share),
         grid=(rows // ROWS_A,),
-        in_specs=[
-            whole(columns.shape),
-            whole(band.shape),
-            whole(response.shape),
-            pl.BlockSpec((bands, ROWS_A, depth), lambda i: (0, i, 0)),
+        in_specs=[SMEM, SMEM]
+        + [whole(a.shape) for a in (gathered, band, response)]
+        + [pl.BlockSpec((bands, ROWS_A, depth), lambda i: (0, i, 0))],
+        out_specs=[pl.BlockSpec((ROWS_A, rank), lambda i: (i, 0))]
+        + [whole(o.shape) for o in outs[1:]],
+        out_shape=outs,
+        scratch_shapes=[
+            pltpu.VMEM((bands * depth, rank), jnp.bfloat16),
+            pltpu.VMEM((depth + 2 * EDGE, rank), jnp.float32),
+            pltpu.VMEM((2, rank, rank), jnp.float32),
         ],
-        out_specs=[pl.BlockSpec((ROWS_A, rank), lambda i: (i, 0)), whole((rank, rank))],
-        out_shape=[
-            jax.ShapeDtypeStruct((rows, rank), jnp.bfloat16),
-            jax.ShapeDtypeStruct((rank, rank), jnp.float32),
-        ],
-        scratch_shapes=[pltpu.VMEM((bands * depth, rank), jnp.bfloat16)],
         compiler_params=params(),
         name="contract_multi",
-    )(columns, band, response, image)
-
-
-def coarse_kernel(taps, columns, before, after, coarse, gram, wide):
-    edge = before.shape[0]
-    size = columns.shape[0]
-    wide[:edge, :] = before[...].astype(jnp.float32)
-    wide[edge : edge + size, :] = columns[...].astype(jnp.float32)
-    wide[edge + size :, :] = after[...].astype(jnp.float32)
-    total = jnp.zeros(coarse.shape, jnp.float32)
-    for offset in range(-W, W + 1):
-        total += taps[offset + W] * wide[pl.ds(edge + offset, size // DEC, stride=DEC), :]
-    coarse[...] = total
-    gram[...] = lax.dot_general(
-        total, total, (((0,), (0,)), ((), ())), precision=FULL_PRECISION,
-        preferred_element_type=jnp.float32,
-    )
-
-
-def coarsen(taps, columns, before, after):
-    size, rank = columns.shape
-    return pl.pallas_call(
-        coarse_kernel,
-        in_specs=[SMEM] + [whole(a.shape) for a in (columns, before, after)],
-        out_specs=[whole((size // DEC, rank)), whole((rank, rank))],
-        out_shape=[
-            jax.ShapeDtypeStruct((size // DEC, rank), jnp.float32),
-            jax.ShapeDtypeStruct((rank, rank), jnp.float32),
-        ],
-        scratch_shapes=[pltpu.VMEM((size + 2 * before.shape[0], rank), jnp.float32)],
-        compiler_params=params(),
-        name="coarsen",
-    )(taps, columns, before, after)
+    )(taps, place, gathered, band, response, in_hbm(image))
 
 
 def hyper_kernel(coarse, band, image, out, total):
@@ -147,32 +161,20 @@
         scratch_shapes=[pltpu.VMEM((rows, rank), jnp.float32)],
         compiler_params=params(),
         name="contract_hyper",
-    )(coarse, band, image)
-
-
-def two_halves(matrix):
-    high = matrix.astype(jnp.bfloat16)
-    low = (matrix - high.astype(jnp.float32)).astype(jnp.bfloat16)
-    return high, low
-
-
-def operator_kernel(
-    taps, band, response, column_gram, coarse_gram, hyper_out, multi_out, hyper_w, multi_w, bound
-):
+    )(coarse, band, in_hbm(image))
+
+
+def operator_kernel(taps, band, response, grams, hyper_out, multi_out, hyper_w, multi_w, bound):
     rank = band.shape[1]
-
-    def gram_of(values):
-        return lax.dot_general(
-            values, values, (((0,), (0,)), ((), ())), precision=FULL_PRECISION,
-            preferred_element_type=jnp.float32,
-        )
-
+    shares = grams.shape[0]
+    share = grams.shape[1] // 2
+    column_gram = jnp.concatenate([grams[i, :share, :] for i in range(shares)], axis=0)
+    coarse_gram = jnp.concatenate([grams[i, share:, :] for i in range(shares)], axis=0)
     merged = jnp.dot(
         response[...], band[...], precision=FULL_PRECISION, preferred_element_type=jnp.float32
     )
-    merged_gram = gram_of(merged)
-    hyper = coarse_gram[...] * gram_of(band[...])
-    multi = column_gram[...] * merged_gram
+    hyper = coarse_gram * gram_of(band[...])
+    multi = column_gram * gram_of(merged)
     eye = (
         lax.broadcasted_iota(jnp.int32, (rank, rank), 0)
         == lax.broadcasted_iota(jnp.int32, (rank, rank), 1)
@@ -207,7 +209,7 @@
         weights[rank:, rank:] = jnp.zeros_like(high)
 
 
-def make_operator(taps, band, response, column_gram, coarse_gram):
+def make_operator(taps, band, response, grams):
     rank = band.shape[1]
     square = jax.ShapeDtypeStruct((rank, rank), jnp.float32)
     weights = jax.ShapeDtypeStruct((2 * rank, 2 * rank), jnp.bfloat16)
@@ -215,12 +217,12 @@
     outs = [square, square, weights, weights, bound]
     return pl.pallas_call(
         operator_kernel,
-        in_specs=[SMEM] + [whole(a.shape) for a in (band, response, column_gram, coarse_gram)],
+        in_specs=[SMEM] + [whole(a.shape) for a in (band, response, grams)],
         out_specs=[whole(o.shape) for o in outs],
         out_shape=outs,
         compiler_params=params(),
         name="make_operator",
-    )(taps, band, response, column_gram, coarse_gram)
+    )(taps, band, response, grams)
 
 
 def times(values, weights):
@@ -269,7 +271,7 @@
     for which, out in ((0, multi), (1, hyper)):
         total = own[which][...].astype(jnp.float32)
         for number in range(count):
-            total += arrived[2 * number + which][...].astype(jnp.float32)
+            total += arrived[2 * number + which][: out.shape[0], :].astype(jnp.float32)
         out[...] = total
     first, second = DEC * RIM_MULTI, DEC * RIM_MULTI + RIM
     for pack, top in ((low, True), (high, False)):
@@ -371,6 +373,11 @@
         rows.append(jnp.sum(total, axis=0, keepdims=True))
     rows.append(jnp.zeros_like(rows[0]))
     block = jnp.concatenate(rows, axis=0)
+    lanes = block.shape[1]
+    half = block.shape[0] // 2
+    block = block + pltpu.roll(block, lanes // 2, 1)
+    lane = lax.broadcasted_iota(jnp.int32, (half, lanes), 1)
+    block = jnp.where(lane < lanes // 2, block[:half, :], block[half:, :])
     for device in range(devices):
         products[device] = block
 
@@ -382,7 +389,7 @@
     arrays = (multi, hyper, start, before, after, hyper_w, multi_w, bound)
     outs = [
         jax.ShapeDtypeStruct((ITERS + 1, DEC, coarse, rank), jnp.float32),
-        jax.ShapeDtypeStruct((devices, len(PAIRS) + 1, rank), jnp.float32),
+        jax.ShapeDtypeStruct((devices, (len(PAIRS) + 1) // 2, rank), jnp.float32),
     ]
     return pl.pallas_call(
         functools.partial(basis_kernel, devices),
@@ -399,10 +406,14 @@
     )(taps, *arrays)
 
 
-def advance_kernel(products, basis, start, bound, solution, residual, amplified):
+def coefficients_kernel(products, bound, out, trusted):
     count = ITERS + 1
-    sums = jnp.sum(products[...], axis=0)
-    sums = jnp.sum(sums, axis=1, keepdims=True)
+    folded = jnp.sum(products[...], axis=0)
+    lanes = folded.shape[1]
+    lane = lax.broadcasted_iota(jnp.int32, folded.shape, 1)
+    left = jnp.sum(jnp.where(lane < lanes // 2, folded, 0.0), axis=1, keepdims=True)
+    right = jnp.sum(jnp.where(lane < lanes // 2, 0.0, folded), axis=1, keepdims=True)
+    sums = jnp.concatenate([left, right], axis=0)
     inner = {}
     for number, (i, j) in enumerate(PAIRS):
         inner[i, j] = inner[j, i] = sums[number : number + 1, :]
@@ -455,37 +466,51 @@
                 c + ratio * heading[j] if j < len(heading) else c for j, c in enumerate(active)
             ]
             norm = following
-    amplified[...] = jnp.broadcast_to(worst, amplified.shape)
     scale = 4.0 / bound[0:1, 0:1]
-    walked = [c * scale for c in walked]
+    rows = [c * scale for c in walked] + rest
+    rows = jnp.concatenate(rows + [zero] * (out.shape[0] - len(rows)), axis=0)
+    out[...] = jnp.broadcast_to(rows, out.shape)
+    trusted[0] = jnp.where(worst < TRUST, 1, 0)[0, 0]
+
+
+def make_coefficients(products, bound):
+    rank = bound.shape[1]
+    return pl.pallas_call(
+        coefficients_kernel,
+        in_specs=[whole(products.shape), whole(bound.shape)],
+        out_specs=[whole((16, rank)), SMEM],
+        out_shape=[
+            jax.ShapeDtypeStruct((16, rank), jnp.float32),
+            jax.ShapeDtypeStruct((1,), jnp.int32),
+        ],
+        compiler_params=params(),
+        name="make_coefficients",
+    )(products, bound)
+
+
+def combine_kernel(coefficients, basis, start, solution, residual):
     coarse = basis.shape[2]
     for phase in range(DEC):
         rows = pl.ds(phase, coarse, stride=DEC)
         total = start[rows, :]
         for j in range(ITERS):
-            total += walked[j] * basis[j, phase]
+            total += coefficients[j : j + 1, :] * basis[j, phase]
         solution[rows, :] = total
-        total = rest[0] * basis[0, phase]
-        for j in range(1, count):
-            total += rest[j] * basis[j, phase]
+        total = coefficients[ITERS : ITERS + 1, :] * basis[0, phase]
+        for j in range(1, ITERS + 1):
+            total += coefficients[ITERS + j : ITERS + j + 1, :] * basis[j, phase]
         residual[rows, :] = total
 
 
-def advance(products, basis, start, bound):
-    rank = start.shape[1]
-    outs = [
-        jax.ShapeDtypeStruct(start.shape, jnp.float32),
-        jax.ShapeDtypeStruct(start.shape, jnp.float32),
-        jax.ShapeDtypeStruct((8, rank), jnp.float32),
-    ]
-    arrays = (products, basis, start, bound)
+def combine(coefficients, basis, start):
+    arrays = (coefficients, basis, start)
     return pl.pallas_call(
-        advance_kernel,
+        combine_kernel,
         in_specs=[whole(a.shape) for a in arrays],
-        out_specs=[whole(o.shape) for o in outs],
-        out_shape=outs,
+        out_specs=[whole(start.shape)] * 2,
+        out_shape=[jax.ShapeDtypeStruct(start.shape, jnp.float32)] * 2,
         compiler_params=params(),
-        name="advance",
+        name="combine",
     )(*arrays)
 
 
@@ -568,30 +593,40 @@
     taps = jnp.sum(
         jnp.where(offsets[:, None] == spread[None, :], blur_taps[:, None], jnp.float32(0.0)), axis=0
     )
-    columns = lax.all_gather(col_factor.T, "row", axis=0, tiled=True).T
-    edge = 2 * W
-    before = to_next(columns[-edge:], "col", across)
-    after = to_previous(columns[:edge], "col", across)
-    multi_part, column_part = contract_multi(columns, band_factor, response, multispectral)
+    transposed = col_factor.T
+    rank = band_factor.shape[1]
+    before = to_next(transposed[:, -EDGE:], "col", across)
+    after = to_previous(transposed[:, :EDGE], "col", across)
+    blank = jnp.zeros((transposed.shape[0], rank - 2 * EDGE), transposed.dtype)
+    gathered = lax.all_gather(
+        jnp.concatenate([transposed, before, after, blank], axis=1), "row", axis=0, tiled=True
+    )
+    share = rank // lax.axis_size("row")
+    multi_part, coarse, gram_part = contract_multi(
+        share, taps, lax.axis_index("row")[None], gathered, band_factor, response, multispectral
+    )
 
     fine = row_start.shape[0]
 
-    def exchange(values, size):
+    def exchange(values, size, more):
         arrived = []
         for distance in range(1, across):
             piece = lax.dynamic_slice_in_dim(values, (place + distance) % across * size, size, 0)
+            piece = jnp.concatenate([piece] + more)
             arrived.append(
                 lax.ppermute(piece, "col", [(i, (i + distance) % across) for i in range(across)])
             )
         return arrived
 
-    multi_arrived = exchange(multi_part, fine)
-    coarse, coarse_part = coarsen(taps, columns, before, after)
-    column_gram, coarse_gram = lax.psum((column_part, coarse_part), "col")
+    multi_arrived = exchange(multi_part, fine, [gram_part])
     hyper_part = contract_hyper(coarse, band_factor, hyperspectral)
-    hyper_arrived = exchange(hyper_part, fine // DEC)
+    hyper_arrived = exchange(hyper_part, fine // DEC, [])
+    gram = sum(a.astype(jnp.float32) for a in [gram_part] + [m[fine:] for m in multi_arrived])
+    gram = gram[: 2 * share] + gram[2 * share :]
+    gram, hyper_part = lax.optimization_barrier((gram, hyper_part))
+    grams = lax.all_gather(gram, "row")
     hyper_gram, multi_gram, hyper_w, multi_w, bound = make_operator(
-        taps, band_factor, response, column_gram, coarse_gram
+        taps, band_factor, response, grams
     )
     arrived = [a for pair in zip(multi_arrived, hyper_arrived) for a in pair]
     multi, hyper, low, high = add_sums(place[None], multi_part, hyper_part, arrived, row_start)
@@ -601,10 +636,10 @@
         devices, taps, multi, hyper, row_start, before_rows, after_rows, hyper_w, multi_w, bound
     )
     products = lax.all_to_all(products, BOTH, 0, 0, tiled=True)
-    solution, residual, amplified = advance(products, basis, row_start, bound)
+    coefficients, trusted = make_coefficients(products, bound)
     return lax.cond(
-        amplified[0, 0] < TRUST,
-        lambda: (solution, residual),
+        trusted[0] != 0,
+        lambda: tuple(combine(coefficients, basis, row_start)),
         lambda: step_by_step(taps, multi, hyper, row_start, hyper_gram, multi_gram, devices),
     )
 

time: 114 us -> 85 us (0.75)
  waiting for transfers between devices: 34.6 us -> 14.8 us
  between operations: 14.9 us -> 1.44 us
  blocking collectives: 10.8 us -> 18.6 us
  starting transfers between devices: 24.5 us -> 21.1 us
  local copies, waits for them, and re-layouts: 7.7 us -> 4.37 us
  Pallas kernels: 20.2 us -> 22.3 us
  other arithmetic: 0.09 us -> 1.61 us
    psum x1 -> x0, waiting for transfers between devices: 19.6 us -> none  [body(): column_gram, coarse_gram = lax.psum((column_part, coarse_part), 'col')]
    all_gather x1 -> x2, blocking collectives: 10.8 us -> 18.6 us  [the longest x1 9.44 us: body(): lax.all_gather(jnp.concatenate([transposed, before, after, blank], axis=1...]
    unnamed x21 -> x11, local copies, waits for them, and re-layouts: 6.32 us -> 2.45 us
    ppermute x6, starting transfers between devices: 11.1 us -> 8.05 us  [exchange(): lax.ppermute(piece, 'col', [(i, (i + distance) % across) for i in range(a...]
    ppermute x2, starting transfers between devices: 0.07 us -> 3.09 us  [to_next(): lax.ppermute(values, axis, [(i, (i + 1) % count) for i in range(count)])]
    pallas_call x3, Pallas kernels: 6.13 us -> 8.07 us  [the longest x1 6.34 us: contract_multi(): pl.pallas_call(functools.partial(multi_kernel, share), grid=(rows // ROWS...]
    all_to_all x1, waiting for transfers between devices: 10.2 us -> 8.4 us  [body(): products = lax.all_to_all(products, BOTH, 0, 0, tiled=True)]
    all_to_all x1, starting transfers between devices: 4.3 us -> 2.58 us  [body(): products = lax.all_to_all(products, BOTH, 0, 0, tiled=True)]
  transfers between devices with their start and end apart: 12 -> 11, of which waited for: 5 -> 5; matrix products, arithmetic and copies ran while one was open for 0% -> 1% of each run, Pallas kernels for 14% -> 12%
where the time goes in v2:
time: 85 us; the launch traced here: 84.4 us
  Pallas kernels  22.3 us (26%)
  starting transfers between devices  21.1 us (25%)
  blocking collectives  18.6 us (22%)
  waiting for transfers between devices  14.8 us (17%)
  local copies, waits for them, and re-layouts  4.37 us (5%)
  other arithmetic  1.61 us (2%)
  between operations  1.44 us (2%)
    all_gather x1, blocking collectives, body(): lax.all_gather(jnp.concatenate([transposed, before, after, blank], axis=1...  9.44 us
    all_gather x1, blocking collectives, body(): grams = lax.all_gather(gram, 'row')  9.18 us
    all_to_all x1, waiting for transfers between devices, body(): products = lax.all_to_all(products, BOTH, 0, 0, tiled=True)  8.4 us
    pallas_call x1, Pallas kernels, contract_hyper(): pl.pallas_call(hyper_kernel, grid=(bands // BANDS_B,), in_specs=[whole(co...  8.08 us
    ppermute x6, starting transfers between devices, exchange(): lax.ppermute(piece, 'col', [(i, (i + distance) % across) for i in range(a...  8.05 us
    ppermute x2, starting transfers between devices, to_previous(): lax.ppermute(values, axis, [((i + 1) % count, i) for i in range(count)])  7.36 us
    pallas_call x1, Pallas kernels, contract_multi(): pl.pallas_call(functools.partial(multi_kernel, share), grid=(rows // ROWS...  6.34 us
    ppermute x6, waiting for transfers between devices, exchange(): lax.ppermute(piece, 'col', [(i, (i + distance) % across) for i in range(a...  5.6 us
  transfers between devices with their start and end apart: 11, of which 5 were waited for; matrix products, arithmetic and copies ran while one was open for 1% of the time, Pallas kernels for 12%

profile of v2, /device:TPU:0, one launch (start us, length us, event | category | flops | bytes accessed | tf_op | source)
XLA Modules:
  0.0 84.4 jit_solution(10091081831271914607)
XLA Ops:
  0.6 1.0 %copy.406.refs_8_.start = f32[512,128]{1,0:T(8,128)S(1)} copy(f32[512,128]{1,0:T(8,128)} %param.14) | data formatting | bytes 524288
  1.6 0.8 fusion.117
  2.4 3.0 %collective-permute-start.6 = (bf16[16,16]{1,0:T(8,128)(2,1)S(1)}, bf16[16,16]{1,0:T(8,128)(2,1)S(1)}, u32[]{:S(2)}, u32[]{:S(2)}) collective-permute-start(bf16[16,16]{1,0:T(8,128)(2,1)S(1)} %get-tuple-element.227), channel_id=1, source_target_pairs={{0,1},{1,2},{2,3},{3,0},{4,5},{5,6},{6,7},{7,4},{8,9},{9,10},{10,1... | collective-permute-start | bytes 1544 | tf_op jit(solution)/shard_map/ppermute | solution.py:518
  5.5 2.0 %collective-permute-start.7 = (bf16[16,16]{1,0:T(8,128)(2,1)S(1)}, bf16[16,16]{1,0:T(8,128)(2,1)S(1)}, u32[]{:S(2)}, u32[]{:S(2)}) collective-permute-start(bf16[16,16]{1,0:T(8,128)(2,1)S(1)} %get-tuple-element.228), channel_id=1, source_target_pairs={{1,0},{2,1},{3,2},{0,3},{5,4},{6,5},{7,6},{4,7},{9,8},{10,9},{11,1... | collective-permute-start | bytes 1544 | tf_op jit(solution)/shard_map/ppermute | solution.py:522
  7.5 0.8 select_reduce_fusion.taps
  8.4 0.8 collective-permute-done.6
  9.1 0.8 maximum_maximum_fusion
  9.9 9.4 %all_gather.9.gathered = bf16[128,640]{1,0:T(8,128)(2,1)S(1)} all-gather(bf16[16,640]{1,0:T(8,128)(2,1)S(1)} %maximum_maximum_fusion), channel_id=1, replica_groups=mesh['row'=8,'col'=4] {'row'}, dimensions={0}, use_global_device_ids=true | all-gather | bytes 184320 | tf_op jit(solution)/shard_map/all_gather | solution.py:601
  19.3 0.8 copy-done
  20.1 0.7 copy-done.2
  20.8 6.3 %contract_multi.1 = (bf16[2048,128]{1,0:T(8,128)(2,1)S(1)}, f32[128,128]{1,0:T(8,128)S(1)}, bf16[64,128]{1,0:T(8,128)(2,1)S(1)}) custom-call(f32[17]{0:T(128)S(1)} %select_reduce_fusion.taps, s32[1]{0:T(128)} %bitcast.54.place, bf16[128,640]{1,0:T(8,128)(2,1)S(1)} %all_gather.9.gathered, f32[96,128]{1,0:T(8,128)S(1)} %copy-done, f32[2,96]{1,0:T(2,128)S(1)} %copy-done.2, ...), custom_call_target="tpu_custom_call" | custom-call | tf_op jit(solution)/shard_map/contract_multi/pallas_call | solution.py:107
  27.3 1.4 %collective-permute-start.8 = (bf16[576,128]{1,0:T(8,128)(2,1)S(1)}, bf16[576,128]{1,0:T(8,128)(2,1)S(1)}, u32[]{:S(2)}, u32[]{:S(2)}) collective-permute-start(bf16[576,128]{1,0:T(8,128)(2,1)S(1)} %get-tuple-element.224), channel_id=1, source_target_pairs={{0,1},{1,2},{2,3},{3,0},{4,5},{5,6},{6,7},{7,4},{8,9},{9,10},{10,1... | collective-permute-start | bytes 442376 | tf_op jit(solution)/shard_map/ppermute | solution.py:617
  28.7 3.0 %collective-permute-start.9 = (bf16[576,128]{1,0:T(8,128)(2,1)S(1)}, bf16[576,128]{1,0:T(8,128)(2,1)S(1)}, u32[]{:S(2)}, u32[]{:S(2)}) collective-permute-start(bf16[576,128]{1,0:T(8,128)(2,1)S(1)} %get-tuple-element.225), channel_id=1, source_target_pairs={{0,2},{1,3},{2,0},{3,1},{4,6},{5,7},{6,4},{7,5},{8,10},{9,11},{10,... | collective-permute-start | bytes 442376 | tf_op jit(solution)/shard_map/ppermute | solution.py:617
  31.7 0.9 %collective-permute-start.10 = (bf16[576,128]{1,0:T(8,128)(2,1)S(1)}, bf16[576,128]{1,0:T(8,128)(2,1)S(1)}, u32[]{:S(2)}, u32[]{:S(2)}) collective-permute-start(bf16[576,128]{1,0:T(8,128)(2,1)S(1)} %get-tuple-element.226), channel_id=1, source_target_pairs={{0,3},{1,0},{2,1},{3,2},{4,7},{5,4},{6,5},{7,6},{8,11},{9,8},{10,9... | collective-permute-start | bytes 442376 | tf_op jit(solution)/shard_map/ppermute | solution.py:617
  32.6 8.1 %contract_hyper.1.refs_1_ = bf16[512,128]{1,0:T(8,128)(2,1)S(1)} custom-call(f32[128,128]{1,0:T(8,128)S(1)} %get-tuple-element.92.coarse, f32[96,128]{1,0:T(8,128)S(1)} %copy-done.1, bf16[96,512,128]{2,1,0:T(8,128)(2,1)} %image.3), custom_call_target="tpu_custom_call" | custom-call | tf_op jit(solution)/shard_map/contract_hyper/pallas_call | solution.py:151
  40.7 0.6 collective-permute-start.13
  41.3 2.0 %collective-permute-start.12 = (bf16[128,128]{1,0:T(8,128)(2,1)S(1)}, bf16[128,128]{1,0:T(8,128)(2,1)S(1)}, u32[]{:S(2)}, u32[]{:S(2)}) collective-permute-start(bf16[128,128]{1,0:T(8,128)(2,1)S(1)} %get-tuple-element.222), channel_id=1, source_target_pairs={{0,2},{1,3},{2,0},{3,1},{4,6},{5,7},{6,4},{7,5},{8,10},{9,11},{10,... | collective-permute-start | bytes 98312 | tf_op jit(solution)/shard_map/ppermute | solution.py:617
  43.4 0.1 collective-permute-start.11
  43.5 1.2 %collective-permute-done.13.refs_7_ = bf16[128,128]{1,0:T(8,128)(2,1)S(1)} collective-permute-done((bf16[128,128]{1,0:T(8,128)(2,1)S(1)}, bf16[128,128]{1,0:T(8,128)(2,1)S(1)}, u32[]{:S(2)}, u32[]{:S(2)}) %collective-permute-start.13) | collective-permute-done | bytes 32800 | tf_op jit(solution)/shard_map/ppermute | solution.py:617
  44.7 2.0 %collective-permute-done.12.refs_5_ = bf16[128,128]{1,0:T(8,128)(2,1)S(1)} collective-permute-done((bf16[128,128]{1,0:T(8,128)(2,1)S(1)}, bf16[128,128]{1,0:T(8,128)(2,1)S(1)}, u32[]{:S(2)}, u32[]{:S(2)}) %collective-permute-start.12) | collective-permute-done | bytes 32800 | tf_op jit(solution)/shard_map/ppermute | solution.py:617
  46.7 2.3 %collective-permute-done.11.refs_3_ = bf16[128,128]{1,0:T(8,128)(2,1)S(1)} collective-permute-done((bf16[128,128]{1,0:T(8,128)(2,1)S(1)}, bf16[128,128]{1,0:T(8,128)(2,1)S(1)}, u32[]{:S(2)}, u32[]{:S(2)}) %collective-permute-start.11) | collective-permute-done | bytes 32800 | tf_op jit(solution)/shard_map/ppermute | solution.py:617
  49.1 0.1 add_sums.1
  49.2 5.3 %collective-permute-start.15 = (f32[184,128]{1,0:T(8,128)S(1)}, f32[184,128]{1,0:T(8,128)S(1)}, u32[]{:S(2)}, u32[]{:S(2)}) collective-permute-start(f32[184,128]{1,0:T(8,128)S(1)} %get-tuple-element.97), channel_id=1, source_target_pairs={{1,0},{2,1},{3,2},{4,3},{5,4},{6,5},{7,6},{8,7},{9,8},{10,9},{11,1... | collective-permute-start | bytes 282632 | tf_op jit(solution)/shard_map/ppermute | solution.py:522
  54.6 9.2 %all-gather = f32[256,128]{1,0:T(8,128)S(1)} all-gather(f32[32,128]{1,0:T(8,128)S(1)} %slice_add_fusion), channel_id=2, replica_groups=mesh['row'=8,'col'=4] {'row'}, dimensions={0}, use_global_device_ids=true | all-gather | bytes 147456 | tf_op jit(solution)/shard_map/all_gather | solution.py:627
  63.8 2.2 %make_operator.1 = (f32[128,128]{1,0:T(8,128)S(1)}, f32[128,128]{1,0:T(8,128)S(1)}, bf16[256,256]{1,0:T(8,128)(2,1)S(1)}, bf16[256,256]{1,0:T(8,128)(2,1)S(1)}, f32[8,128]{1,0:T(8,128)S(1)}) custom-call(f32[17]{0:T(128)S(1)} %select_reduce_fusion.taps, f32[96,128]{1,0:T(8,128)S(1)} %copy-done.1, f32[2,96]{1,0:T(2,128)S(1)} %copy-done.3, ...), custom_call_target="tpu_custom_call" | custom-call | tf_op jit(solution)/shard_map/make_operator/pallas_call | solution.py:218
  66.0 3.8 %make_basis.1 = (f32[5,4,128,128]{3,2,1,0:T(8,128)S(1)}, f32[32,8,128]{2,1,0:T(8,128)}) custom-call(f32[17]{0:T(128)S(1)} %select_reduce_fusion.taps, f32[512,128]{1,0:T(8,128)S(1)} %get-tuple-element.94.multi, f32[128,128]{1,0:T(8,128)S(1)} %get-tuple-element.95.hyper, f32[512,128]{1,0:T(8,128)S(1)} %copy.406.refs_8_.start, ...), custom_call_target="tpu_custom_call" | custom-call | tf_op jit(solution)/shard_map/make_basis/pallas_call | solution.py:394
  69.8 2.6 %all-to-all-start = ((f32[32,8,128]{2,1,0:T(8,128)}), f32[32,8,128]{2,1,0:T(8,128)S(1)}, u32[]{:S(2)}, u32[]{:S(2)}) async-start(f32[32,8,128]{2,1,0:T(8,128)} %get-tuple-element.102), calls=%async_computation | async-start | bytes 262144 | tf_op jit(solution)/shard_map/all_to_all | solution.py:638
  72.4 8.4 %all-to-all-done.products = f32[32,8,128]{2,1,0:T(8,128)S(1)} async-done(((f32[32,8,128]{2,1,0:T(8,128)}), f32[32,8,128]{2,1,0:T(8,128)S(1)}, u32[]{:S(2)}, u32[]{:S(2)}) %all-to-all-start) | async-done | bytes 131104 | tf_op jit(solution)/shard_map/all_to_all | solution.py:638
  80.8 0.8 make_coefficients.1
  82.2 2.1 %conditional.1 = ((f32[512,128]{1,0:T(8,128)}, f32[512,128]{1,0:T(8,128)})) conditional(s32[]{:T(128)} %bitcast.57, (f32[17]{0:T(128)S(1)}, f32[128,128]{1,0:T(8,128)S(1)}, f32[512,128]{1,0:T(8,128)S(1)}, f32[512,128]{1,0:T(8,128)}, f32[128,128]{1,0:T(8,128)S(1)}, /*index=5*/f32[128,128]{1,0:T(8,128)S(1)}) %tuple.138, (f32[16,128]{1,0:T(8,128)S(1)}, ...), branch_computations={%region_1.10_spmd, %region_10.11_spmd} | conditional | flops 257770496 | bytes 22511804 | solution.py:640
  82.5 1.0 %copy.405.start = f32[512,128]{1,0:T(8,128)S(1)} copy(f32[512,128]{1,0:T(8,128)} %get-tuple-element.69) | data formatting | bytes 524288 | tf_op jit(solution)/shard_map/cond
  83.4 0.9 %combine.1 = (f32[512,128]{1,0:T(8,128)}, f32[512,128]{1,0:T(8,128)}) custom-call(f32[16,128]{1,0:T(8,128)S(1)} %get-tuple-element.67.coefficients, f32[5,4,128,128]{3,2,1,0:T(8,128)S(1)} %get-tuple-element.68.basis, f32[512,128]{1,0:T(8,128)S(1)} %copy.405.start), custom_call_target="tpu_custom_call" | custom-call | tf_op jit(solution)/shard_map/cond/branch_1_fun/combine/pallas_call | solution.py:507
  (23 shorter events, 0.3 us)
Async XLA Ops:
  0.6 32.0 %copy-start.1 = (f32[96,128]{1,0:T(8,128)S(1)}, f32[96,128]{1,0:T(8,128)}, u32[]{:S(2)}) copy-start(f32[96,128]{1,0:T(8,128)} %band.5) | copy-start | bytes 147460
  1.6 80.6 %copy-start.5 = (f32[512,128]{1,0:T(8,128)}, f32[512,128]{1,0:T(8,128)S(1)}, u32[]{:S(2)}) copy-start(f32[512,128]{1,0:T(8,128)S(1)} %copy.406.refs_8_.start) | copy-start | bytes 786436
  2.4 6.7 %collective-permute-start.6 = (bf16[16,16]{1,0:T(8,128)(2,1)S(1)}, bf16[16,16]{1,0:T(8,128)(2,1)S(1)}, u32[]{:S(2)}, u32[]{:S(2)}) collective-permute-start(bf16[16,16]{1,0:T(8,128)(2,1)S(1)} %get-tuple-element.227), channel_id=1, source_target_pairs={{0,1},{1,2},{2,3},{3,0},{4,5},{5,6},{6,7},{7,4},{8,9},{9,10},{10,1... | collective-permute-start | bytes 1544 | tf_op jit(solution)/shard_map/ppermute | solution.py:518
  5.5 3.7 %collective-permute-start.7 = (bf16[16,16]{1,0:T(8,128)(2,1)S(1)}, bf16[16,16]{1,0:T(8,128)(2,1)S(1)}, u32[]{:S(2)}, u32[]{:S(2)}) collective-permute-start(bf16[16,16]{1,0:T(8,128)(2,1)S(1)} %get-tuple-element.228), channel_id=1, source_target_pairs={{1,0},{2,1},{3,2},{0,3},{5,4},{6,5},{7,6},{4,7},{9,8},{10,9},{11,1... | collective-permute-start | bytes 1544 | tf_op jit(solution)/shard_map/ppermute | solution.py:522
  19.3 0.8 copy-start
  20.1 0.7 copy-start.2
  27.3 16.1 %collective-permute-start.8 = (bf16[576,128]{1,0:T(8,128)(2,1)S(1)}, bf16[576,128]{1,0:T(8,128)(2,1)S(1)}, u32[]{:S(2)}, u32[]{:S(2)}) collective-permute-start(bf16[576,128]{1,0:T(8,128)(2,1)S(1)} %get-tuple-element.224), channel_id=1, source_target_pairs={{0,1},{1,2},{2,3},{3,0},{4,5},{5,6},{6,7},{7,4},{8,9},{9,10},{10,1... | collective-permute-start | bytes 442376 | tf_op jit(solution)/shard_map/ppermute | solution.py:617
  28.7 14.8 %collective-permute-start.9 = (bf16[576,128]{1,0:T(8,128)(2,1)S(1)}, bf16[576,128]{1,0:T(8,128)(2,1)S(1)}, u32[]{:S(2)}, u32[]{:S(2)}) collective-permute-start(bf16[576,128]{1,0:T(8,128)(2,1)S(1)} %get-tuple-element.225), channel_id=1, source_target_pairs={{0,2},{1,3},{2,0},{3,1},{4,6},{5,7},{6,4},{7,5},{8,10},{9,11},{10,... | collective-permute-start | bytes 442376 | tf_op jit(solution)/shard_map/ppermute | solution.py:617
  31.7 11.8 %collective-permute-start.10 = (bf16[576,128]{1,0:T(8,128)(2,1)S(1)}, bf16[576,128]{1,0:T(8,128)(2,1)S(1)}, u32[]{:S(2)}, u32[]{:S(2)}) collective-permute-start(bf16[576,128]{1,0:T(8,128)(2,1)S(1)} %get-tuple-element.226), channel_id=1, source_target_pairs={{0,3},{1,0},{2,1},{3,2},{4,7},{5,4},{6,5},{7,6},{8,11},{9,8},{10,9... | collective-permute-start | bytes 442376 | tf_op jit(solution)/shard_map/ppermute | solution.py:617
  32.6 31.2 %copy-start.3 = (f32[2,96]{1,0:T(2,128)S(1)}, f32[2,96]{1,0:T(2,128)}, u32[]{:S(2)}) copy-start(f32[2,96]{1,0:T(2,128)} %response.3) | copy-start | bytes 2308
  40.7 4.0 %collective-permute-start.13 = (bf16[128,128]{1,0:T(8,128)(2,1)S(1)}, bf16[128,128]{1,0:T(8,128)(2,1)S(1)}, u32[]{:S(2)}, u32[]{:S(2)}) collective-permute-start(bf16[128,128]{1,0:T(8,128)(2,1)S(1)} %get-tuple-element.221), channel_id=1, source_target_pairs={{0,3},{1,0},{2,1},{3,2},{4,7},{5,4},{6,5},{7,6},{8,11},{9,8},{10,9... | collective-permute-start | bytes 98312 | tf_op jit(solution)/shard_map/ppermute | solution.py:617
  41.3 5.4 %collective-permute-start.12 = (bf16[128,128]{1,0:T(8,128)(2,1)S(1)}, bf16[128,128]{1,0:T(8,128)(2,1)S(1)}, u32[]{:S(2)}, u32[]{:S(2)}) collective-permute-start(bf16[128,128]{1,0:T(8,128)(2,1)S(1)} %get-tuple-element.222), channel_id=1, source_target_pairs={{0,2},{1,3},{2,0},{3,1},{4,6},{5,7},{6,4},{7,5},{8,10},{9,11},{10,... | collective-permute-start | bytes 98312 | tf_op jit(solution)/shard_map/ppermute | solution.py:617
  43.4 5.7 %collective-permute-start.11 = (bf16[128,128]{1,0:T(8,128)(2,1)S(1)}, bf16[128,128]{1,0:T(8,128)(2,1)S(1)}, u32[]{:S(2)}, u32[]{:S(2)}) collective-permute-start(bf16[128,128]{1,0:T(8,128)(2,1)S(1)} %get-tuple-element.223), channel_id=1, source_target_pairs={{0,1},{1,2},{2,3},{3,0},{4,5},{5,6},{6,7},{7,4},{8,9},{9,10},{10,1... | collective-permute-start | bytes 98312 | tf_op jit(solution)/shard_map/ppermute | solution.py:617
  49.2 16.8 %collective-permute-start.14 = (f32[184,128]{1,0:T(8,128)S(1)}, f32[184,128]{1,0:T(8,128)S(1)}, u32[]{:S(2)}, u32[]{:S(2)}) collective-permute-start(f32[184,128]{1,0:T(8,128)S(1)} %get-tuple-element.96), channel_id=1, source_target_pairs={{0,1},{1,2},{2,3},{3,4},{4,5},{5,6},{6,7},{7,8},{8,9},{9,10},{10,1... | collective-permute-start | bytes 282632 | tf_op jit(solution)/shard_map/ppermute | solution.py:518
  49.2 16.7 %collective-permute-start.15 = (f32[184,128]{1,0:T(8,128)S(1)}, f32[184,128]{1,0:T(8,128)S(1)}, u32[]{:S(2)}, u32[]{:S(2)}) collective-permute-start(f32[184,128]{1,0:T(8,128)S(1)} %get-tuple-element.97), channel_id=1, source_target_pairs={{1,0},{2,1},{3,2},{4,3},{5,4},{6,5},{7,6},{8,7},{9,8},{10,9},{11,1... | collective-permute-start | bytes 282632 | tf_op jit(solution)/shard_map/ppermute | solution.py:522
  69.8 11.0 %all-to-all-start = ((f32[32,8,128]{2,1,0:T(8,128)}), f32[32,8,128]{2,1,0:T(8,128)S(1)}, u32[]{:S(2)}, u32[]{:S(2)}) async-start(f32[32,8,128]{2,1,0:T(8,128)} %get-tuple-element.102), calls=%async_computation | async-start | bytes 262144 | tf_op jit(solution)/shard_map/all_to_all | solution.py:638

commit v3 on v2

--- a/solution.py
+++ b/solution.py
@@ -14,14 +14,13 @@
 RIDGE_TERM = 0.1
 FULL_PRECISION = lax.Precision.HIGHEST
 BOTH = ("row", "col")
-ROWS_A = 256
-BANDS_B = 16
+ROWS_A = 512
 RIM = 24
 RIM_MULTI = 16
 PAIRS = [(i, j) for i in range(ITERS + 1) for j in range(i, ITERS + 1)]
 TRUST = 2.0e4
 EDGE = 16
-VMEM_LIMIT = 48 * 1024 * 1024
+VMEM_LIMIT = 32 * 1024 * 1024
 
 
 def params():
@@ -33,10 +32,11 @@
 
 
 SMEM = pl.BlockSpec(memory_space=pltpu.SMEM)
-
-
-def in_hbm(values):
-    return pltpu.with_memory_space_constraint(values, pltpu.HBM)
+VMEM = pl.BlockSpec(memory_space=pltpu.VMEM)
+
+
+def in_space(values, space):
+    return pltpu.with_memory_space_constraint(values, space)
 
 
 def two_halves(matrix):
@@ -52,133 +52,180 @@
     )
 
 
-def multi_kernel(
-    share, taps, place, gathered, band, response, image, out, coarse, gram, pairs, wide, grams
-):
+def load_kernel(parts, *refs):
+    count = len(parts)
+    copies = []
+    for source, target, number in zip(refs[:count], refs[count : 2 * count], parts):
+        size = source.shape[0] // number
+        for part in range(number):
+            rows = pl.ds(part * size, size)
+            copies.append(
+                pltpu.make_async_copy(
+                    source.at[rows], target.at[rows], refs[2 * count].at[len(copies)]
+                )
+            )
+    for copy in copies:
+        copy.start()
+    for copy in copies:
+        copy.wait()
+
+
+def load(arrays, parts, name):
+    size = sum(a.size * a.dtype.itemsize for a in arrays)
+    return pl.pallas_call(
+        functools.partial(load_kernel, parts),
+        in_specs=[pl.BlockSpec(memory_space=pl.ANY)] * len(arrays),
+        out_specs=[VMEM] * len(arrays),
+        out_shape=[pltpu.VMEM(a.shape, a.dtype) for a in arrays],
+        scratch_shapes=[pltpu.SemaphoreType.DMA((sum(parts),))],
+        compiler_params=params(),
+        cost_estimate=pl.CostEstimate(flops=0, bytes_accessed=2 * size, transcendentals=0),
+        name=name,
+    )(*[in_space(a, pltpu.HBM) for a in arrays])
+
+
+def in_rank_order(place, share, pieces, target):
+    pair = place[0] // 2
+    core = place[0] % 2
+    for distance, piece in enumerate(pieces):
+        slot = 2 * (pair ^ distance)
+        values = piece.astype(jnp.float32)
+        first = pl.multiple_of((slot + core) * share, share)
+        target[pl.ds(first, share), : values.shape[1]] = values[:share, :]
+        second = pl.multiple_of((slot + 1 - core) * share, share)
+        target[pl.ds(second, share), : values.shape[1]] = values[share:, :]
+
+
+def multi_kernel(count, place, band, response, image, *refs):
+    pieces = refs[:count]
+    out, columns, pairs, ranks = refs[count:]
     depth = image.shape[2]
     rank = out.shape[1]
-    edge = EDGE
-
-    @pl.when(pl.program_id(0) == 0)
-    def _():
-        for start in range(0, depth, rank):
-            square = gathered[:, start : start + rank].astype(jnp.float32)
-            wide[edge + start : edge + start + rank, :] = square.T
-        edges = gathered[:, depth : depth + rank].astype(jnp.float32).T
-        wide[:edge, :] = edges[:edge, :]
-        wide[edge + depth :, :] = edges[edge : 2 * edge, :]
-        columns = wide[edge : edge + depth, :]
-        merged = jnp.dot(
-            response[...], band[...], precision=FULL_PRECISION, preferred_element_type=jnp.float32
-        )
-        for k in range(2):
-            pairs[k * depth : (k + 1) * depth, :] = (merged[k : k + 1, :] * columns).astype(
-                jnp.bfloat16
-            )
-        total = jnp.zeros(coarse.shape, jnp.float32)
-        for offset in range(-W, W + 1):
-            total += taps[offset + W] * wide[pl.ds(edge + offset, depth // DEC, stride=DEC), :]
-        coarse[...] = total
-        exact = columns.astype(jnp.bfloat16)
-        grams[0] = lax.dot_general(
-            exact, exact, (((0,), (0,)), ((), ())), preferred_element_type=jnp.float32
-        )
-        grams[1] = gram_of(total)
-        first = pl.multiple_of(place[0] * share, share)
-        halves = two_halves(
-            jnp.concatenate([grams[0, pl.ds(first, share), :], grams[1, pl.ds(first, share), :]])
-        )
-        gram[: 2 * share, :] = halves[0]
-        gram[2 * share :, :] = halves[1]
-
-    total = jnp.dot(image[0], pairs[:depth, :], preferred_element_type=jnp.float32)
-    total += jnp.dot(image[1], pairs[depth:, :], preferred_element_type=jnp.float32)
-    out[...] = total.astype(jnp.bfloat16)
-
-
-def contract_multi(share, taps, place, gathered, band, response, image):
+    in_rank_order(place, pieces[0].shape[0] // 2, [p[...] for p in pieces], ranks)
+    for start in range(0, depth, rank):
+        columns[start : start + rank, :] = ranks[:, start : start + rank].T
+    merged = jnp.dot(
+        response[...], band[...], precision=FULL_PRECISION, preferred_element_type=jnp.float32
+    )
+    field = columns[...]
+    for k in range(2):
+        pairs[k * depth : (k + 1) * depth, :] = (merged[k : k + 1, :] * field).astype(jnp.bfloat16)
+    for start in range(0, out.shape[0], ROWS_A):
+        rows = slice(start, start + ROWS_A)
+        pixels = jnp.concatenate([image[0, rows, :], image[1, rows, :]], axis=1)
+        total = jnp.dot(pixels, pairs[...], preferred_element_type=jnp.float32)
+        out[rows, :] = total.astype(jnp.bfloat16)
+
+
+def contract_multi(place, band, response, image, pieces):
     bands, rows, depth = image.shape
     rank = band.shape[1]
     outs = [
         jax.ShapeDtypeStruct((rows, rank), jnp.bfloat16),
-        jax.ShapeDtypeStruct((depth // DEC, rank), jnp.float32),
-        jax.ShapeDtypeStruct((4 * share, rank), jnp.bfloat16),
+        jax.ShapeDtypeStruct((depth, rank), jnp.float32),
     ]
     return pl.pallas_call(
-        functools.partial(multi_kernel, share),
-        grid=(rows // ROWS_A,),
-        in_specs=[SMEM, SMEM]
-        + [whole(a.shape) for a in (gathered, band, response)]
-        + [pl.BlockSpec((bands, ROWS_A, depth), lambda i: (0, i, 0))],
-        out_specs=[pl.BlockSpec((ROWS_A, rank), lambda i: (i, 0))]
-        + [whole(o.shape) for o in outs[1:]],
+        functools.partial(multi_kernel, len(pieces)),
+        in_specs=[SMEM, whole(band.shape), whole(response.shape), VMEM]
+        + [whole(p.shape) for p in pieces],
+        out_specs=[whole(o.shape) for o in outs],
         out_shape=outs,
         scratch_shapes=[
             pltpu.VMEM((bands * depth, rank), jnp.bfloat16),
-            pltpu.VMEM((depth + 2 * EDGE, rank), jnp.float32),
-            pltpu.VMEM((2, rank, rank), jnp.float32),
+            pltpu.VMEM((rank, depth), jnp.float32),
         ],
         compiler_params=params(),
+        cost_estimate=pl.CostEstimate(
+            flops=2 * bands * rows * depth * rank, bytes_accessed=1 << 23, transcendentals=0
+        ),
         name="contract_multi",
-    )(taps, place, gathered, band, response, in_hbm(image))
-
-
-def hyper_kernel(coarse, band, image, out, total):
-    step = pl.program_id(0)
-    field = coarse[...]
+    )(place, band, response, in_space(image, pltpu.VMEM), *pieces)
+
+
+def hyper_kernel(share, place, taps, columns, before, after, band, image, out, gram, wide, ranks, packed):
+    depth, rank = columns.shape
+    wide[EDGE : EDGE + depth, :] = columns[...]
+    for edge, first in ((before, 0), (after, EDGE + depth)):
+        values = edge[...].astype(jnp.float32)
+        size = 2 * share
+        in_rank_order(
+            place, share, [values[i : i + size, :] for i in range(0, rank, size)], ranks
+        )
+        wide[first : first + EDGE, :] = ranks[...].T[:EDGE, :]
+    coarse = jnp.zeros((depth // DEC, rank), jnp.float32)
+    for offset in range(-W, W + 1):
+        coarse += taps[offset + W] * wide[pl.ds(EDGE + offset, depth // DEC, stride=DEC), :]
+
+    exact = columns[...].astype(jnp.bfloat16)
+    fine_gram = lax.dot_general(
+        exact, exact, (((0,), (0,)), ((), ())), preferred_element_type=jnp.float32
+    )
+    coarse_gram = gram_of(coarse)
+    down = lax.broadcasted_iota(jnp.int32, (rank, rank), 0)
+    along = lax.broadcasted_iota(jnp.int32, (rank, rank), 1)
+    packed[:rank, :] = jnp.where(along >= down, fine_gram, coarse_gram)
+    diagonal = jnp.sum(jnp.where(along == down, coarse_gram, 0.0), axis=0, keepdims=True)
+    packed[rank:, :] = jnp.broadcast_to(diagonal, (packed.shape[0] - rank, rank))
+    half = packed.shape[0] // 2
+    part = packed[pl.ds(pl.multiple_of(place[0] % 2 * half, 8), half), :]
+    high = part.astype(jnp.bfloat16).astype(jnp.float32)
+    gram[...] = jnp.concatenate([high, part - high], axis=0).astype(jnp.bfloat16)
+
+    bands = image.shape[0]
     pairs = jnp.concatenate(
-        [(band[k : k + 1, :] * field).astype(jnp.bfloat16) for k in range(BANDS_B)], axis=0
-    )
-    pixels = jnp.concatenate([image[k] for k in range(BANDS_B)], axis=1)
-    part = jnp.dot(pixels, pairs, preferred_element_type=jnp.float32)
-
-    @pl.when(step == 0)
-    def _():
-        total[...] = part
-
-    @pl.when(step > 0)
-    def _():
-        total[...] += part
-
-    @pl.when(step == pl.num_programs(0) - 1)
-    def _():
-        out[...] = total[...].astype(jnp.bfloat16)
-
-
-def contract_hyper(coarse, band, image):
+        [(band[k : k + 1, :] * coarse).astype(jnp.bfloat16) for k in range(bands)], axis=0
+    )
+    pixels = jnp.concatenate([image[k] for k in range(bands)], axis=1)
+    total = jnp.dot(pixels, pairs, preferred_element_type=jnp.float32)
+    out[...] = total.astype(jnp.bfloat16)
+
+
+def contract_hyper(share, place, taps, columns, before, after, band, image):
     bands, rows, depth = image.shape
-    rank = coarse.shape[1]
-    return pl.pallas_call(
-        hyper_kernel,
-        grid=(bands // BANDS_B,),
-        in_specs=[
-            whole(coarse.shape),
-            pl.BlockSpec((BANDS_B, rank), lambda i: (i, 0)),
-            pl.BlockSpec((BANDS_B, rows, depth), lambda i: (i, 0, 0)),
+    fine, rank = columns.shape
+    outs = [
+        jax.ShapeDtypeStruct((rows, rank), jnp.bfloat16),
+        jax.ShapeDtypeStruct((rank + 16, rank), jnp.bfloat16),
+    ]
+    return pl.pallas_call(
+        functools.partial(hyper_kernel, share),
+        in_specs=[SMEM, SMEM] + [whole(a.shape) for a in (columns, before, after, band)] + [VMEM],
+        out_specs=[whole(o.shape) for o in outs],
+        out_shape=outs,
+        scratch_shapes=[
+            pltpu.VMEM((fine + 2 * EDGE, rank), jnp.float32),
+            pltpu.VMEM((rank, rank), jnp.float32),
+            pltpu.VMEM((rank + 16, rank), jnp.float32),
         ],
-        out_specs=whole((rows, rank)),
-        out_shape=jax.ShapeDtypeStruct((rows, rank), jnp.bfloat16),
-        scratch_shapes=[pltpu.VMEM((rows, rank), jnp.float32)],
-        compiler_params=params(),
+        compiler_params=params(),
+        cost_estimate=pl.CostEstimate(
+            flops=2 * bands * rows * depth * rank, bytes_accessed=1 << 24, transcendentals=0
+        ),
         name="contract_hyper",
-    )(coarse, band, in_hbm(image))
-
-
-def operator_kernel(taps, band, response, grams, hyper_out, multi_out, hyper_w, multi_w, bound):
+    )(place, taps, columns, before, after, band, in_space(image, pltpu.VMEM))
+
+
+def operator_kernel(
+    place, taps, band, response, own, other, hyper_out, multi_out, hyper_w, multi_w, bound
+):
     rank = band.shape[1]
-    shares = grams.shape[0]
-    share = grams.shape[1] // 2
-    column_gram = jnp.concatenate([grams[i, :share, :] for i in range(shares)], axis=0)
-    coarse_gram = jnp.concatenate([grams[i, share:, :] for i in range(shares)], axis=0)
+    even = place[0] % 2 == 0
+    lower = jnp.where(even, own[...], other[...])
+    upper = jnp.where(even, other[...], own[...])
+    packed = jnp.concatenate([lower, upper], axis=0)
+    diagonal = packed[rank : rank + 1, :]
+    packed = packed[:rank, :]
+    turned = packed.T
+    down = lax.broadcasted_iota(jnp.int32, (rank, rank), 0)
+    along = lax.broadcasted_iota(jnp.int32, (rank, rank), 1)
+    column_gram = jnp.where(along >= down, packed, turned)
+    coarse_gram = jnp.where(along < down, packed, jnp.where(along == down, diagonal, turned))
     merged = jnp.dot(
         response[...], band[...], precision=FULL_PRECISION, preferred_element_type=jnp.float32
     )
     hyper = coarse_gram * gram_of(band[...])
     multi = column_gram * gram_of(merged)
-    eye = (
-        lax.broadcasted_iota(jnp.int32, (rank, rank), 0)
-        == lax.broadcasted_iota(jnp.int32, (rank, rank), 1)
-    ).astype(jnp.float32)
+    eye = (along == down).astype(jnp.float32)
     multi = multi + RIDGE_TERM * eye
     hyper_out[...] = hyper
     multi_out[...] = multi
@@ -209,7 +256,7 @@
         weights[rank:, rank:] = jnp.zeros_like(high)
 
 
-def make_operator(taps, band, response, grams):
+def make_operator(place, taps, band, response, own, other):
     rank = band.shape[1]
     square = jax.ShapeDtypeStruct((rank, rank), jnp.float32)
     weights = jax.ShapeDtypeStruct((2 * rank, 2 * rank), jnp.bfloat16)
@@ -217,12 +264,12 @@
     outs = [square, square, weights, weights, bound]
     return pl.pallas_call(
         operator_kernel,
-        in_specs=[SMEM] + [whole(a.shape) for a in (band, response, grams)],
+        in_specs=[SMEM, SMEM] + [whole(a.shape) for a in (band, response, own, other)],
         out_specs=[whole(o.shape) for o in outs],
         out_shape=outs,
         compiler_params=params(),
         name="make_operator",
-    )(taps, band, response, grams)
+    )(place, taps, band, response, own, other)
 
 
 def times(values, weights):
@@ -262,17 +309,46 @@
     return total
 
 
+def sum_kernel(place, own, *refs):
+    del place
+    total = own[...].astype(jnp.float32)
+    for values in refs[:-1]:
+        total += values[...].astype(jnp.float32)
+    refs[-1][...] = total
+
+
+def sum_arrived(place, own, arrived):
+    shape = arrived[0].shape
+    return pl.pallas_call(
+        sum_kernel,
+        grid_spec=pltpu.PrefetchScalarGridSpec(
+            num_scalar_prefetch=1,
+            grid=(1,),
+            in_specs=[pl.BlockSpec(shape, lambda i, place: (place[0], 0))]
+            + [whole(shape) for _ in arrived],
+            out_specs=whole(shape),
+        ),
+        out_shape=jax.ShapeDtypeStruct(shape, jnp.float32),
+        compiler_params=params(),
+        cost_estimate=pl.CostEstimate(flops=0, bytes_accessed=1 << 26, transcendentals=0),
+        name="sum_arrived",
+    )(place, own, *arrived)
+
+
 def sums_kernel(count, place, *refs):
     del place
-    own = refs[:2]
-    arrived = refs[2 : 2 + 2 * count]
-    start = refs[2 + 2 * count]
-    multi, hyper, low, high = refs[3 + 2 * count :]
-    for which, out in ((0, multi), (1, hyper)):
-        total = own[which][...].astype(jnp.float32)
-        for number in range(count):
-            total += arrived[2 * number + which][: out.shape[0], :].astype(jnp.float32)
-        out[...] = total
+    own, own_gram, multi, start = refs[:4]
+    arrived = refs[4 : 4 + count]
+    hyper, gram, low, high = refs[4 + count :]
+    rows = hyper.shape[0]
+    total = own[...].astype(jnp.float32)
+    grams = own_gram[...].astype(jnp.float32)
+    for values in arrived:
+        total += values[:rows, :].astype(jnp.float32)
+        grams += values[rows:, :].astype(jnp.float32)
+    hyper[...] = total
+    half = gram.shape[0]
+    gram[...] = grams[:half, :] + grams[half:, :]
     first, second = DEC * RIM_MULTI, DEC * RIM_MULTI + RIM
     for pack, top in ((low, True), (high, False)):
         for source, begin, size in (
@@ -285,34 +361,29 @@
             pack[begin : begin + size, :] = source[at : at + size, :]
 
 
-def add_sums(place, multi_part, hyper_part, arrived, start):
+def add_sums(place, hyper_part, gram_part, multi, start, arrived):
     fine, rank = start.shape
     coarse = fine // DEC
-    count = len(arrived) // 2
     pack = jax.ShapeDtypeStruct((DEC * RIM_MULTI + RIM + DEC * RIM, rank), jnp.float32)
     outs = [
-        jax.ShapeDtypeStruct((fine, rank), jnp.float32),
         jax.ShapeDtypeStruct((coarse, rank), jnp.float32),
+        jax.ShapeDtypeStruct((gram_part.shape[0] // 2, rank), jnp.float32),
         pack,
         pack,
     ]
     return pl.pallas_call(
-        functools.partial(sums_kernel, count),
+        functools.partial(sums_kernel, len(arrived)),
         grid_spec=pltpu.PrefetchScalarGridSpec(
             num_scalar_prefetch=1,
             grid=(1,),
-            in_specs=[
-                pl.BlockSpec((fine, rank), lambda i, place: (place[0], 0)),
-                pl.BlockSpec((coarse, rank), lambda i, place: (place[0], 0)),
-            ]
-            + [whole(a.shape) for a in arrived]
-            + [whole(start.shape)],
+            in_specs=[pl.BlockSpec((coarse, rank), lambda i, place: (place[0], 0))]
+            + [whole(a.shape) for a in (gram_part, multi, start, *arrived)],
             out_specs=[whole(o.shape) for o in outs],
         ),
         out_shape=outs,
         compiler_params=params(),
         name="add_sums",
-    )(place, multi_part, hyper_part, *arrived, start)
+    )(place, hyper_part, gram_part, multi, start, *arrived)
 
 
 def basis_kernel(
@@ -334,6 +405,7 @@
     natural[DEC * RIM + fine :, :] = after[second:, :]
     for phase in range(DEC):
         held[1, phase] = natural[pl.ds(phase, wide, stride=DEC), :]
+        basis[ITERS + 1, phase] = held[1, phase, own, :]
     mapped = apply(lambda phase: held[1, phase])
 
     lifted[:RIM, :] = before[first:second, :]
@@ -388,7 +460,7 @@
     wide = coarse + 2 * RIM
     arrays = (multi, hyper, start, before, after, hyper_w, multi_w, bound)
     outs = [
-        jax.ShapeDtypeStruct((ITERS + 1, DEC, coarse, rank), jnp.float32),
+        jax.ShapeDtypeStruct((ITERS + 2, DEC, coarse, rank), jnp.float32),
         jax.ShapeDtypeStruct((devices, (len(PAIRS) + 1) // 2, rank), jnp.float32),
     ]
     return pl.pallas_call(
@@ -488,11 +560,11 @@
     )(products, bound)
 
 
-def combine_kernel(coefficients, basis, start, solution, residual):
+def combine_kernel(coefficients, basis, solution, residual):
     coarse = basis.shape[2]
     for phase in range(DEC):
         rows = pl.ds(phase, coarse, stride=DEC)
-        total = start[rows, :]
+        total = basis[ITERS + 1, phase]
         for j in range(ITERS):
             total += coefficients[j : j + 1, :] * basis[j, phase]
         solution[rows, :] = total
@@ -502,13 +574,14 @@
         residual[rows, :] = total
 
 
-def combine(coefficients, basis, start):
-    arrays = (coefficients, basis, start)
+def combine(coefficients, basis):
+    arrays = (coefficients, basis)
+    out = jax.ShapeDtypeStruct((DEC * basis.shape[2], basis.shape[3]), jnp.float32)
     return pl.pallas_call(
         combine_kernel,
         in_specs=[whole(a.shape) for a in arrays],
-        out_specs=[whole(start.shape)] * 2,
-        out_shape=[jax.ShapeDtypeStruct(start.shape, jnp.float32)] * 2,
+        out_specs=[whole(out.shape)] * 2,
+        out_shape=[out] * 2,
         compiler_params=params(),
         name="combine",
     )(*arrays)
@@ -587,61 +660,69 @@
     multispectral, hyperspectral, row_start, col_factor, band_factor, response, blur_taps, offsets
 ):
     across = lax.axis_size("col")
-    devices = across * lax.axis_size("row")
+    along = lax.axis_size("row")
+    devices = across * along
     place = lax.axis_index("col")
+    row = lax.axis_index("row")[None]
+    rank = band_factor.shape[1]
+    share = rank // along
+    fine = row_start.shape[0]
+
+    def exchanged(values, distance):
+        return lax.ppermute(values, "row", [(i, i ^ distance) for i in range(along)])
+
+    own = col_factor.T
+    pair = jnp.concatenate([own, exchanged(own, 1)])
+    multispectral, band_factor, response, row_start = load(
+        (multispectral, band_factor, response, row_start), (2, 1, 1, 1), "load_multi"
+    )
+    pair, hyperspectral = lax.optimization_barrier((pair, hyperspectral))
+    pieces = [pair] + [exchanged(pair, distance) for distance in range(2, along, 2)]
+    (hyperspectral,) = load((hyperspectral,), (8,), "load_hyper")
+    before = to_next(jnp.concatenate([p[:, -EDGE:] for p in pieces]), "col", across)
+    after = to_previous(jnp.concatenate([p[:, :EDGE] for p in pieces]), "col", across)
     spread = jnp.arange(-W, W + 1, dtype=jnp.int32)
     taps = jnp.sum(
         jnp.where(offsets[:, None] == spread[None, :], blur_taps[:, None], jnp.float32(0.0)), axis=0
     )
-    transposed = col_factor.T
-    rank = band_factor.shape[1]
-    before = to_next(transposed[:, -EDGE:], "col", across)
-    after = to_previous(transposed[:, :EDGE], "col", across)
-    blank = jnp.zeros((transposed.shape[0], rank - 2 * EDGE), transposed.dtype)
-    gathered = lax.all_gather(
-        jnp.concatenate([transposed, before, after, blank], axis=1), "row", axis=0, tiled=True
-    )
-    share = rank // lax.axis_size("row")
-    multi_part, coarse, gram_part = contract_multi(
-        share, taps, lax.axis_index("row")[None], gathered, band_factor, response, multispectral
-    )
-
-    fine = row_start.shape[0]
+    multi_part, columns = contract_multi(row, band_factor, response, multispectral, pieces)
 
     def exchange(values, size, more):
         arrived = []
         for distance in range(1, across):
             piece = lax.dynamic_slice_in_dim(values, (place + distance) % across * size, size, 0)
-            piece = jnp.concatenate([piece] + more)
+            if more:
+                piece = jnp.concatenate([piece] + more)
             arrived.append(
                 lax.ppermute(piece, "col", [(i, (i + distance) % across) for i in range(across)])
             )
         return arrived
 
-    multi_arrived = exchange(multi_part, fine, [gram_part])
-    hyper_part = contract_hyper(coarse, band_factor, hyperspectral)
-    hyper_arrived = exchange(hyper_part, fine // DEC, [])
-    gram = sum(a.astype(jnp.float32) for a in [gram_part] + [m[fine:] for m in multi_arrived])
-    gram = gram[: 2 * share] + gram[2 * share :]
-    gram, hyper_part = lax.optimization_barrier((gram, hyper_part))
-    grams = lax.all_gather(gram, "row")
-    hyper_gram, multi_gram, hyper_w, multi_w, bound = make_operator(
-        taps, band_factor, response, grams
-    )
-    arrived = [a for pair in zip(multi_arrived, hyper_arrived) for a in pair]
-    multi, hyper, low, high = add_sums(place[None], multi_part, hyper_part, arrived, row_start)
+    multi_arrived = exchange(multi_part, fine, [])
+    hyper_part, gram_part = contract_hyper(
+        share, row, taps, columns, before, after, band_factor, hyperspectral
+    )
+    hyper_arrived = exchange(hyper_part, fine // DEC, [gram_part])
+    multi = sum_arrived(place[None], multi_part, multi_arrived)
+    hyper, gram, low, high = add_sums(
+        place[None], hyper_part, gram_part, multi, row_start, hyper_arrived
+    )
     before_rows = to_next(high, BOTH, devices)
     after_rows = to_previous(low, BOTH, devices)
+    hyper_gram, multi_gram, hyper_w, multi_w, bound = make_operator(
+        row, taps, band_factor, response, gram, exchanged(gram, 1)
+    )
     basis, products = make_basis(
         devices, taps, multi, hyper, row_start, before_rows, after_rows, hyper_w, multi_w, bound
     )
     products = lax.all_to_all(products, BOTH, 0, 0, tiled=True)
     coefficients, trusted = make_coefficients(products, bound)
-    return lax.cond(
-        trusted[0] != 0,
-        lambda: tuple(combine(coefficients, basis, row_start)),
-        lambda: step_by_step(taps, multi, hyper, row_start, hyper_gram, multi_gram, devices),
-    )
+
+    def from_start():
+        start = jnp.stack(list(basis[ITERS + 1]), axis=1).reshape(fine, rank)
+        return step_by_step(taps, multi, hyper, start, hyper_gram, multi_gram, devices)
+
+    return lax.cond(trusted[0] != 0, lambda: tuple(combine(coefficients, basis)), from_start)
 
 
 def solution(mesh):

time: 85 us -> 66.6 us (0.78)
  blocking collectives: 18.6 us -> 0 us
  starting transfers between devices: 21.1 us -> 25.8 us
  local copies, waits for them, and re-layouts: 4.37 us -> 0.36 us
  waiting for transfers between devices: 14.8 us -> 17.1 us
  Pallas kernels: 22.3 us -> 20.5 us
    all_gather x2 -> x0, blocking collectives: 18.6 us -> none  [the longest x1 9.44 us: body(): lax.all_gather(jnp.concatenate([transposed, before, after, blank], axis=1...]
    ppermute x0 -> x5, starting transfers between devices: none -> 4.67 us  [exchanged(): lax.ppermute(values, 'row', [(i, i ^ distance) for i in range(along)])]
    unnamed x11 -> x2, local copies, waits for them, and re-layouts: 2.45 us -> 0.01 us
    all_to_all x1, starting transfers between devices: 2.58 us -> 4.55 us  [body(): products = lax.all_to_all(products, BOTH, 0, 0, tiled=True)]
    ppermute x6, waiting for transfers between devices: 5.6 us -> 7.48 us  [exchange(): lax.ppermute(piece, 'col', [(i, (i + distance) % across) for i in range(a...]
    pallas_call x4 -> x7, Pallas kernels: 16.7 us -> 15 us  [the longest x2 6.99 us: load(): pl.pallas_call(functools.partial(load_kernel, parts), in_specs=[pl.BlockS...]
    ppermute x0 -> x5, waiting for transfers between devices: none -> 1.22 us  [exchanged(): lax.ppermute(values, 'row', [(i, i ^ distance) for i in range(along)])]
    ppermute x6, starting transfers between devices: 8.05 us -> 7.08 us  [exchange(): lax.ppermute(piece, 'col', [(i, (i + distance) % across) for i in range(a...]
  transfers between devices with their start and end apart: 11 -> 16, of which waited for: 5 -> 4; matrix products, arithmetic and copies ran while one was open for 1% -> 2% of each run, Pallas kernels for 12% -> 23%
where the time goes in v3:
time: 66.6 us; the launch traced here: 66.4 us
  starting transfers between devices  25.8 us (39%)
  Pallas kernels  20.5 us (31%)
  waiting for transfers between devices  17.1 us (26%)
  between operations  1.51 us (2%)
  other arithmetic  0.81 us (1%)
    all_to_all x1, waiting for transfers between devices, body(): products = lax.all_to_all(products, BOTH, 0, 0, tiled=True)  8.4 us
    ppermute x6, waiting for transfers between devices, exchange(): lax.ppermute(piece, 'col', [(i, (i + distance) % across) for i in range(a...  7.48 us
    ppermute x2, starting transfers between devices, to_previous(): lax.ppermute(values, axis, [((i + 1) % count, i) for i in range(count)])  7.12 us
    ppermute x6, starting transfers between devices, exchange(): lax.ppermute(piece, 'col', [(i, (i + distance) % across) for i in range(a...  7.08 us
    pallas_call x2, Pallas kernels, load(): pl.pallas_call(functools.partial(load_kernel, parts), in_specs=[pl.BlockS...  6.99 us
    ppermute x5, starting transfers between devices, exchanged(): lax.ppermute(values, 'row', [(i, i ^ distance) for i in range(along)])  4.67 us
    all_to_all x1, starting transfers between devices, body(): products = lax.all_to_all(products, BOTH, 0, 0, tiled=True)  4.55 us
    pallas_call x1, Pallas kernels, contract_hyper(): pl.pallas_call(functools.partial(hyper_kernel, share), in_specs=[SMEM, SM...  4.18 us
  transfers between devices with their start and end apart: 16, of which 4 were waited for; matrix products, arithmetic and copies ran while one was open for 2% of the time, Pallas kernels for 23%

profile of v3, /device:TPU:0, one launch (start us, length us, event | category | flops | bytes accessed | tf_op | source)
XLA Modules:
  0.0 66.4 jit_solution(9893160245326014458)
XLA Ops:
  0.6 0.5 collective-permute-start.6
  1.2 0.8 %select_reduce_fusion.taps = f32[17]{0:T(128)S(1)} fusion(f32[9]{0:T(128)} %param.18, s32[17]{0:T(128)S(1)} %iota_add_fusion, s32[9]{0:T(128)} %param.19), kind=kLoop, calls=%fused_computation.155 | loop fusion | flops 442 | bytes 208 | tf_op jit(solution)/shard_map/reduce_sum | solution.py:685
  2.0 2.3 %load_multi.1 = (bf16[2,2048,512]{2,1,0:T(8,128)(2,1)S(1)}, f32[96,128]{1,0:T(8,128)S(1)}, f32[2,96]{1,0:T(2,128)S(1)}, f32[512,128]{1,0:T(8,128)S(1)}) custom-call(bf16[2,2048,512]{2,1,0:T(8,128)(2,1)} %refs_0_.1, f32[96,128]{1,0:T(8,128)} %refs_1_.1, f32[2,96]{1,0:T(2,128)} %refs_2_.1, f32[512,128]{1,0:T(8,128)} %refs_3_.1), custom_call_target="tpu_custom_call" | custom-call | bytes 9012736 | tf_op jit(solution)/shard_map/load_multi/pallas_call | solution.py:75
  4.3 3.5 %collective-permute-start.9 = (bf16[32,512]{1,0:T(8,128)(2,1)S(1)}, bf16[32,512]{1,0:T(8,128)(2,1)S(1)}, u32[]{:S(2)}, u32[]{:S(2)}) collective-permute-start(bf16[32,512]{1,0:T(8,128)(2,1)S(1)} %pad_maximum_fusion.10.refs_0_), channel_id=1, source_target_pairs={{0,24},{4,28},{8,16},{12,20},{16,8},{20,12},{24,0},{28,4},{1,25},{... | collective-permute-start | bytes 98312 | tf_op jit(solution)/shard_map/ppermute | solution.py:672
  7.8 0.1 fusion.117
  7.9 0.5 collective-permute-start.8
  8.4 0.1 collective-permute-start.7
  8.5 4.7 %load_hyper.1.image = bf16[96,512,128]{2,1,0:T(8,128)(2,1)S(1)} custom-call(bf16[96,512,128]{2,1,0:T(8,128)(2,1)} %refs_0_.2), custom_call_target="tpu_custom_call" | custom-call | bytes 25165824 | tf_op jit(solution)/shard_map/load_hyper/pallas_call | solution.py:75
  13.3 0.1 fusion.120
  13.3 0.1 fusion.119
  13.4 0.1 fusion.118
  13.5 2.1 %collective-permute-start.13 = (bf16[128,16]{1,0:T(8,128)(2,1)S(1)}, bf16[128,16]{1,0:T(8,128)(2,1)S(1)}, u32[]{:S(2)}, u32[]{:S(2)}) collective-permute-start(bf16[128,16]{1,0:T(8,128)(2,1)S(1)} %pad_maximum_fusion.11), channel_id=1, source_target_pairs={{0,1},{1,2},{2,3},{3,0},{4,5},{5,6},{6,7},{7,4},{8,9},{9,10},{10,1... | collective-permute-start | bytes 12296 | tf_op jit(solution)/shard_map/ppermute | solution.py:591
  15.6 2.1 %collective-permute-start.14 = (bf16[128,16]{1,0:T(8,128)(2,1)S(1)}, bf16[128,16]{1,0:T(8,128)(2,1)S(1)}, u32[]{:S(2)}, u32[]{:S(2)}) collective-permute-start(bf16[128,16]{1,0:T(8,128)(2,1)S(1)} %pad_maximum_fusion.12), channel_id=1, source_target_pairs={{1,0},{2,1},{3,2},{0,3},{5,4},{6,5},{7,6},{4,7},{9,8},{10,9},{11,1... | collective-permute-start | bytes 12296 | tf_op jit(solution)/shard_map/ppermute | solution.py:595
  17.7 1.5 %contract_multi.1 = (bf16[2048,128]{1,0:T(8,128)(2,1)S(1)}, f32[512,128]{1,0:T(8,128)S(1)}) custom-call(s32[1]{0:T(128)} %bitcast.61.place, f32[96,128]{1,0:T(8,128)S(1)} %get-tuple-element.92.band, f32[2,96]{1,0:T(2,128)S(1)} %get-tuple-element.93.response, bf16[2,2048,512]{2,1,0:T(8,128)(2,1)S(1)} %get-tuple-element.94.image, ...), custom_call_target="tpu_custom_call" | custom-call | flops 536870912 | bytes 8388608 | tf_op jit(solution)/shard_map/contract_multi/pallas_call | solution.py:127
  19.3 2.1 %collective-permute-start.12 = (bf16[512,128]{1,0:T(8,128)(2,1)S(1)}, bf16[512,128]{1,0:T(8,128)(2,1)S(1)}, u32[]{:S(2)}, u32[]{:S(2)}) collective-permute-start(bf16[512,128]{1,0:T(8,128)(2,1)S(1)} %get-tuple-element.229), channel_id=1, source_target_pairs={{0,3},{1,0},{2,1},{3,2},{4,7},{5,4},{6,5},{7,6},{8,11},{9,8},{10,9... | collective-permute-start | bytes 393224 | tf_op jit(solution)/shard_map/ppermute | solution.py:697
  21.3 1.0 %collective-permute-start.10 = (bf16[512,128]{1,0:T(8,128)(2,1)S(1)}, bf16[512,128]{1,0:T(8,128)(2,1)S(1)}, u32[]{:S(2)}, u32[]{:S(2)}) collective-permute-start(bf16[512,128]{1,0:T(8,128)(2,1)S(1)} %get-tuple-element.231), channel_id=1, source_target_pairs={{0,1},{1,2},{2,3},{3,0},{4,5},{5,6},{6,7},{7,4},{8,9},{9,10},{10,1... | collective-permute-start | bytes 393224 | tf_op jit(solution)/shard_map/ppermute | solution.py:697
  22.3 4.2 %contract_hyper.1 = (bf16[512,128]{1,0:T(8,128)(2,1)S(1)}, bf16[144,128]{1,0:T(8,128)(2,1)S(1)}) custom-call(s32[1]{0:T(128)} %bitcast.61.place, f32[17]{0:T(128)S(1)} %select_reduce_fusion.taps, f32[512,128]{1,0:T(8,128)S(1)} %get-tuple-element.97.columns, bf16[128,16]{1,0:T(8,128)(2,1)S(1)} %collective-permute-done.13.before, ...), custom_call_target="tpu_custom_call" | custom-call | flops 1610612736 | bytes 16777216 | tf_op jit(solution)/shard_map/contract_hyper/pallas_call | solution.py:190
  26.6 2.9 %collective-permute-start.17 = (bf16[272,128]{1,0:T(8,128)(2,1)S(1)}, bf16[272,128]{1,0:T(8,128)(2,1)S(1)}, u32[]{:S(2)}, u32[]{:S(2)}) collective-permute-start(bf16[272,128]{1,0:T(8,128)(2,1)S(1)} %get-tuple-element.235), channel_id=1, source_target_pairs={{0,3},{1,0},{2,1},{3,2},{4,7},{5,4},{6,5},{7,6},{8,11},{9,8},{10,9... | collective-permute-start | bytes 208904 | tf_op jit(solution)/shard_map/ppermute | solution.py:697
  29.4 1.1 %collective-permute-start.16 = (bf16[272,128]{1,0:T(8,128)(2,1)S(1)}, bf16[272,128]{1,0:T(8,128)(2,1)S(1)}, u32[]{:S(2)}, u32[]{:S(2)}) collective-permute-start(bf16[272,128]{1,0:T(8,128)(2,1)S(1)} %get-tuple-element.236), channel_id=1, source_target_pairs={{0,2},{1,3},{2,0},{3,1},{4,6},{5,7},{6,4},{7,5},{8,10},{9,11},{10,... | collective-permute-start | bytes 208904 | tf_op jit(solution)/shard_map/ppermute | solution.py:697
  30.6 4.7 %collective-permute-done.11.refs_1_ = bf16[512,128]{1,0:T(8,128)(2,1)S(1)} collective-permute-done((bf16[512,128]{1,0:T(8,128)(2,1)S(1)}, bf16[512,128]{1,0:T(8,128)(2,1)S(1)}, u32[]{:S(2)}, u32[]{:S(2)}) %collective-permute-start.11) | collective-permute-done | bytes 131104 | tf_op jit(solution)/shard_map/ppermute | solution.py:697
  35.3 0.1 sum_arrived.1.refs_2_.multi
  35.4 2.7 %collective-permute-done.16.refs_5_ = bf16[272,128]{1,0:T(8,128)(2,1)S(1)} collective-permute-done((bf16[272,128]{1,0:T(8,128)(2,1)S(1)}, bf16[272,128]{1,0:T(8,128)(2,1)S(1)}, u32[]{:S(2)}, u32[]{:S(2)}) %collective-permute-start.16) | collective-permute-done | bytes 69664 | tf_op jit(solution)/shard_map/ppermute | solution.py:697
  38.2 0.4 collective-permute-start.18
  38.6 5.0 %collective-permute-start.19 = (f32[184,128]{1,0:T(8,128)S(1)}, f32[184,128]{1,0:T(8,128)S(1)}, u32[]{:S(2)}, u32[]{:S(2)}) collective-permute-start(f32[184,128]{1,0:T(8,128)S(1)} %get-tuple-element.104), channel_id=1, source_target_pairs={{1,0},{2,1},{3,2},{4,3},{5,4},{6,5},{7,6},{8,7},{9,8},{10,9},{11,1... | collective-permute-start | bytes 282632 | tf_op jit(solution)/shard_map/ppermute | solution.py:595
  43.6 1.2 %collective-permute-done.20.other = f32[72,128]{1,0:T(8,128)S(1)} collective-permute-done((f32[72,128]{1,0:T(8,128)S(1)}, f32[72,128]{1,0:T(8,128)S(1)}, u32[]{:S(2)}, u32[]{:S(2)}) %collective-permute-start.20) | collective-permute-done | bytes 36896 | tf_op jit(solution)/shard_map/ppermute | solution.py:672
  44.8 2.2 %make_operator.1 = (f32[128,128]{1,0:T(8,128)S(1)}, f32[128,128]{1,0:T(8,128)S(1)}, bf16[256,256]{1,0:T(8,128)(2,1)S(1)}, bf16[256,256]{1,0:T(8,128)(2,1)S(1)}, f32[8,128]{1,0:T(8,128)S(1)}) custom-call(s32[1]{0:T(128)} %bitcast.61.place, f32[17]{0:T(128)S(1)} %select_reduce_fusion.taps, f32[96,128]{1,0:T(8,128)S(1)} %get-tuple-element.92.band, ...), custom_call_target="tpu_custom_call" | custom-call | tf_op jit(solution)/shard_map/make_operator/pallas_call | solution.py:265
  47.0 3.8 %make_basis.1 = (f32[6,4,128,128]{3,2,1,0:T(8,128)S(1)}, f32[32,8,128]{2,1,0:T(8,128)}) custom-call(f32[17]{0:T(128)S(1)} %select_reduce_fusion.taps, f32[512,128]{1,0:T(8,128)S(1)} %sum_arrived.1.refs_2_.multi, f32[128,128]{1,0:T(8,128)S(1)} %get-tuple-element.102.hyper, f32[512,128]{1,0:T(8,128)S(1)} %get-tuple-element.101.refs_3_.start, ...), custom_call_target="tpu_custom_call" | custom-call | tf_op jit(solution)/shard_map/make_basis/pallas_call | solution.py:466
  50.8 4.5 %all-to-all-start = ((f32[32,8,128]{2,1,0:T(8,128)}), f32[32,8,128]{2,1,0:T(8,128)S(1)}, u32[]{:S(2)}, u32[]{:S(2)}) async-start(f32[32,8,128]{2,1,0:T(8,128)} %get-tuple-element.109), calls=%async_computation | async-start | bytes 262144 | tf_op jit(solution)/shard_map/all_to_all | solution.py:718
  55.4 8.4 %all-to-all-done.products = f32[32,8,128]{2,1,0:T(8,128)S(1)} async-done(((f32[32,8,128]{2,1,0:T(8,128)}), f32[32,8,128]{2,1,0:T(8,128)S(1)}, u32[]{:S(2)}, u32[]{:S(2)}) %all-to-all-start) | async-done | bytes 131104 | tf_op jit(solution)/shard_map/all_to_all | solution.py:718
  63.8 0.8 %make_coefficients.1 = (f32[16,128]{1,0:T(8,128)S(1)}, s32[1]{0:T(128)}) custom-call(f32[32,8,128]{2,1,0:T(8,128)S(1)} %all-to-all-done.products, f32[8,128]{1,0:T(8,128)S(1)} %get-tuple-element.108.bound), custom_call_target="tpu_custom_call" | custom-call | tf_op jit(solution)/shard_map/make_coefficients/pallas_call | solution.py:550
  65.2 1.2 %conditional.1 = ((f32[512,128]{1,0:T(8,128)}, f32[512,128]{1,0:T(8,128)})) conditional(s32[]{:T(128)} %bitcast.63, (f32[6,4,128,128]{3,2,1,0:T(8,128)S(1)}, f32[17]{0:T(128)S(1)}, f32[128,128]{1,0:T(8,128)S(1)}, f32[512,128]{1,0:T(8,128)S(1)}, f32[128,128]{1,0:T(8,128)S(1)}, /*index=5*/f32[128,128]{1,0:T(8,128)S(1)}) %tuple.20, ...), branch_computations={%region_1.10_spmd, %region_10.11_spmd} | conditional | flops 257967104 | bytes 23068832 | solution.py:725
  65.5 0.9 %combine.1 = (f32[512,128]{1,0:T(8,128)}, f32[512,128]{1,0:T(8,128)}) custom-call(f32[16,128]{1,0:T(8,128)S(1)} %get-tuple-element.65.coefficients, f32[6,4,128,128]{3,2,1,0:T(8,128)S(1)} %get-tuple-element.66.basis), custom_call_target="tpu_custom_call" | custom-call | tf_op jit(solution)/shard_map/cond/branch_1_fun/combine/pallas_call | solution.py:580
  (25 shorter events, 0.2 us)
Async XLA Ops:
  0.6 3.7 %copy-start.2 = (bf16[512,16]{0,1:T(8,128)(2,1)S(1)}, bf16[512,16]{0,1:T(8,128)(2,1)}, u32[]{:S(2)}) copy-start(bf16[512,16]{0,1:T(8,128)(2,1)} %param.15) | copy-start | bytes 49156
  0.6 3.6 %collective-permute-start.6 = (bf16[16,512]{1,0:T(8,128)(2,1)}, bf16[16,512]{1,0:T(8,128)(2,1)S(1)}, u32[]{:S(2)}, u32[]{:S(2)}) collective-permute-start(bf16[16,512]{1,0:T(8,128)(2,1)} %bitcast.164), channel_id=1, source_target_pairs={{0,4},{4,0},{8,12},{12,8},{16,20},{20,16},{24,28},{28,24},{1,5},{5... | collective-permute-start | bytes 49160 | tf_op jit(solution)/shard_map/ppermute | solution.py:672
  4.3 8.9 %collective-permute-start.9 = (bf16[32,512]{1,0:T(8,128)(2,1)S(1)}, bf16[32,512]{1,0:T(8,128)(2,1)S(1)}, u32[]{:S(2)}, u32[]{:S(2)}) collective-permute-start(bf16[32,512]{1,0:T(8,128)(2,1)S(1)} %pad_maximum_fusion.10.refs_0_), channel_id=1, source_target_pairs={{0,24},{4,28},{8,16},{12,20},{16,8},{20,12},{24,0},{28,4},{1,25},{... | collective-permute-start | bytes 98312 | tf_op jit(solution)/shard_map/ppermute | solution.py:672
  7.9 5.4 %collective-permute-start.8 = (bf16[32,512]{1,0:T(8,128)(2,1)S(1)}, bf16[32,512]{1,0:T(8,128)(2,1)S(1)}, u32[]{:S(2)}, u32[]{:S(2)}) collective-permute-start(bf16[32,512]{1,0:T(8,128)(2,1)S(1)} %pad_maximum_fusion.10.refs_0_), channel_id=1, source_target_pairs={{0,16},{4,20},{8,24},{12,28},{16,0},{20,4},{24,8},{28,12},{1,17},{... | collective-permute-start | bytes 98312 | tf_op jit(solution)/shard_map/ppermute | solution.py:672
  8.4 5.0 %collective-permute-start.7 = (bf16[32,512]{1,0:T(8,128)(2,1)S(1)}, bf16[32,512]{1,0:T(8,128)(2,1)S(1)}, u32[]{:S(2)}, u32[]{:S(2)}) collective-permute-start(bf16[32,512]{1,0:T(8,128)(2,1)S(1)} %pad_maximum_fusion.10.refs_0_), channel_id=1, source_target_pairs={{0,8},{4,12},{8,0},{12,4},{16,24},{20,28},{24,16},{28,20},{1,9},{5... | collective-permute-start | bytes 98312 | tf_op jit(solution)/shard_map/ppermute | solution.py:672
  13.5 8.8 %collective-permute-start.13 = (bf16[128,16]{1,0:T(8,128)(2,1)S(1)}, bf16[128,16]{1,0:T(8,128)(2,1)S(1)}, u32[]{:S(2)}, u32[]{:S(2)}) collective-permute-start(bf16[128,16]{1,0:T(8,128)(2,1)S(1)} %pad_maximum_fusion.11), channel_id=1, source_target_pairs={{0,1},{1,2},{2,3},{3,0},{4,5},{5,6},{6,7},{7,4},{8,9},{9,10},{10,1... | collective-permute-start | bytes 12296 | tf_op jit(solution)/shard_map/ppermute | solution.py:591
  15.6 6.8 %collective-permute-start.14 = (bf16[128,16]{1,0:T(8,128)(2,1)S(1)}, bf16[128,16]{1,0:T(8,128)(2,1)S(1)}, u32[]{:S(2)}, u32[]{:S(2)}) collective-permute-start(bf16[128,16]{1,0:T(8,128)(2,1)S(1)} %pad_maximum_fusion.12), channel_id=1, source_target_pairs={{1,0},{2,1},{3,2},{0,3},{5,4},{6,5},{7,6},{4,7},{9,8},{10,9},{11,1... | collective-permute-start | bytes 12296 | tf_op jit(solution)/shard_map/ppermute | solution.py:595
  19.3 11.3 %collective-permute-start.12 = (bf16[512,128]{1,0:T(8,128)(2,1)S(1)}, bf16[512,128]{1,0:T(8,128)(2,1)S(1)}, u32[]{:S(2)}, u32[]{:S(2)}) collective-permute-start(bf16[512,128]{1,0:T(8,128)(2,1)S(1)} %get-tuple-element.229), channel_id=1, source_target_pairs={{0,3},{1,0},{2,1},{3,2},{4,7},{5,4},{6,5},{7,6},{8,11},{9,8},{10,9... | collective-permute-start | bytes 393224 | tf_op jit(solution)/shard_map/ppermute | solution.py:697
  21.3 14.0 %collective-permute-start.11 = (bf16[512,128]{1,0:T(8,128)(2,1)S(1)}, bf16[512,128]{1,0:T(8,128)(2,1)S(1)}, u32[]{:S(2)}, u32[]{:S(2)}) collective-permute-start(bf16[512,128]{1,0:T(8,128)(2,1)S(1)} %get-tuple-element.230), channel_id=1, source_target_pairs={{0,2},{1,3},{2,0},{3,1},{4,6},{5,7},{6,4},{7,5},{8,10},{9,11},{10,... | collective-permute-start | bytes 393224 | tf_op jit(solution)/shard_map/ppermute | solution.py:697
  21.3 14.0 %collective-permute-start.10 = (bf16[512,128]{1,0:T(8,128)(2,1)S(1)}, bf16[512,128]{1,0:T(8,128)(2,1)S(1)}, u32[]{:S(2)}, u32[]{:S(2)}) collective-permute-start(bf16[512,128]{1,0:T(8,128)(2,1)S(1)} %get-tuple-element.231), channel_id=1, source_target_pairs={{0,1},{1,2},{2,3},{3,0},{4,5},{5,6},{6,7},{7,4},{8,9},{9,10},{10,1... | collective-permute-start | bytes 393224 | tf_op jit(solution)/shard_map/ppermute | solution.py:697
  26.6 8.8 %collective-permute-start.17 = (bf16[272,128]{1,0:T(8,128)(2,1)S(1)}, bf16[272,128]{1,0:T(8,128)(2,1)S(1)}, u32[]{:S(2)}, u32[]{:S(2)}) collective-permute-start(bf16[272,128]{1,0:T(8,128)(2,1)S(1)} %get-tuple-element.235), channel_id=1, source_target_pairs={{0,3},{1,0},{2,1},{3,2},{4,7},{5,4},{6,5},{7,6},{8,11},{9,8},{10,9... | collective-permute-start | bytes 208904 | tf_op jit(solution)/shard_map/ppermute | solution.py:697
  29.4 8.7 %collective-permute-start.16 = (bf16[272,128]{1,0:T(8,128)(2,1)S(1)}, bf16[272,128]{1,0:T(8,128)(2,1)S(1)}, u32[]{:S(2)}, u32[]{:S(2)}) collective-permute-start(bf16[272,128]{1,0:T(8,128)(2,1)S(1)} %get-tuple-element.236), channel_id=1, source_target_pairs={{0,2},{1,3},{2,0},{3,1},{4,6},{5,7},{6,4},{7,5},{8,10},{9,11},{10,... | collective-permute-start | bytes 208904 | tf_op jit(solution)/shard_map/ppermute | solution.py:697
  30.6 7.6 %collective-permute-start.15 = (bf16[272,128]{1,0:T(8,128)(2,1)S(1)}, bf16[272,128]{1,0:T(8,128)(2,1)S(1)}, u32[]{:S(2)}, u32[]{:S(2)}) collective-permute-start(bf16[272,128]{1,0:T(8,128)(2,1)S(1)} %get-tuple-element.237), channel_id=1, source_target_pairs={{0,1},{1,2},{2,3},{3,0},{4,5},{5,6},{6,7},{7,4},{8,9},{9,10},{10,1... | collective-permute-start | bytes 208904 | tf_op jit(solution)/shard_map/ppermute | solution.py:697
  38.2 8.8 %collective-permute-start.18 = (f32[184,128]{1,0:T(8,128)S(1)}, f32[184,128]{1,0:T(8,128)S(1)}, u32[]{:S(2)}, u32[]{:S(2)}) collective-permute-start(f32[184,128]{1,0:T(8,128)S(1)} %get-tuple-element.103), channel_id=1, source_target_pairs={{0,1},{1,2},{2,3},{3,4},{4,5},{5,6},{6,7},{7,8},{8,9},{9,10},{10,1... | collective-permute-start | bytes 282632 | tf_op jit(solution)/shard_map/ppermute | solution.py:591
  38.6 8.5 %collective-permute-start.19 = (f32[184,128]{1,0:T(8,128)S(1)}, f32[184,128]{1,0:T(8,128)S(1)}, u32[]{:S(2)}, u32[]{:S(2)}) collective-permute-start(f32[184,128]{1,0:T(8,128)S(1)} %get-tuple-element.104), channel_id=1, source_target_pairs={{1,0},{2,1},{3,2},{4,3},{5,4},{6,5},{7,6},{8,7},{9,8},{10,9},{11,1... | collective-permute-start | bytes 282632 | tf_op jit(solution)/shard_map/ppermute | solution.py:595
  43.6 1.2 %collective-permute-start.20 = (f32[72,128]{1,0:T(8,128)S(1)}, f32[72,128]{1,0:T(8,128)S(1)}, u32[]{:S(2)}, u32[]{:S(2)}) collective-permute-start(f32[72,128]{1,0:T(8,128)S(1)} %get-tuple-element.105.own), channel_id=1, source_target_pairs={{0,4},{4,0},{8,12},{12,8},{16,20},{20,16},{24,28},{28,24},{1,5},{5... | collective-permute-start | bytes 110600 | tf_op jit(solution)/shard_map/ppermute | solution.py:672
  50.8 13.0 %all-to-all-start = ((f32[32,8,128]{2,1,0:T(8,128)}), f32[32,8,128]{2,1,0:T(8,128)S(1)}, u32[]{:S(2)}, u32[]{:S(2)}) async-start(f32[32,8,128]{2,1,0:T(8,128)} %get-tuple-element.109), calls=%async_computation | async-start | bytes 262144 | tf_op jit(solution)/shard_map/all_to_all | solution.py:718

commit v4 on v3

--- a/solution.py
+++ b/solution.py
@@ -1,4 +1,5 @@
 import functools
+import math
 
 import jax
 import jax.numpy as jnp
@@ -17,10 +18,13 @@
 ROWS_A = 512
 RIM = 24
 RIM_MULTI = 16
+RIM_START = 20
 PAIRS = [(i, j) for i in range(ITERS + 1) for j in range(i, ITERS + 1)]
 TRUST = 2.0e4
 EDGE = 16
-VMEM_LIMIT = 32 * 1024 * 1024
+EARLY = 36
+LATER = 20
+VMEM_LIMIT = 20 * 1024 * 1024
 
 
 def params():
@@ -52,16 +56,16 @@
     )
 
 
-def load_kernel(parts, *refs):
-    count = len(parts)
+def load_kernel(ranges, *refs):
+    count = len(ranges)
     copies = []
-    for source, target, number in zip(refs[:count], refs[count : 2 * count], parts):
-        size = source.shape[0] // number
-        for part in range(number):
-            rows = pl.ds(part * size, size)
+    for source, target, (rows, parts, _) in zip(refs[:count], refs[count : 2 * count], ranges):
+        size = rows // parts
+        for part in range(parts):
+            piece = pl.ds(part * size, size)
             copies.append(
                 pltpu.make_async_copy(
-                    source.at[rows], target.at[rows], refs[2 * count].at[len(copies)]
+                    source.at[piece], target.at[piece], refs[2 * count].at[len(copies)]
                 )
             )
     for copy in copies:
@@ -70,17 +74,18 @@
         copy.wait()
 
 
-def load(arrays, parts, name):
-    size = sum(a.size * a.dtype.itemsize for a in arrays)
+def load(arrays, ranges):
+    shapes = [(room, *a.shape[1:]) for a, (_, _, room) in zip(arrays, ranges)]
+    size = sum(a.dtype.itemsize * math.prod(shape) for a, shape in zip(arrays, shapes))
     return pl.pallas_call(
-        functools.partial(load_kernel, parts),
+        functools.partial(load_kernel, ranges),
         in_specs=[pl.BlockSpec(memory_space=pl.ANY)] * len(arrays),
         out_specs=[VMEM] * len(arrays),
-        out_shape=[pltpu.VMEM(a.shape, a.dtype) for a in arrays],
-        scratch_shapes=[pltpu.SemaphoreType.DMA((sum(parts),))],
+        out_shape=[pltpu.VMEM(shape, a.dtype) for a, shape in zip(arrays, shapes)],
+        scratch_shapes=[pltpu.SemaphoreType.DMA((sum(parts for _, parts, _ in ranges),))],
         compiler_params=params(),
         cost_estimate=pl.CostEstimate(flops=0, bytes_accessed=2 * size, transcendentals=0),
-        name=name,
+        name="load",
     )(*[in_space(a, pltpu.HBM) for a in arrays])
 
 
@@ -96,12 +101,16 @@
         target[pl.ds(second, share), : values.shape[1]] = values[share:, :]
 
 
-def multi_kernel(count, place, band, response, image, *refs):
+def multi_kernel(count, first, place, band, response, image, other, held, *refs):
+    del held
     pieces = refs[:count]
-    out, columns, pairs, ranks = refs[count:]
+    out, columns, bands, pairs, ranks, semaphore = refs[count:]
+    rows = pl.ds(first, bands.shape[0] - first)
+    copy = pltpu.make_async_copy(other.at[rows], bands.at[rows], semaphore)
+    copy.start()
     depth = image.shape[2]
     rank = out.shape[1]
-    in_rank_order(place, pieces[0].shape[0] // 2, [p[...] for p in pieces], ranks)
+    in_rank_order(place, pieces[0].shape[0] // 2, [p[:, :depth] for p in pieces], ranks)
     for start in range(0, depth, rank):
         columns[start : start + rank, :] = ranks[:, start : start + rank].T
     merged = jnp.dot(
@@ -110,47 +119,63 @@
     field = columns[...]
     for k in range(2):
         pairs[k * depth : (k + 1) * depth, :] = (merged[k : k + 1, :] * field).astype(jnp.bfloat16)
-    for start in range(0, out.shape[0], ROWS_A):
-        rows = slice(start, start + ROWS_A)
-        pixels = jnp.concatenate([image[0, rows, :], image[1, rows, :]], axis=1)
-        total = jnp.dot(pixels, pairs[...], preferred_element_type=jnp.float32)
-        out[rows, :] = total.astype(jnp.bfloat16)
-
-
-def contract_multi(place, band, response, image, pieces):
+
+    @pl.when(place[0] >= 0)
+    def _():
+        for start in range(0, out.shape[0], ROWS_A):
+            rows = slice(start, start + ROWS_A)
+            pixels = jnp.concatenate([image[0, rows, :], image[1, rows, :]], axis=1)
+            total = jnp.dot(pixels, pairs[...], preferred_element_type=jnp.float32)
+            out[rows, :] = total.astype(jnp.bfloat16)
+
+    copy.wait()
+
+
+def contract_multi(place, band, response, image, pieces, other, held, first):
     bands, rows, depth = image.shape
     rank = band.shape[1]
     outs = [
         jax.ShapeDtypeStruct((rows, rank), jnp.bfloat16),
         jax.ShapeDtypeStruct((depth, rank), jnp.float32),
+        pltpu.VMEM(held.shape, held.dtype),
     ]
     return pl.pallas_call(
-        functools.partial(multi_kernel, len(pieces)),
+        functools.partial(multi_kernel, len(pieces), first),
         in_specs=[SMEM, whole(band.shape), whole(response.shape), VMEM]
+        + [pl.BlockSpec(memory_space=pl.ANY), VMEM]
         + [whole(p.shape) for p in pieces],
-        out_specs=[whole(o.shape) for o in outs],
+        out_specs=[whole(o.shape) for o in outs[:2]] + [VMEM],
+        input_output_aliases={5: 2},
         out_shape=outs,
         scratch_shapes=[
             pltpu.VMEM((bands * depth, rank), jnp.bfloat16),
             pltpu.VMEM((rank, depth), jnp.float32),
+            pltpu.SemaphoreType.DMA,
         ],
         compiler_params=params(),
         cost_estimate=pl.CostEstimate(
             flops=2 * bands * rows * depth * rank, bytes_accessed=1 << 23, transcendentals=0
         ),
         name="contract_multi",
-    )(place, band, response, in_space(image, pltpu.VMEM), *pieces)
-
-
-def hyper_kernel(share, place, taps, columns, before, after, band, image, out, gram, wide, ranks, packed):
+    )(
+        place, band, response, in_space(image, pltpu.VMEM), in_space(other, pltpu.HBM),
+        in_space(held, pltpu.VMEM), *pieces,
+    )
+
+
+def hyper_kernel(
+    share, place, taps, columns, before, after, band, held, image, out, gram, wide, ranks, packed,
+    rest, total, semaphore,
+):
     depth, rank = columns.shape
+    ready = held.shape[0]
+    copy = pltpu.make_async_copy(image.at[pl.ds(ready, rest.shape[0])], rest, semaphore)
+    copy.start()
     wide[EDGE : EDGE + depth, :] = columns[...]
     for edge, first in ((before, 0), (after, EDGE + depth)):
         values = edge[...].astype(jnp.float32)
         size = 2 * share
-        in_rank_order(
-            place, share, [values[i : i + size, :] for i in range(0, rank, size)], ranks
-        )
+        in_rank_order(place, share, [values[i : i + size, :] for i in range(0, rank, size)], ranks)
         wide[first : first + EDGE, :] = ranks[...].T[:EDGE, :]
     coarse = jnp.zeros((depth // DEC, rank), jnp.float32)
     for offset in range(-W, W + 1):
@@ -171,44 +196,61 @@
     high = part.astype(jnp.bfloat16).astype(jnp.float32)
     gram[...] = jnp.concatenate([high, part - high], axis=0).astype(jnp.bfloat16)
 
-    bands = image.shape[0]
-    pairs = jnp.concatenate(
-        [(band[k : k + 1, :] * coarse).astype(jnp.bfloat16) for k in range(bands)], axis=0
-    )
-    pixels = jnp.concatenate([image[k] for k in range(bands)], axis=1)
-    total = jnp.dot(pixels, pairs, preferred_element_type=jnp.float32)
-    out[...] = total.astype(jnp.bfloat16)
-
-
-def contract_hyper(share, place, taps, columns, before, after, band, image):
+    def product(source, offset):
+        pixels = [source[k] for k in range(source.shape[0])]
+        pairs = [
+            (band[offset + k : offset + k + 1, :] * coarse).astype(jnp.bfloat16)
+            for k in range(len(pixels))
+        ]
+        return jnp.dot(
+            jnp.concatenate(pixels, axis=1),
+            jnp.concatenate(pairs, axis=0),
+            preferred_element_type=jnp.float32,
+        )
+
+    @pl.when(place[0] >= 0)
+    def _():
+        total[...] = product(held, 0)
+
+    copy.wait()
+    out[...] = (total[...] + product(rest, ready)).astype(jnp.bfloat16)
+
+
+def contract_hyper(share, place, taps, columns, before, after, band, held, image):
     bands, rows, depth = image.shape
     fine, rank = columns.shape
+    rest = bands - held.shape[0]
     outs = [
         jax.ShapeDtypeStruct((rows, rank), jnp.bfloat16),
         jax.ShapeDtypeStruct((rank + 16, rank), jnp.bfloat16),
     ]
     return pl.pallas_call(
         functools.partial(hyper_kernel, share),
-        in_specs=[SMEM, SMEM] + [whole(a.shape) for a in (columns, before, after, band)] + [VMEM],
+        in_specs=[SMEM, SMEM]
+        + [whole(a.shape) for a in (columns, before, after, band)]
+        + [VMEM, pl.BlockSpec(memory_space=pl.ANY)],
         out_specs=[whole(o.shape) for o in outs],
         out_shape=outs,
         scratch_shapes=[
             pltpu.VMEM((fine + 2 * EDGE, rank), jnp.float32),
             pltpu.VMEM((rank, rank), jnp.float32),
             pltpu.VMEM((rank + 16, rank), jnp.float32),
+            pltpu.VMEM((rest, rows, depth), image.dtype),
+            pltpu.VMEM((rows, rank), jnp.float32),
+            pltpu.SemaphoreType.DMA,
         ],
         compiler_params=params(),
-        cost_estimate=pl.CostEstimate(
-            flops=2 * bands * rows * depth * rank, bytes_accessed=1 << 24, transcendentals=0
-        ),
         name="contract_hyper",
-    )(place, taps, columns, before, after, band, in_space(image, pltpu.VMEM))
+    )(
+        place, taps, columns, before, after, band, in_space(held, pltpu.VMEM),
+        in_space(image, pltpu.HBM),
+    )
 
 
 def operator_kernel(
-    place, taps, band, response, own, other, hyper_out, multi_out, hyper_w, multi_w, bound
+    place, taps, band_gram, merged_gram, own, other, hyper_out, multi_out, hyper_w, multi_w, bound
 ):
-    rank = band.shape[1]
+    rank = band_gram.shape[1]
     even = place[0] % 2 == 0
     lower = jnp.where(even, own[...], other[...])
     upper = jnp.where(even, other[...], own[...])
@@ -220,13 +262,8 @@
     along = lax.broadcasted_iota(jnp.int32, (rank, rank), 1)
     column_gram = jnp.where(along >= down, packed, turned)
     coarse_gram = jnp.where(along < down, packed, jnp.where(along == down, diagonal, turned))
-    merged = jnp.dot(
-        response[...], band[...], precision=FULL_PRECISION, preferred_element_type=jnp.float32
-    )
-    hyper = coarse_gram * gram_of(band[...])
-    multi = column_gram * gram_of(merged)
-    eye = (along == down).astype(jnp.float32)
-    multi = multi + RIDGE_TERM * eye
+    hyper = coarse_gram * band_gram[...]
+    multi = column_gram * merged_gram[...] + jnp.where(along == down, RIDGE_TERM, 0.0)
     hyper_out[...] = hyper
     multi_out[...] = multi
     squared = jnp.float32(0.0)
@@ -238,15 +275,16 @@
         squared = squared + in_phase * in_phase
     largest = squared * hyper + multi
 
+    def total_of(values):
+        return jnp.sum(jnp.sum(values, axis=1, keepdims=True), axis=0, keepdims=True)
+
     def trace(values):
-        return jnp.sum(jnp.sum(values * eye, axis=1, keepdims=True), axis=0, keepdims=True)
+        return total_of(jnp.where(along == down, values, 0.0))
 
     power = largest / trace(largest)
     for _ in range(4):
         power = jnp.dot(power, power, preferred_element_type=jnp.float32)
-        power = power / trace(power)
-    value = jnp.sum(jnp.sum(power * largest, axis=1, keepdims=True), axis=0, keepdims=True)
-    top = 1.1 * value
+    top = 1.1 * total_of(power * largest) / trace(power)
     bound[...] = jnp.broadcast_to(top, bound.shape)
     for matrix, weights in ((hyper, hyper_w), (multi, multi_w)):
         high, low = two_halves(matrix * (4.0 / top))
@@ -256,20 +294,22 @@
         weights[rank:, rank:] = jnp.zeros_like(high)
 
 
-def make_operator(place, taps, band, response, own, other):
-    rank = band.shape[1]
+def make_operator(place, taps, band_gram, merged_gram, own, other):
+    rank = band_gram.shape[1]
     square = jax.ShapeDtypeStruct((rank, rank), jnp.float32)
     weights = jax.ShapeDtypeStruct((2 * rank, 2 * rank), jnp.bfloat16)
     bound = jax.ShapeDtypeStruct((8, rank), jnp.float32)
     outs = [square, square, weights, weights, bound]
+    arrays = (band_gram, merged_gram, own, other)
     return pl.pallas_call(
         operator_kernel,
-        in_specs=[SMEM, SMEM] + [whole(a.shape) for a in (band, response, own, other)],
+        in_specs=[SMEM, SMEM] + [whole(a.shape) for a in arrays],
         out_specs=[whole(o.shape) for o in outs],
         out_shape=outs,
         compiler_params=params(),
+        cost_estimate=pl.CostEstimate(flops=0, bytes_accessed=1 << 26, transcendentals=0),
         name="make_operator",
-    )(place, taps, band, response, own, other)
+    )(place, taps, *arrays)
 
 
 def times(values, weights):
@@ -309,30 +349,39 @@
     return total
 
 
-def sum_kernel(place, own, *refs):
+def sum_kernel(place, band, response, own, *refs):
     del place
+    out, band_gram, merged_gram = refs[-3:]
     total = own[...].astype(jnp.float32)
-    for values in refs[:-1]:
+    for values in refs[:-3]:
         total += values[...].astype(jnp.float32)
-    refs[-1][...] = total
-
-
-def sum_arrived(place, own, arrived):
+    out[...] = total
+    merged = jnp.dot(
+        response[...], band[...], precision=FULL_PRECISION, preferred_element_type=jnp.float32
+    )
+    band_gram[...] = gram_of(band[...])
+    merged_gram[...] = gram_of(merged)
+
+
+def sum_arrived(place, band, response, own, arrived):
     shape = arrived[0].shape
+    rank = band.shape[1]
+    square = jax.ShapeDtypeStruct((rank, rank), jnp.float32)
+    outs = [jax.ShapeDtypeStruct(shape, jnp.float32), square, square]
     return pl.pallas_call(
         sum_kernel,
         grid_spec=pltpu.PrefetchScalarGridSpec(
             num_scalar_prefetch=1,
             grid=(1,),
-            in_specs=[pl.BlockSpec(shape, lambda i, place: (place[0], 0))]
+            in_specs=[whole(band.shape), whole(response.shape)]
+            + [pl.BlockSpec(shape, lambda i, place: (place[0], 0))]
             + [whole(shape) for _ in arrived],
-            out_specs=whole(shape),
+            out_specs=[whole(o.shape) for o in outs],
         ),
-        out_shape=jax.ShapeDtypeStruct(shape, jnp.float32),
+        out_shape=outs,
         compiler_params=params(),
-        cost_estimate=pl.CostEstimate(flops=0, bytes_accessed=1 << 26, transcendentals=0),
         name="sum_arrived",
-    )(place, own, *arrived)
+    )(place, band, response, own, *arrived)
 
 
 def sums_kernel(count, place, *refs):
@@ -354,7 +403,7 @@
         for source, begin, size in (
             (multi, 0, first),
             (hyper, first, RIM),
-            (start, second, DEC * RIM),
+            (start, second, DEC * RIM_START),
         ):
             rows = source.shape[0]
             at = 0 if top else rows - size
@@ -364,7 +413,7 @@
 def add_sums(place, hyper_part, gram_part, multi, start, arrived):
     fine, rank = start.shape
     coarse = fine // DEC
-    pack = jax.ShapeDtypeStruct((DEC * RIM_MULTI + RIM + DEC * RIM, rank), jnp.float32)
+    pack = jax.ShapeDtypeStruct((DEC * (RIM_MULTI + RIM_START) + RIM, rank), jnp.float32)
     outs = [
         jax.ShapeDtypeStruct((coarse, rank), jnp.float32),
         jax.ShapeDtypeStruct((gram_part.shape[0] // 2, rank), jnp.float32),
@@ -386,6 +435,12 @@
     )(place, hyper_part, gram_part, multi, start, *arrived)
 
 
+def on_diagonal(rows, lanes):
+    down = lax.broadcasted_iota(jnp.int32, (rows, lanes), 0)
+    along = lax.broadcasted_iota(jnp.int32, (rows, lanes), 1)
+    return down == along
+
+
 def basis_kernel(
     devices, taps, multi, hyper, start, before, after, hyper_w, multi_w, bound, basis, products,
     natural, lifted, held,
@@ -400,9 +455,13 @@
         lowered = times(blur_down(taps, field), hyper_w[...])
         return [blur_up(taps, lowered, phase) + times(field(phase), multi_w[...]) for phase in range(DEC)]
 
-    natural[: DEC * RIM, :] = before[second:, :]
+    margin = DEC * (RIM - RIM_START)
+    none = jnp.zeros((margin, multi.shape[1]), jnp.float32)
+    natural[:margin, :] = none
+    natural[margin : DEC * RIM, :] = before[second:, :]
     natural[DEC * RIM : DEC * RIM + fine, :] = start[...]
-    natural[DEC * RIM + fine :, :] = after[second:, :]
+    natural[DEC * RIM + fine : 2 * DEC * RIM + fine - margin, :] = after[second:, :]
+    natural[2 * DEC * RIM + fine - margin :, :] = none
     for phase in range(DEC):
         held[1, phase] = natural[pl.ds(phase, wide, stride=DEC), :]
         basis[ITERS + 1, phase] = held[1, phase, own, :]
@@ -444,12 +503,9 @@
             total += basis[i, phase] * basis[j, phase]
         rows.append(jnp.sum(total, axis=0, keepdims=True))
     rows.append(jnp.zeros_like(rows[0]))
-    block = jnp.concatenate(rows, axis=0)
-    lanes = block.shape[1]
-    half = block.shape[0] // 2
-    block = block + pltpu.roll(block, lanes // 2, 1)
-    lane = lax.broadcasted_iota(jnp.int32, (half, lanes), 1)
-    block = jnp.where(lane < lanes // 2, block[:half, :], block[half:, :])
+    block = jnp.sum(jnp.concatenate(rows, axis=0), axis=1, keepdims=True)
+    block = jnp.where(on_diagonal(block.shape[0], multi.shape[1]), block, 0.0)
+    block = jnp.sum(block, axis=0, keepdims=True)
     for device in range(devices):
         products[device] = block
 
@@ -461,7 +517,7 @@
     arrays = (multi, hyper, start, before, after, hyper_w, multi_w, bound)
     outs = [
         jax.ShapeDtypeStruct((ITERS + 2, DEC, coarse, rank), jnp.float32),
-        jax.ShapeDtypeStruct((devices, (len(PAIRS) + 1) // 2, rank), jnp.float32),
+        jax.ShapeDtypeStruct((devices, 1, rank), jnp.float32),
     ]
     return pl.pallas_call(
         functools.partial(basis_kernel, devices),
@@ -480,12 +536,9 @@
 
 def coefficients_kernel(products, bound, out, trusted):
     count = ITERS + 1
-    folded = jnp.sum(products[...], axis=0)
-    lanes = folded.shape[1]
-    lane = lax.broadcasted_iota(jnp.int32, folded.shape, 1)
-    left = jnp.sum(jnp.where(lane < lanes // 2, folded, 0.0), axis=1, keepdims=True)
-    right = jnp.sum(jnp.where(lane < lanes // 2, 0.0, folded), axis=1, keepdims=True)
-    sums = jnp.concatenate([left, right], axis=0)
+    row = jnp.sum(products[...], axis=0)
+    sums = jnp.broadcast_to(row, (16, row.shape[1]))
+    sums = jnp.sum(jnp.where(on_diagonal(*sums.shape), sums, 0.0), axis=1, keepdims=True)
     inner = {}
     for number, (i, j) in enumerate(PAIRS):
         inner[i, j] = inner[j, i] = sums[number : number + 1, :]
@@ -672,20 +725,30 @@
         return lax.ppermute(values, "row", [(i, i ^ distance) for i in range(along)])
 
     own = col_factor.T
-    pair = jnp.concatenate([own, exchanged(own, 1)])
-    multispectral, band_factor, response, row_start = load(
-        (multispectral, band_factor, response, row_start), (2, 1, 1, 1), "load_multi"
-    )
-    pair, hyperspectral = lax.optimization_barrier((pair, hyperspectral))
+    partner = exchanged(own, 1)
+    half = lax.optimization_barrier(jnp.concatenate([own, jnp.zeros_like(own)]))
+    pair = jnp.concatenate([half[:share], partner])
+    pair, image = lax.optimization_barrier((pair, multispectral))
     pieces = [pair] + [exchanged(pair, distance) for distance in range(2, along, 2)]
-    (hyperspectral,) = load((hyperspectral,), (8,), "load_hyper")
+    image, band_factor, response, row_start, held = load(
+        (image, band_factor, response, row_start, hyperspectral),
+        (
+            (2, 2, 2),
+            (band_factor.shape[0], 1, band_factor.shape[0]),
+            (2, 1, 2),
+            (fine, 1, fine),
+            (EARLY, 4, EARLY + LATER),
+        ),
+    )
     before = to_next(jnp.concatenate([p[:, -EDGE:] for p in pieces]), "col", across)
     after = to_previous(jnp.concatenate([p[:, :EDGE] for p in pieces]), "col", across)
+    multi_part, columns, held = contract_multi(
+        row, band_factor, response, image, pieces, hyperspectral, held, EARLY
+    )
     spread = jnp.arange(-W, W + 1, dtype=jnp.int32)
     taps = jnp.sum(
         jnp.where(offsets[:, None] == spread[None, :], blur_taps[:, None], jnp.float32(0.0)), axis=0
     )
-    multi_part, columns = contract_multi(row, band_factor, response, multispectral, pieces)
 
     def exchange(values, size, more):
         arrived = []
@@ -700,18 +763,20 @@
 
     multi_arrived = exchange(multi_part, fine, [])
     hyper_part, gram_part = contract_hyper(
-        share, row, taps, columns, before, after, band_factor, hyperspectral
+        share, row, taps, columns, before, after, band_factor, held, hyperspectral
     )
     hyper_arrived = exchange(hyper_part, fine // DEC, [gram_part])
-    multi = sum_arrived(place[None], multi_part, multi_arrived)
+    multi, band_gram, merged_gram = sum_arrived(
+        place[None], band_factor, response, multi_part, multi_arrived
+    )
     hyper, gram, low, high = add_sums(
         place[None], hyper_part, gram_part, multi, row_start, hyper_arrived
     )
+    hyper_gram, multi_gram, hyper_w, multi_w, bound = make_operator(
+        row, taps, band_gram, merged_gram, gram, exchanged(gram, 1)
+    )
     before_rows = to_next(high, BOTH, devices)
     after_rows = to_previous(low, BOTH, devices)
-    hyper_gram, multi_gram, hyper_w, multi_w, bound = make_operator(
-        row, taps, band_factor, response, gram, exchanged(gram, 1)
-    )
     basis, products = make_basis(
         devices, taps, multi, hyper, row_start, before_rows, after_rows, hyper_w, multi_w, bound
     )

time: 66.6 us -> 63.5 us (0.953)
  waiting for transfers between devices: 17.1 us -> 14 us
  Pallas kernels: 20.5 us -> 17.6 us
  starting transfers between devices: 25.8 us -> 28 us
  local copies, waits for them, and re-layouts: 0.36 us -> 1.09 us
    pallas_call x3 -> x2, Pallas kernels: 8.52 us -> 5.51 us  [the longest x1 3.74 us: load(): pl.pallas_call(functools.partial(load_kernel, ranges), in_specs=[pl.Block...]
    ppermute x6, waiting for transfers between devices: 7.48 us -> 4.84 us  [exchange(): lax.ppermute(piece, 'col', [(i, (i + distance) % across) for i in range(a...]
    ppermute x6, starting transfers between devices: 7.08 us -> 8.87 us  [exchange(): lax.ppermute(piece, 'col', [(i, (i + distance) % across) for i in range(a...]
    all_to_all x1, waiting for transfers between devices: 8.4 us -> 7.1 us  [body(): products = lax.all_to_all(products, BOTH, 0, 0, tiled=True)]
    ppermute x5, waiting for transfers between devices: 1.22 us -> 2.02 us  [exchanged(): lax.ppermute(values, 'row', [(i, i ^ distance) for i in range(along)])]
    pallas_call x1, Pallas kernels: 2.22 us -> 1.43 us  [make_operator(): pl.pallas_call(operator_kernel, in_specs=[SMEM, SMEM] + [whole(a.shape) f...]
    ppermute x2, starting transfers between devices: 7.12 us -> 6.34 us  [to_previous(): lax.ppermute(values, axis, [((i + 1) % count, i) for i in range(count)])]
    concatenate x0 -> x1, local copies, waits for them, and re-layouts: none -> 0.72 us  [body(): half = lax.optimization_barrier(jnp.concatenate([own, jnp.zeros_like(own)]))]
  transfers between devices with their start and end apart: 16 -> 16, of which waited for: 4 -> 5; matrix products, arithmetic and copies ran while one was open for 2% -> 3% of each run, Pallas kernels for 23% -> 19%
where the time goes in v4:
time: 63.5 us; the launch traced here: 63.3 us
  starting transfers between devices  28 us (44%)
  Pallas kernels  17.6 us (28%)
  waiting for transfers between devices  14 us (22%)
  between operations  1.47 us (2%)
  local copies, waits for them, and re-layouts  1.09 us (2%)
  other arithmetic  0.8 us (1%)
    ppermute x6, starting transfers between devices, exchange(): lax.ppermute(piece, 'col', [(i, (i + distance) % across) for i in range(a...  8.87 us
    all_to_all x1, waiting for transfers between devices, body(): products = lax.all_to_all(products, BOTH, 0, 0, tiled=True)  7.1 us
    ppermute x2, starting transfers between devices, to_previous(): lax.ppermute(values, axis, [((i + 1) % count, i) for i in range(count)])  6.34 us
    all_to_all x1, starting transfers between devices, body(): products = lax.all_to_all(products, BOTH, 0, 0, tiled=True)  5.21 us
    ppermute x6, waiting for transfers between devices, exchange(): lax.ppermute(piece, 'col', [(i, (i + distance) % across) for i in range(a...  4.84 us
    ppermute x5, starting transfers between devices, exchanged(): lax.ppermute(values, 'row', [(i, i ^ distance) for i in range(along)])  4.64 us
    pallas_call x1, Pallas kernels, contract_hyper(): pl.pallas_call(functools.partial(hyper_kernel, share), in_specs=[SMEM, SM...  4.61 us
    pallas_call x1, Pallas kernels, make_basis(): pl.pallas_call(functools.partial(basis_kernel, devices), in_specs=[SMEM]...  3.79 us
  transfers between devices with their start and end apart: 16, of which 5 were waited for; matrix products, arithmetic and copies ran while one was open for 3% of the time, Pallas kernels for 19%

profile of v4, /device:TPU:0, one launch (start us, length us, event | category | flops | bytes accessed | tf_op | source)
XLA Modules:
  0.0 63.3 jit_solution(11566678594706817527)
XLA Ops:
  0.6 0.5 collective-permute-start.6
  1.2 0.8 %select_reduce_fusion.taps = f32[17]{0:T(128)S(1)} fusion(f32[9]{0:T(128)} %param.18, s32[17]{0:T(128)S(1)} %iota_add_fusion, s32[9]{0:T(128)} %param.19), kind=kLoop, calls=%fused_computation.155 | loop fusion | flops 442 | bytes 208 | tf_op jit(solution)/shard_map/reduce_sum | solution.py:749
  2.0 0.7 %concatenate.36 = bf16[32,512]{1,0:T(8,128)(2,1)S(1)} pad(bf16[16,512]{1,0:T(8,128)(2,1)} %bitcast.165, bf16[]{:T(256)} %constant.54.clone.1), padding=0_16x0_0 | pad | bytes 49154 | tf_op jit(solution)/shard_map/concatenate | solution.py:729
  2.7 2.6 %collective-permute-start.7 = (bf16[32,512]{1,0:T(8,128)(2,1)S(1)}, bf16[32,512]{1,0:T(8,128)(2,1)S(1)}, u32[]{:S(2)}, u32[]{:S(2)}) collective-permute-start(bf16[32,512]{1,0:T(8,128)(2,1)S(1)} %pad_maximum_fusion.10.refs_0_), channel_id=1, source_target_pairs={{0,8},{4,12},{8,0},{12,4},{16,24},{20,28},{24,16},{28,20},{1,9},{5... | collective-permute-start | bytes 98312 | tf_op jit(solution)/shard_map/ppermute | solution.py:725
  5.3 1.5 %collective-permute-start.8 = (bf16[32,512]{1,0:T(8,128)(2,1)S(1)}, bf16[32,512]{1,0:T(8,128)(2,1)S(1)}, u32[]{:S(2)}, u32[]{:S(2)}) collective-permute-start(bf16[32,512]{1,0:T(8,128)(2,1)S(1)} %pad_maximum_fusion.10.refs_0_), channel_id=1, source_target_pairs={{0,16},{4,20},{8,24},{12,28},{16,0},{20,4},{24,8},{28,12},{1,17},{... | collective-permute-start | bytes 98312 | tf_op jit(solution)/shard_map/ppermute | solution.py:725
  6.8 0.1 fusion.117
  6.9 3.7 %load.1 = (bf16[2,2048,512]{2,1,0:T(8,128)(2,1)S(1)}, f32[96,128]{1,0:T(8,128)S(1)}, f32[2,96]{1,0:T(2,128)S(1)}, f32[512,128]{1,0:T(8,128)S(1)}, bf16[56,512,128]{2,1,0:T(8,128)(2,1)S(1)}) custom-call(bf16[2,2048,512]{2,1,0:T(8,128)(2,1)} %refs_0_, f32[96,128]{1,0:T(8,128)} %refs_1_.1, f32[2,96]{1,0:T(2,128)} %refs_2_.1, f32[512,128]{1,0:T(8,128)} %refs_3_.1, ...), custom_call_target="tpu_custom_call" | custom-call | bytes 23692800 | tf_op jit(solution)/shard_map/load/pallas_call | solution.py:80
  10.6 0.1 fusion.118
  10.7 0.1 fusion.119
  10.8 0.8 %collective-permute-done.9.refs_3_ = bf16[32,512]{1,0:T(8,128)(2,1)S(1)} collective-permute-done((bf16[32,512]{1,0:T(8,128)(2,1)S(1)}, bf16[32,512]{1,0:T(8,128)(2,1)S(1)}, u32[]{:S(2)}, u32[]{:S(2)}) %collective-permute-start.9) | collective-permute-done | bytes 32800 | tf_op jit(solution)/shard_map/ppermute | solution.py:725
  11.7 1.6 %collective-permute-start.13 = (bf16[128,16]{1,0:T(8,128)(2,1)S(1)}, bf16[128,16]{1,0:T(8,128)(2,1)S(1)}, u32[]{:S(2)}, u32[]{:S(2)}) collective-permute-start(bf16[128,16]{1,0:T(8,128)(2,1)S(1)} %pad_maximum_fusion.11), channel_id=1, source_target_pairs={{0,1},{1,2},{2,3},{3,0},{4,5},{5,6},{6,7},{7,4},{8,9},{9,10},{10,1... | collective-permute-start | bytes 12296 | tf_op jit(solution)/shard_map/ppermute | solution.py:644
  13.3 2.3 %collective-permute-start.14 = (bf16[128,16]{1,0:T(8,128)(2,1)S(1)}, bf16[128,16]{1,0:T(8,128)(2,1)S(1)}, u32[]{:S(2)}, u32[]{:S(2)}) collective-permute-start(bf16[128,16]{1,0:T(8,128)(2,1)S(1)} %pad_maximum_fusion.12), channel_id=1, source_target_pairs={{1,0},{2,1},{3,2},{0,3},{5,4},{6,5},{7,6},{4,7},{9,8},{10,9},{11,1... | collective-permute-start | bytes 12296 | tf_op jit(solution)/shard_map/ppermute | solution.py:648
  15.6 1.8 %contract_multi.1 = (bf16[2048,128]{1,0:T(8,128)(2,1)S(1)}, f32[512,128]{1,0:T(8,128)S(1)}, bf16[56,512,128]{2,1,0:T(8,128)(2,1)S(1)}) custom-call(s32[1]{0:T(128)} %bitcast.62.place, f32[96,128]{1,0:T(8,128)S(1)} %get-tuple-element.98.band, f32[2,96]{1,0:T(2,128)S(1)} %get-tuple-element.99.response, ...), custom_call_target="tpu_custom_call", output_to_operand_aliasing={{2}: (5, {})} | custom-call | flops 536870912 | bytes 8388608 | tf_op jit(solution)/shard_map/contract_multi/pallas_call | solution.py:142
  17.5 2.4 %collective-permute-start.11 = (bf16[512,128]{1,0:T(8,128)(2,1)S(1)}, bf16[512,128]{1,0:T(8,128)(2,1)S(1)}, u32[]{:S(2)}, u32[]{:S(2)}) collective-permute-start(bf16[512,128]{1,0:T(8,128)(2,1)S(1)} %get-tuple-element.240), channel_id=1, source_target_pairs={{0,2},{1,3},{2,0},{3,1},{4,6},{5,7},{6,4},{7,5},{8,10},{9,11},{10,... | collective-permute-start | bytes 393224 | tf_op jit(solution)/shard_map/ppermute | solution.py:760
  19.9 1.5 %collective-permute-start.12 = (bf16[512,128]{1,0:T(8,128)(2,1)S(1)}, bf16[512,128]{1,0:T(8,128)(2,1)S(1)}, u32[]{:S(2)}, u32[]{:S(2)}) collective-permute-start(bf16[512,128]{1,0:T(8,128)(2,1)S(1)} %get-tuple-element.239), channel_id=1, source_target_pairs={{0,3},{1,0},{2,1},{3,2},{4,7},{5,4},{6,5},{7,6},{8,11},{9,8},{10,9... | collective-permute-start | bytes 393224 | tf_op jit(solution)/shard_map/ppermute | solution.py:760
  21.3 4.6 %contract_hyper.1 = (bf16[512,128]{1,0:T(8,128)(2,1)S(1)}, bf16[144,128]{1,0:T(8,128)(2,1)S(1)}) custom-call(s32[1]{0:T(128)} %bitcast.62.place, f32[17]{0:T(128)S(1)} %select_reduce_fusion.taps, f32[512,128]{1,0:T(8,128)S(1)} %get-tuple-element.105.columns, bf16[128,16]{1,0:T(8,128)(2,1)S(1)} %collective-permute-done.13.before, ...), custom_call_target="tpu_custom_call" | custom-call | tf_op jit(solution)/shard_map/contract_hyper/pallas_call | solution.py:227
  26.0 0.6 collective-permute-start.15
  26.6 1.5 %collective-permute-start.16 = (bf16[272,128]{1,0:T(8,128)(2,1)S(1)}, bf16[272,128]{1,0:T(8,128)(2,1)S(1)}, u32[]{:S(2)}, u32[]{:S(2)}) collective-permute-start(bf16[272,128]{1,0:T(8,128)(2,1)S(1)} %get-tuple-element.246), channel_id=1, source_target_pairs={{0,2},{1,3},{2,0},{3,1},{4,6},{5,7},{6,4},{7,5},{8,10},{9,11},{10,... | collective-permute-start | bytes 208904 | tf_op jit(solution)/shard_map/ppermute | solution.py:760
  28.2 2.8 %collective-permute-start.17 = (bf16[272,128]{1,0:T(8,128)(2,1)S(1)}, bf16[272,128]{1,0:T(8,128)(2,1)S(1)}, u32[]{:S(2)}, u32[]{:S(2)}) collective-permute-start(bf16[272,128]{1,0:T(8,128)(2,1)S(1)} %get-tuple-element.245), channel_id=1, source_target_pairs={{0,3},{1,0},{2,1},{3,2},{4,7},{5,4},{6,5},{7,6},{8,11},{9,8},{10,9... | collective-permute-start | bytes 208904 | tf_op jit(solution)/shard_map/ppermute | solution.py:760
  31.0 0.5 sum_arrived.1
  31.6 0.8 %collective-permute-done.15.refs_4_ = bf16[272,128]{1,0:T(8,128)(2,1)S(1)} collective-permute-done((bf16[272,128]{1,0:T(8,128)(2,1)S(1)}, bf16[272,128]{1,0:T(8,128)(2,1)S(1)}, u32[]{:S(2)}, u32[]{:S(2)}) %collective-permute-start.15) | collective-permute-done | bytes 69664 | tf_op jit(solution)/shard_map/ppermute | solution.py:760
  32.4 4.0 %collective-permute-done.16.refs_5_ = bf16[272,128]{1,0:T(8,128)(2,1)S(1)} collective-permute-done((bf16[272,128]{1,0:T(8,128)(2,1)S(1)}, bf16[272,128]{1,0:T(8,128)(2,1)S(1)}, u32[]{:S(2)}, u32[]{:S(2)}) %collective-permute-start.16) | collective-permute-done | bytes 69664 | tf_op jit(solution)/shard_map/ppermute | solution.py:760
  36.5 1.4 %collective-permute-start.18 = (f32[168,128]{1,0:T(8,128)S(1)}, f32[168,128]{1,0:T(8,128)S(1)}, u32[]{:S(2)}, u32[]{:S(2)}) collective-permute-start(f32[168,128]{1,0:T(8,128)S(1)} %get-tuple-element.111), channel_id=1, source_target_pairs={{0,1},{1,2},{2,3},{3,4},{4,5},{5,6},{6,7},{7,8},{8,9},{9,10},{10,1... | collective-permute-start | bytes 258056 | tf_op jit(solution)/shard_map/ppermute | solution.py:644
  37.8 4.0 %collective-permute-start.19 = (f32[168,128]{1,0:T(8,128)S(1)}, f32[168,128]{1,0:T(8,128)S(1)}, u32[]{:S(2)}, u32[]{:S(2)}) collective-permute-start(f32[168,128]{1,0:T(8,128)S(1)} %get-tuple-element.112), channel_id=1, source_target_pairs={{1,0},{2,1},{3,2},{4,3},{5,4},{6,5},{7,6},{8,7},{9,8},{10,9},{11,1... | collective-permute-start | bytes 258056 | tf_op jit(solution)/shard_map/ppermute | solution.py:648
  41.9 1.2 %collective-permute-done.20.other = f32[72,128]{1,0:T(8,128)S(1)} collective-permute-done((f32[72,128]{1,0:T(8,128)S(1)}, f32[72,128]{1,0:T(8,128)S(1)}, u32[]{:S(2)}, u32[]{:S(2)}) %collective-permute-start.20) | collective-permute-done | bytes 36896 | tf_op jit(solution)/shard_map/ppermute | solution.py:725
  43.1 1.4 %make_operator.1 = (f32[128,128]{1,0:T(8,128)S(1)}, f32[128,128]{1,0:T(8,128)S(1)}, bf16[256,256]{1,0:T(8,128)(2,1)S(1)}, bf16[256,256]{1,0:T(8,128)(2,1)S(1)}, f32[8,128]{1,0:T(8,128)S(1)}) custom-call(s32[1]{0:T(128)} %bitcast.62.place, f32[17]{0:T(128)S(1)} %select_reduce_fusion.taps, f32[128,128]{1,0:T(8,128)S(1)} %get-tuple-element.113.band_gram, ...), custom_call_target="tpu_custom_call" | custom-call | bytes 67108864 | tf_op jit(solution)/shard_map/make_operator/pallas_call | solution.py:304
  44.5 3.8 %make_basis.1 = (f32[6,4,128,128]{3,2,1,0:T(8,128)S(1)}, f32[32,1,128]{2,1,0:T(1,128)}) custom-call(f32[17]{0:T(128)S(1)} %select_reduce_fusion.taps, f32[512,128]{1,0:T(8,128)S(1)} %get-tuple-element.104.refs_2_.multi, f32[128,128]{1,0:T(8,128)S(1)} %get-tuple-element.110.hyper, f32[512,128]{1,0:T(8,128)S(1)} %get-tuple-element.109.refs_3_.start, ...), custom_call_target="tpu_custom_call" | custom-call | tf_op jit(solution)/shard_map/make_basis/pallas_call | solution.py:522
  48.3 5.2 %all-to-all-start = ((f32[32,1,128]{2,1,0:T(1,128)}), f32[32,1,128]{2,1,0:T(1,128)S(1)}, u32[]{:S(2)}, u32[]{:S(2)}) async-start(f32[32,1,128]{2,1,0:T(1,128)} %get-tuple-element.119), calls=%async_computation | async-start | bytes 32768 | tf_op jit(solution)/shard_map/all_to_all | solution.py:783
  53.5 7.1 %all-to-all-done.products = f32[32,1,128]{2,1,0:T(1,128)S(1)} async-done(((f32[32,1,128]{2,1,0:T(1,128)}), f32[32,1,128]{2,1,0:T(1,128)S(1)}, u32[]{:S(2)}, u32[]{:S(2)}) %all-to-all-start) | async-done | bytes 16416 | tf_op jit(solution)/shard_map/all_to_all | solution.py:783
  60.6 0.8 %make_coefficients.1 = (f32[16,128]{1,0:T(8,128)S(1)}, s32[1]{0:T(128)}) custom-call(f32[32,1,128]{2,1,0:T(1,128)S(1)} %all-to-all-done.products, f32[8,128]{1,0:T(8,128)S(1)} %get-tuple-element.118.bound), custom_call_target="tpu_custom_call" | custom-call | tf_op jit(solution)/shard_map/make_coefficients/pallas_call | solution.py:603
  62.1 1.2 %conditional.1 = ((f32[512,128]{1,0:T(8,128)}, f32[512,128]{1,0:T(8,128)})) conditional(s32[]{:T(128)} %bitcast.63, (f32[6,4,128,128]{3,2,1,0:T(8,128)S(1)}, f32[17]{0:T(128)S(1)}, f32[128,128]{1,0:T(8,128)S(1)}, f32[512,128]{1,0:T(8,128)S(1)}, f32[128,128]{1,0:T(8,128)S(1)}, /*index=5*/f32[128,128]{1,0:T(8,128)S(1)}) %tuple.20, ...), branch_computations={%region_1.10_spmd, %region_10.11_spmd} | conditional | flops 257967104 | bytes 23068832 | solution.py:790
  62.3 0.9 %combine.1 = (f32[512,128]{1,0:T(8,128)}, f32[512,128]{1,0:T(8,128)}) custom-call(f32[16,128]{1,0:T(8,128)S(1)} %get-tuple-element.65.coefficients, f32[6,4,128,128]{3,2,1,0:T(8,128)S(1)} %get-tuple-element.66.basis), custom_call_target="tpu_custom_call" | custom-call | tf_op jit(solution)/shard_map/cond/branch_1_fun/combine/pallas_call | solution.py:633
  (24 shorter events, 0.3 us)
Async XLA Ops:
  0.6 2.1 %collective-permute-start.6 = (bf16[16,512]{1,0:T(8,128)(2,1)}, bf16[16,512]{1,0:T(8,128)(2,1)S(1)}, u32[]{:S(2)}, u32[]{:S(2)}) collective-permute-start(bf16[16,512]{1,0:T(8,128)(2,1)} %bitcast.164), channel_id=1, source_target_pairs={{0,4},{4,0},{8,12},{12,8},{16,20},{20,16},{24,28},{28,24},{1,5},{5... | collective-permute-start | bytes 49160 | tf_op jit(solution)/shard_map/ppermute | solution.py:725
  2.7 7.9 %collective-permute-start.7 = (bf16[32,512]{1,0:T(8,128)(2,1)S(1)}, bf16[32,512]{1,0:T(8,128)(2,1)S(1)}, u32[]{:S(2)}, u32[]{:S(2)}) collective-permute-start(bf16[32,512]{1,0:T(8,128)(2,1)S(1)} %pad_maximum_fusion.10.refs_0_), channel_id=1, source_target_pairs={{0,8},{4,12},{8,0},{12,4},{16,24},{20,28},{24,16},{28,20},{1,9},{5... | collective-permute-start | bytes 98312 | tf_op jit(solution)/shard_map/ppermute | solution.py:725
  5.3 5.5 %collective-permute-start.8 = (bf16[32,512]{1,0:T(8,128)(2,1)S(1)}, bf16[32,512]{1,0:T(8,128)(2,1)S(1)}, u32[]{:S(2)}, u32[]{:S(2)}) collective-permute-start(bf16[32,512]{1,0:T(8,128)(2,1)S(1)} %pad_maximum_fusion.10.refs_0_), channel_id=1, source_target_pairs={{0,16},{4,20},{8,24},{12,28},{16,0},{20,4},{24,8},{28,12},{1,17},{... | collective-permute-start | bytes 98312 | tf_op jit(solution)/shard_map/ppermute | solution.py:725
  6.8 4.8 %collective-permute-start.9 = (bf16[32,512]{1,0:T(8,128)(2,1)S(1)}, bf16[32,512]{1,0:T(8,128)(2,1)S(1)}, u32[]{:S(2)}, u32[]{:S(2)}) collective-permute-start(bf16[32,512]{1,0:T(8,128)(2,1)S(1)} %pad_maximum_fusion.10.refs_0_), channel_id=1, source_target_pairs={{0,24},{4,28},{8,16},{12,20},{16,8},{20,12},{24,0},{28,4},{1,25},{... | collective-permute-start | bytes 98312 | tf_op jit(solution)/shard_map/ppermute | solution.py:725
  11.7 9.6 %collective-permute-start.13 = (bf16[128,16]{1,0:T(8,128)(2,1)S(1)}, bf16[128,16]{1,0:T(8,128)(2,1)S(1)}, u32[]{:S(2)}, u32[]{:S(2)}) collective-permute-start(bf16[128,16]{1,0:T(8,128)(2,1)S(1)} %pad_maximum_fusion.11), channel_id=1, source_target_pairs={{0,1},{1,2},{2,3},{3,0},{4,5},{5,6},{6,7},{7,4},{8,9},{9,10},{10,1... | collective-permute-start | bytes 12296 | tf_op jit(solution)/shard_map/ppermute | solution.py:644
  13.3 8.0 %collective-permute-start.14 = (bf16[128,16]{1,0:T(8,128)(2,1)S(1)}, bf16[128,16]{1,0:T(8,128)(2,1)S(1)}, u32[]{:S(2)}, u32[]{:S(2)}) collective-permute-start(bf16[128,16]{1,0:T(8,128)(2,1)S(1)} %pad_maximum_fusion.12), channel_id=1, source_target_pairs={{1,0},{2,1},{3,2},{0,3},{5,4},{6,5},{7,6},{4,7},{9,8},{10,9},{11,1... | collective-permute-start | bytes 12296 | tf_op jit(solution)/shard_map/ppermute | solution.py:648
  17.5 10.7 %collective-permute-start.10 = (bf16[512,128]{1,0:T(8,128)(2,1)S(1)}, bf16[512,128]{1,0:T(8,128)(2,1)S(1)}, u32[]{:S(2)}, u32[]{:S(2)}) collective-permute-start(bf16[512,128]{1,0:T(8,128)(2,1)S(1)} %get-tuple-element.241), channel_id=1, source_target_pairs={{0,1},{1,2},{2,3},{3,0},{4,5},{5,6},{6,7},{7,4},{8,9},{9,10},{10,1... | collective-permute-start | bytes 393224 | tf_op jit(solution)/shard_map/ppermute | solution.py:760
  17.5 13.5 %collective-permute-start.11 = (bf16[512,128]{1,0:T(8,128)(2,1)S(1)}, bf16[512,128]{1,0:T(8,128)(2,1)S(1)}, u32[]{:S(2)}, u32[]{:S(2)}) collective-permute-start(bf16[512,128]{1,0:T(8,128)(2,1)S(1)} %get-tuple-element.240), channel_id=1, source_target_pairs={{0,2},{1,3},{2,0},{3,1},{4,6},{5,7},{6,4},{7,5},{8,10},{9,11},{10,... | collective-permute-start | bytes 393224 | tf_op jit(solution)/shard_map/ppermute | solution.py:760
  19.9 11.1 %collective-permute-start.12 = (bf16[512,128]{1,0:T(8,128)(2,1)S(1)}, bf16[512,128]{1,0:T(8,128)(2,1)S(1)}, u32[]{:S(2)}, u32[]{:S(2)}) collective-permute-start(bf16[512,128]{1,0:T(8,128)(2,1)S(1)} %get-tuple-element.239), channel_id=1, source_target_pairs={{0,3},{1,0},{2,1},{3,2},{4,7},{5,4},{6,5},{7,6},{8,11},{9,8},{10,9... | collective-permute-start | bytes 393224 | tf_op jit(solution)/shard_map/ppermute | solution.py:760
  26.0 6.3 %collective-permute-start.15 = (bf16[272,128]{1,0:T(8,128)(2,1)S(1)}, bf16[272,128]{1,0:T(8,128)(2,1)S(1)}, u32[]{:S(2)}, u32[]{:S(2)}) collective-permute-start(bf16[272,128]{1,0:T(8,128)(2,1)S(1)} %get-tuple-element.247), channel_id=1, source_target_pairs={{0,1},{1,2},{2,3},{3,0},{4,5},{5,6},{6,7},{7,4},{8,9},{9,10},{10,1... | collective-permute-start | bytes 208904 | tf_op jit(solution)/shard_map/ppermute | solution.py:760
  26.6 9.8 %collective-permute-start.16 = (bf16[272,128]{1,0:T(8,128)(2,1)S(1)}, bf16[272,128]{1,0:T(8,128)(2,1)S(1)}, u32[]{:S(2)}, u32[]{:S(2)}) collective-permute-start(bf16[272,128]{1,0:T(8,128)(2,1)S(1)} %get-tuple-element.246), channel_id=1, source_target_pairs={{0,2},{1,3},{2,0},{3,1},{4,6},{5,7},{6,4},{7,5},{8,10},{9,11},{10,... | collective-permute-start | bytes 208904 | tf_op jit(solution)/shard_map/ppermute | solution.py:760
  28.2 8.2 %collective-permute-start.17 = (bf16[272,128]{1,0:T(8,128)(2,1)S(1)}, bf16[272,128]{1,0:T(8,128)(2,1)S(1)}, u32[]{:S(2)}, u32[]{:S(2)}) collective-permute-start(bf16[272,128]{1,0:T(8,128)(2,1)S(1)} %get-tuple-element.245), channel_id=1, source_target_pairs={{0,3},{1,0},{2,1},{3,2},{4,7},{5,4},{6,5},{7,6},{8,11},{9,8},{10,9... | collective-permute-start | bytes 208904 | tf_op jit(solution)/shard_map/ppermute | solution.py:760
  36.5 8.1 %collective-permute-start.18 = (f32[168,128]{1,0:T(8,128)S(1)}, f32[168,128]{1,0:T(8,128)S(1)}, u32[]{:S(2)}, u32[]{:S(2)}) collective-permute-start(f32[168,128]{1,0:T(8,128)S(1)} %get-tuple-element.111), channel_id=1, source_target_pairs={{0,1},{1,2},{2,3},{3,4},{4,5},{5,6},{6,7},{7,8},{8,9},{9,10},{10,1... | collective-permute-start | bytes 258056 | tf_op jit(solution)/shard_map/ppermute | solution.py:644
  37.8 6.7 %collective-permute-start.19 = (f32[168,128]{1,0:T(8,128)S(1)}, f32[168,128]{1,0:T(8,128)S(1)}, u32[]{:S(2)}, u32[]{:S(2)}) collective-permute-start(f32[168,128]{1,0:T(8,128)S(1)} %get-tuple-element.112), channel_id=1, source_target_pairs={{1,0},{2,1},{3,2},{4,3},{5,4},{6,5},{7,6},{8,7},{9,8},{10,9},{11,1... | collective-permute-start | bytes 258056 | tf_op jit(solution)/shard_map/ppermute | solution.py:648
  41.9 1.2 %collective-permute-start.20 = (f32[72,128]{1,0:T(8,128)S(1)}, f32[72,128]{1,0:T(8,128)S(1)}, u32[]{:S(2)}, u32[]{:S(2)}) collective-permute-start(f32[72,128]{1,0:T(8,128)S(1)} %get-tuple-element.115.own), channel_id=1, source_target_pairs={{0,4},{4,0},{8,12},{12,8},{16,20},{20,16},{24,28},{28,24},{1,5},{5... | collective-permute-start | bytes 110600 | tf_op jit(solution)/shard_map/ppermute | solution.py:725
  48.3 12.3 %all-to-all-start = ((f32[32,1,128]{2,1,0:T(1,128)}), f32[32,1,128]{2,1,0:T(1,128)S(1)}, u32[]{:S(2)}, u32[]{:S(2)}) async-start(f32[32,1,128]{2,1,0:T(1,128)} %get-tuple-element.119), calls=%async_computation | async-start | bytes 32768 | tf_op jit(solution)/shard_map/all_to_all | solution.py:783

commit v5 on v4

--- a/solution.py
+++ b/solution.py
@@ -451,9 +451,14 @@
     first, second = DEC * RIM_MULTI, DEC * RIM_MULTI + RIM
     own = slice(RIM, RIM + coarse)
 
-    def apply(field):
-        lowered = times(blur_down(taps, field), hyper_w[...])
-        return [blur_up(taps, lowered, phase) + times(field(phase), multi_w[...]) for phase in range(DEC)]
+    def apply(which, rim):
+        rows = slice(RIM - rim, RIM + coarse + rim)
+        fields = [held[which, phase, rows, :] for phase in range(DEC)]
+        lowered = times(blur_down(taps, lambda phase: fields[phase]), hyper_w[...])
+        return rows, [
+            blur_up(taps, lowered, phase) + times(fields[phase], multi_w[...])
+            for phase in range(DEC)
+        ]
 
     margin = DEC * (RIM - RIM_START)
     none = jnp.zeros((margin, multi.shape[1]), jnp.float32)
@@ -465,7 +470,7 @@
     for phase in range(DEC):
         held[1, phase] = natural[pl.ds(phase, wide, stride=DEC), :]
         basis[ITERS + 1, phase] = held[1, phase, own, :]
-    mapped = apply(lambda phase: held[1, phase])
+    _, mapped = apply(1, RIM)
 
     lifted[:RIM, :] = before[first:second, :]
     lifted[own, :] = hyper[...]
@@ -485,17 +490,19 @@
 
     for step in range(ITERS):
         now = step % 2
-        mapped = apply(lambda phase: held[now, phase])
+        rim = -(-REACH * 2 * (ITERS - step) // 8) * 8
+        rows, mapped = apply(now, rim)
         for phase in range(DEC):
             basis[step, phase] = held[now, phase, own, :]
+            field = held[now, phase, rows, :]
             if step == 0:
-                result = 0.5 * mapped[phase] - held[now, phase]
+                result = 0.5 * mapped[phase] - field
             else:
-                result = mapped[phase] - 2.0 * held[now, phase] - held[1 - now, phase]
+                result = mapped[phase] - 2.0 * field - held[1 - now, phase, rows, :]
             if step < ITERS - 1:
-                held[1 - now, phase] = result
+                held[1 - now, phase, rows, :] = result
             else:
-                basis[ITERS, phase] = result[own, :]
+                basis[ITERS, phase] = result[rim : rim + coarse, :]
     rows = []
     for i, j in PAIRS:
         total = jnp.zeros((coarse, multi.shape[1]), jnp.float32)
@@ -517,7 +524,7 @@
     arrays = (multi, hyper, start, before, after, hyper_w, multi_w, bound)
     outs = [
         jax.ShapeDtypeStruct((ITERS + 2, DEC, coarse, rank), jnp.float32),
-        jax.ShapeDtypeStruct((devices, 1, rank), jnp.float32),
+        pltpu.VMEM((devices, 1, rank), jnp.float32),
     ]
     return pl.pallas_call(
         functools.partial(basis_kernel, devices),
@@ -606,7 +613,7 @@
         out_specs=[whole((16, rank)), SMEM],
         out_shape=[
             jax.ShapeDtypeStruct((16, rank), jnp.float32),
-            jax.ShapeDtypeStruct((1,), jnp.int32),
+            pltpu.SMEM((1,), jnp.int32),
         ],
         compiler_params=params(),
         name="make_coefficients",

time: 63.5 us -> 62.1 us (0.978)
  Pallas kernels: 17.6 us -> 16.9 us
  between operations: 1.47 us -> 0.81 us
  transfers between devices with their start and end apart: 16 -> 16, of which waited for: 5 -> 5; matrix products, arithmetic and copies ran while one was open for 3% -> 3% of each run, Pallas kernels for 19% -> 20%
where the time goes in v5:
time: 62.1 us; the launch traced here: 61.8 us
  starting transfers between devices  28 us (45%)
  Pallas kernels  16.9 us (27%)
  waiting for transfers between devices  14 us (23%)
  local copies, waits for them, and re-layouts  1.09 us (2%)
  between operations  0.81 us (1%)
  other arithmetic  0.8 us (1%)
    ppermute x6, starting transfers between devices, exchange(): lax.ppermute(piece, 'col', [(i, (i + distance) % across) for i in range(a...  8.87 us
    all_to_all x1, waiting for transfers between devices, body(): products = lax.all_to_all(products, BOTH, 0, 0, tiled=True)  7.1 us
    ppermute x2, starting transfers between devices, to_previous(): lax.ppermute(values, axis, [((i + 1) % count, i) for i in range(count)])  6.34 us
    all_to_all x1, starting transfers between devices, body(): products = lax.all_to_all(products, BOTH, 0, 0, tiled=True)  5.21 us
    ppermute x6, waiting for transfers between devices, exchange(): lax.ppermute(piece, 'col', [(i, (i + distance) % across) for i in range(a...  4.84 us
    ppermute x5, starting transfers between devices, exchanged(): lax.ppermute(values, 'row', [(i, i ^ distance) for i in range(along)])  4.64 us
    pallas_call x1, Pallas kernels, contract_hyper(): pl.pallas_call(functools.partial(hyper_kernel, share), in_specs=[SMEM, SM...  4.61 us
    pallas_call x1, Pallas kernels, load(): pl.pallas_call(functools.partial(load_kernel, ranges), in_specs=[pl.Block...  3.74 us
  transfers between devices with their start and end apart: 16, of which 5 were waited for; matrix products, arithmetic and copies ran while one was open for 3% of the time, Pallas kernels for 20%

profile of v5, /device:TPU:0, one launch (start us, length us, event | category | flops | bytes accessed | tf_op | source)
XLA Modules:
  0.0 61.8 jit_solution(16154324493376990945)
XLA Ops:
  0.6 0.5 collective-permute-start.6
  1.2 0.8 %select_reduce_fusion.taps = f32[17]{0:T(128)S(1)} fusion(f32[9]{0:T(128)} %param.18, s32[17]{0:T(128)S(1)} %iota_add_fusion, s32[9]{0:T(128)} %param.19), kind=kLoop, calls=%fused_computation.155 | loop fusion | flops 442 | bytes 208 | tf_op jit(solution)/shard_map/reduce_sum | solution.py:756
  2.0 0.7 %concatenate.36 = bf16[32,512]{1,0:T(8,128)(2,1)S(1)} pad(bf16[16,512]{1,0:T(8,128)(2,1)} %bitcast.165, bf16[]{:T(256)} %constant.54.clone.1), padding=0_16x0_0 | pad | bytes 49154 | tf_op jit(solution)/shard_map/concatenate | solution.py:736
  2.7 2.6 %collective-permute-start.7 = (bf16[32,512]{1,0:T(8,128)(2,1)S(1)}, bf16[32,512]{1,0:T(8,128)(2,1)S(1)}, u32[]{:S(2)}, u32[]{:S(2)}) collective-permute-start(bf16[32,512]{1,0:T(8,128)(2,1)S(1)} %pad_maximum_fusion.10.refs_0_), channel_id=1, source_target_pairs={{0,8},{4,12},{8,0},{12,4},{16,24},{20,28},{24,16},{28,20},{1,9},{5... | collective-permute-start | bytes 98312 | tf_op jit(solution)/shard_map/ppermute | solution.py:732
  5.3 1.5 %collective-permute-start.8 = (bf16[32,512]{1,0:T(8,128)(2,1)S(1)}, bf16[32,512]{1,0:T(8,128)(2,1)S(1)}, u32[]{:S(2)}, u32[]{:S(2)}) collective-permute-start(bf16[32,512]{1,0:T(8,128)(2,1)S(1)} %pad_maximum_fusion.10.refs_0_), channel_id=1, source_target_pairs={{0,16},{4,20},{8,24},{12,28},{16,0},{20,4},{24,8},{28,12},{1,17},{... | collective-permute-start | bytes 98312 | tf_op jit(solution)/shard_map/ppermute | solution.py:732
  6.8 0.1 fusion.117
  6.9 3.7 %load.1 = (bf16[2,2048,512]{2,1,0:T(8,128)(2,1)S(1)}, f32[96,128]{1,0:T(8,128)S(1)}, f32[2,96]{1,0:T(2,128)S(1)}, f32[512,128]{1,0:T(8,128)S(1)}, bf16[56,512,128]{2,1,0:T(8,128)(2,1)S(1)}) custom-call(bf16[2,2048,512]{2,1,0:T(8,128)(2,1)} %refs_0_, f32[96,128]{1,0:T(8,128)} %refs_1_.1, f32[2,96]{1,0:T(2,128)} %refs_2_.1, f32[512,128]{1,0:T(8,128)} %refs_3_.1, ...), custom_call_target="tpu_custom_call" | custom-call | bytes 23692800 | tf_op jit(solution)/shard_map/load/pallas_call | solution.py:80
  10.6 0.1 fusion.118
  10.7 0.1 fusion.119
  10.8 0.8 %collective-permute-done.9.refs_3_ = bf16[32,512]{1,0:T(8,128)(2,1)S(1)} collective-permute-done((bf16[32,512]{1,0:T(8,128)(2,1)S(1)}, bf16[32,512]{1,0:T(8,128)(2,1)S(1)}, u32[]{:S(2)}, u32[]{:S(2)}) %collective-permute-start.9) | collective-permute-done | bytes 32800 | tf_op jit(solution)/shard_map/ppermute | solution.py:732
  11.7 1.6 %collective-permute-start.13 = (bf16[128,16]{1,0:T(8,128)(2,1)S(1)}, bf16[128,16]{1,0:T(8,128)(2,1)S(1)}, u32[]{:S(2)}, u32[]{:S(2)}) collective-permute-start(bf16[128,16]{1,0:T(8,128)(2,1)S(1)} %pad_maximum_fusion.11), channel_id=1, source_target_pairs={{0,1},{1,2},{2,3},{3,0},{4,5},{5,6},{6,7},{7,4},{8,9},{9,10},{10,1... | collective-permute-start | bytes 12296 | tf_op jit(solution)/shard_map/ppermute | solution.py:651
  13.3 2.3 %collective-permute-start.14 = (bf16[128,16]{1,0:T(8,128)(2,1)S(1)}, bf16[128,16]{1,0:T(8,128)(2,1)S(1)}, u32[]{:S(2)}, u32[]{:S(2)}) collective-permute-start(bf16[128,16]{1,0:T(8,128)(2,1)S(1)} %pad_maximum_fusion.12), channel_id=1, source_target_pairs={{1,0},{2,1},{3,2},{0,3},{5,4},{6,5},{7,6},{4,7},{9,8},{10,9},{11,1... | collective-permute-start | bytes 12296 | tf_op jit(solution)/shard_map/ppermute | solution.py:655
  15.6 1.8 %contract_multi.1 = (bf16[2048,128]{1,0:T(8,128)(2,1)S(1)}, f32[512,128]{1,0:T(8,128)S(1)}, bf16[56,512,128]{2,1,0:T(8,128)(2,1)S(1)}) custom-call(s32[1]{0:T(128)} %bitcast.62.place, f32[96,128]{1,0:T(8,128)S(1)} %get-tuple-element.98.band, f32[2,96]{1,0:T(2,128)S(1)} %get-tuple-element.99.response, ...), custom_call_target="tpu_custom_call", output_to_operand_aliasing={{2}: (5, {})} | custom-call | flops 536870912 | bytes 8388608 | tf_op jit(solution)/shard_map/contract_multi/pallas_call | solution.py:142
  17.5 2.4 %collective-permute-start.11 = (bf16[512,128]{1,0:T(8,128)(2,1)S(1)}, bf16[512,128]{1,0:T(8,128)(2,1)S(1)}, u32[]{:S(2)}, u32[]{:S(2)}) collective-permute-start(bf16[512,128]{1,0:T(8,128)(2,1)S(1)} %get-tuple-element.240), channel_id=1, source_target_pairs={{0,2},{1,3},{2,0},{3,1},{4,6},{5,7},{6,4},{7,5},{8,10},{9,11},{10,... | collective-permute-start | bytes 393224 | tf_op jit(solution)/shard_map/ppermute | solution.py:767
  19.9 1.5 %collective-permute-start.12 = (bf16[512,128]{1,0:T(8,128)(2,1)S(1)}, bf16[512,128]{1,0:T(8,128)(2,1)S(1)}, u32[]{:S(2)}, u32[]{:S(2)}) collective-permute-start(bf16[512,128]{1,0:T(8,128)(2,1)S(1)} %get-tuple-element.239), channel_id=1, source_target_pairs={{0,3},{1,0},{2,1},{3,2},{4,7},{5,4},{6,5},{7,6},{8,11},{9,8},{10,9... | collective-permute-start | bytes 393224 | tf_op jit(solution)/shard_map/ppermute | solution.py:767
  21.3 4.6 %contract_hyper.1 = (bf16[512,128]{1,0:T(8,128)(2,1)S(1)}, bf16[144,128]{1,0:T(8,128)(2,1)S(1)}) custom-call(s32[1]{0:T(128)} %bitcast.62.place, f32[17]{0:T(128)S(1)} %select_reduce_fusion.taps, f32[512,128]{1,0:T(8,128)S(1)} %get-tuple-element.105.columns, bf16[128,16]{1,0:T(8,128)(2,1)S(1)} %collective-permute-done.13.before, ...), custom_call_target="tpu_custom_call" | custom-call | tf_op jit(solution)/shard_map/contract_hyper/pallas_call | solution.py:227
  26.0 0.6 %collective-permute-start.15 = (bf16[272,128]{1,0:T(8,128)(2,1)S(1)}, bf16[272,128]{1,0:T(8,128)(2,1)S(1)}, u32[]{:S(2)}, u32[]{:S(2)}) collective-permute-start(bf16[272,128]{1,0:T(8,128)(2,1)S(1)} %get-tuple-element.247), channel_id=1, source_target_pairs={{0,1},{1,2},{2,3},{3,0},{4,5},{5,6},{6,7},{7,4},{8,9},{9,10},{10,1... | collective-permute-start | bytes 208904 | tf_op jit(solution)/shard_map/ppermute | solution.py:767
  26.6 1.5 %collective-permute-start.16 = (bf16[272,128]{1,0:T(8,128)(2,1)S(1)}, bf16[272,128]{1,0:T(8,128)(2,1)S(1)}, u32[]{:S(2)}, u32[]{:S(2)}) collective-permute-start(bf16[272,128]{1,0:T(8,128)(2,1)S(1)} %get-tuple-element.246), channel_id=1, source_target_pairs={{0,2},{1,3},{2,0},{3,1},{4,6},{5,7},{6,4},{7,5},{8,10},{9,11},{10,... | collective-permute-start | bytes 208904 | tf_op jit(solution)/shard_map/ppermute | solution.py:767
  28.2 2.8 %collective-permute-start.17 = (bf16[272,128]{1,0:T(8,128)(2,1)S(1)}, bf16[272,128]{1,0:T(8,128)(2,1)S(1)}, u32[]{:S(2)}, u32[]{:S(2)}) collective-permute-start(bf16[272,128]{1,0:T(8,128)(2,1)S(1)} %get-tuple-element.245), channel_id=1, source_target_pairs={{0,3},{1,0},{2,1},{3,2},{4,7},{5,4},{6,5},{7,6},{8,11},{9,8},{10,9... | collective-permute-start | bytes 208904 | tf_op jit(solution)/shard_map/ppermute | solution.py:767
  31.0 0.5 sum_arrived.1
  31.6 0.8 %collective-permute-done.15.refs_4_ = bf16[272,128]{1,0:T(8,128)(2,1)S(1)} collective-permute-done((bf16[272,128]{1,0:T(8,128)(2,1)S(1)}, bf16[272,128]{1,0:T(8,128)(2,1)S(1)}, u32[]{:S(2)}, u32[]{:S(2)}) %collective-permute-start.15) | collective-permute-done | bytes 69664 | tf_op jit(solution)/shard_map/ppermute | solution.py:767
  32.4 4.0 %collective-permute-done.16.refs_5_ = bf16[272,128]{1,0:T(8,128)(2,1)S(1)} collective-permute-done((bf16[272,128]{1,0:T(8,128)(2,1)S(1)}, bf16[272,128]{1,0:T(8,128)(2,1)S(1)}, u32[]{:S(2)}, u32[]{:S(2)}) %collective-permute-start.16) | collective-permute-done | bytes 69664 | tf_op jit(solution)/shard_map/ppermute | solution.py:767
  36.5 1.4 %collective-permute-start.18 = (f32[168,128]{1,0:T(8,128)S(1)}, f32[168,128]{1,0:T(8,128)S(1)}, u32[]{:S(2)}, u32[]{:S(2)}) collective-permute-start(f32[168,128]{1,0:T(8,128)S(1)} %get-tuple-element.111), channel_id=1, source_target_pairs={{0,1},{1,2},{2,3},{3,4},{4,5},{5,6},{6,7},{7,8},{8,9},{9,10},{10,1... | collective-permute-start | bytes 258056 | tf_op jit(solution)/shard_map/ppermute | solution.py:651
  37.8 4.0 %collective-permute-start.19 = (f32[168,128]{1,0:T(8,128)S(1)}, f32[168,128]{1,0:T(8,128)S(1)}, u32[]{:S(2)}, u32[]{:S(2)}) collective-permute-start(f32[168,128]{1,0:T(8,128)S(1)} %get-tuple-element.112), channel_id=1, source_target_pairs={{1,0},{2,1},{3,2},{4,3},{5,4},{6,5},{7,6},{8,7},{9,8},{10,9},{11,1... | collective-permute-start | bytes 258056 | tf_op jit(solution)/shard_map/ppermute | solution.py:655
  41.9 1.2 %collective-permute-done.20.other = f32[72,128]{1,0:T(8,128)S(1)} collective-permute-done((f32[72,128]{1,0:T(8,128)S(1)}, f32[72,128]{1,0:T(8,128)S(1)}, u32[]{:S(2)}, u32[]{:S(2)}) %collective-permute-start.20) | collective-permute-done | bytes 36896 | tf_op jit(solution)/shard_map/ppermute | solution.py:732
  43.1 1.4 %make_operator.1 = (f32[128,128]{1,0:T(8,128)S(1)}, f32[128,128]{1,0:T(8,128)S(1)}, bf16[256,256]{1,0:T(8,128)(2,1)S(1)}, bf16[256,256]{1,0:T(8,128)(2,1)S(1)}, f32[8,128]{1,0:T(8,128)S(1)}) custom-call(s32[1]{0:T(128)} %bitcast.62.place, f32[17]{0:T(128)S(1)} %select_reduce_fusion.taps, f32[128,128]{1,0:T(8,128)S(1)} %get-tuple-element.113.band_gram, ...), custom_call_target="tpu_custom_call" | custom-call | bytes 67108864 | tf_op jit(solution)/shard_map/make_operator/pallas_call | solution.py:304
  44.5 3.5 %make_basis.1 = (f32[6,4,128,128]{3,2,1,0:T(8,128)S(1)}, f32[32,1,128]{2,1,0:T(1,128)}) custom-call(f32[17]{0:T(128)S(1)} %select_reduce_fusion.taps, f32[512,128]{1,0:T(8,128)S(1)} %get-tuple-element.104.refs_2_.multi, f32[128,128]{1,0:T(8,128)S(1)} %get-tuple-element.110.hyper, f32[512,128]{1,0:T(8,128)S(1)} %get-tuple-element.109.refs_3_.start, ...), custom_call_target="tpu_custom_call" | custom-call | tf_op jit(solution)/shard_map/make_basis/pallas_call | solution.py:529
  48.1 5.2 %all-to-all-start = ((f32[32,1,128]{2,1,0:T(1,128)}), f32[32,1,128]{2,1,0:T(1,128)S(1)}, u32[]{:S(2)}, u32[]{:S(2)}) async-start(f32[32,1,128]{2,1,0:T(1,128)} %get-tuple-element.119), calls=%async_computation | async-start | bytes 32768 | tf_op jit(solution)/shard_map/all_to_all | solution.py:790
  53.3 7.1 %all-to-all-done.products = f32[32,1,128]{2,1,0:T(1,128)S(1)} async-done(((f32[32,1,128]{2,1,0:T(1,128)}), f32[32,1,128]{2,1,0:T(1,128)S(1)}, u32[]{:S(2)}, u32[]{:S(2)}) %all-to-all-start) | async-done | bytes 16416 | tf_op jit(solution)/shard_map/all_to_all | solution.py:790
  60.4 0.3 make_coefficients.1
  60.7 1.2 %conditional.1 = ((f32[512,128]{1,0:T(8,128)}, f32[512,128]{1,0:T(8,128)})) conditional(s32[]{:T(128)} %bitcast.63, (f32[6,4,128,128]{3,2,1,0:T(8,128)S(1)}, f32[17]{0:T(128)S(1)}, f32[128,128]{1,0:T(8,128)S(1)}, f32[512,128]{1,0:T(8,128)S(1)}, f32[128,128]{1,0:T(8,128)S(1)}, /*index=5*/f32[128,128]{1,0:T(8,128)S(1)}) %tuple.20, ...), branch_computations={%region_1.10_spmd, %region_10.11_spmd} | conditional | flops 257967104 | bytes 23068832 | solution.py:797
  60.9 0.9 %combine.1 = (f32[512,128]{1,0:T(8,128)}, f32[512,128]{1,0:T(8,128)}) custom-call(f32[16,128]{1,0:T(8,128)S(1)} %get-tuple-element.65.coefficients, f32[6,4,128,128]{3,2,1,0:T(8,128)S(1)} %get-tuple-element.66.basis), custom_call_target="tpu_custom_call" | custom-call | tf_op jit(solution)/shard_map/cond/branch_1_fun/combine/pallas_call | solution.py:640
  (24 shorter events, 0.3 us)
Async XLA Ops:
  0.6 2.1 %collective-permute-start.6 = (bf16[16,512]{1,0:T(8,128)(2,1)}, bf16[16,512]{1,0:T(8,128)(2,1)S(1)}, u32[]{:S(2)}, u32[]{:S(2)}) collective-permute-start(bf16[16,512]{1,0:T(8,128)(2,1)} %bitcast.164), channel_id=1, source_target_pairs={{0,4},{4,0},{8,12},{12,8},{16,20},{20,16},{24,28},{28,24},{1,5},{5... | collective-permute-start | bytes 49160 | tf_op jit(solution)/shard_map/ppermute | solution.py:732
  2.7 7.9 %collective-permute-start.7 = (bf16[32,512]{1,0:T(8,128)(2,1)S(1)}, bf16[32,512]{1,0:T(8,128)(2,1)S(1)}, u32[]{:S(2)}, u32[]{:S(2)}) collective-permute-start(bf16[32,512]{1,0:T(8,128)(2,1)S(1)} %pad_maximum_fusion.10.refs_0_), channel_id=1, source_target_pairs={{0,8},{4,12},{8,0},{12,4},{16,24},{20,28},{24,16},{28,20},{1,9},{5... | collective-permute-start | bytes 98312 | tf_op jit(solution)/shard_map/ppermute | solution.py:732
  5.3 5.5 %collective-permute-start.8 = (bf16[32,512]{1,0:T(8,128)(2,1)S(1)}, bf16[32,512]{1,0:T(8,128)(2,1)S(1)}, u32[]{:S(2)}, u32[]{:S(2)}) collective-permute-start(bf16[32,512]{1,0:T(8,128)(2,1)S(1)} %pad_maximum_fusion.10.refs_0_), channel_id=1, source_target_pairs={{0,16},{4,20},{8,24},{12,28},{16,0},{20,4},{24,8},{28,12},{1,17},{... | collective-permute-start | bytes 98312 | tf_op jit(solution)/shard_map/ppermute | solution.py:732
  6.8 4.8 %collective-permute-start.9 = (bf16[32,512]{1,0:T(8,128)(2,1)S(1)}, bf16[32,512]{1,0:T(8,128)(2,1)S(1)}, u32[]{:S(2)}, u32[]{:S(2)}) collective-permute-start(bf16[32,512]{1,0:T(8,128)(2,1)S(1)} %pad_maximum_fusion.10.refs_0_), channel_id=1, source_target_pairs={{0,24},{4,28},{8,16},{12,20},{16,8},{20,12},{24,0},{28,4},{1,25},{... | collective-permute-start | bytes 98312 | tf_op jit(solution)/shard_map/ppermute | solution.py:732
  11.7 9.6 %collective-permute-start.13 = (bf16[128,16]{1,0:T(8,128)(2,1)S(1)}, bf16[128,16]{1,0:T(8,128)(2,1)S(1)}, u32[]{:S(2)}, u32[]{:S(2)}) collective-permute-start(bf16[128,16]{1,0:T(8,128)(2,1)S(1)} %pad_maximum_fusion.11), channel_id=1, source_target_pairs={{0,1},{1,2},{2,3},{3,0},{4,5},{5,6},{6,7},{7,4},{8,9},{9,10},{10,1... | collective-permute-start | bytes 12296 | tf_op jit(solution)/shard_map/ppermute | solution.py:651
  13.3 8.0 %collective-permute-start.14 = (bf16[128,16]{1,0:T(8,128)(2,1)S(1)}, bf16[128,16]{1,0:T(8,128)(2,1)S(1)}, u32[]{:S(2)}, u32[]{:S(2)}) collective-permute-start(bf16[128,16]{1,0:T(8,128)(2,1)S(1)} %pad_maximum_fusion.12), channel_id=1, source_target_pairs={{1,0},{2,1},{3,2},{0,3},{5,4},{6,5},{7,6},{4,7},{9,8},{10,9},{11,1... | collective-permute-start | bytes 12296 | tf_op jit(solution)/shard_map/ppermute | solution.py:655
  17.5 10.7 %collective-permute-start.10 = (bf16[512,128]{1,0:T(8,128)(2,1)S(1)}, bf16[512,128]{1,0:T(8,128)(2,1)S(1)}, u32[]{:S(2)}, u32[]{:S(2)}) collective-permute-start(bf16[512,128]{1,0:T(8,128)(2,1)S(1)} %get-tuple-element.241), channel_id=1, source_target_pairs={{0,1},{1,2},{2,3},{3,0},{4,5},{5,6},{6,7},{7,4},{8,9},{9,10},{10,1... | collective-permute-start | bytes 393224 | tf_op jit(solution)/shard_map/ppermute | solution.py:767
  17.5 13.5 %collective-permute-start.11 = (bf16[512,128]{1,0:T(8,128)(2,1)S(1)}, bf16[512,128]{1,0:T(8,128)(2,1)S(1)}, u32[]{:S(2)}, u32[]{:S(2)}) collective-permute-start(bf16[512,128]{1,0:T(8,128)(2,1)S(1)} %get-tuple-element.240), channel_id=1, source_target_pairs={{0,2},{1,3},{2,0},{3,1},{4,6},{5,7},{6,4},{7,5},{8,10},{9,11},{10,... | collective-permute-start | bytes 393224 | tf_op jit(solution)/shard_map/ppermute | solution.py:767
  19.9 11.1 %collective-permute-start.12 = (bf16[512,128]{1,0:T(8,128)(2,1)S(1)}, bf16[512,128]{1,0:T(8,128)(2,1)S(1)}, u32[]{:S(2)}, u32[]{:S(2)}) collective-permute-start(bf16[512,128]{1,0:T(8,128)(2,1)S(1)} %get-tuple-element.239), channel_id=1, source_target_pairs={{0,3},{1,0},{2,1},{3,2},{4,7},{5,4},{6,5},{7,6},{8,11},{9,8},{10,9... | collective-permute-start | bytes 393224 | tf_op jit(solution)/shard_map/ppermute | solution.py:767
  26.0 6.3 %collective-permute-start.15 = (bf16[272,128]{1,0:T(8,128)(2,1)S(1)}, bf16[272,128]{1,0:T(8,128)(2,1)S(1)}, u32[]{:S(2)}, u32[]{:S(2)}) collective-permute-start(bf16[272,128]{1,0:T(8,128)(2,1)S(1)} %get-tuple-element.247), channel_id=1, source_target_pairs={{0,1},{1,2},{2,3},{3,0},{4,5},{5,6},{6,7},{7,4},{8,9},{9,10},{10,1... | collective-permute-start | bytes 208904 | tf_op jit(solution)/shard_map/ppermute | solution.py:767
  26.6 9.8 %collective-permute-start.16 = (bf16[272,128]{1,0:T(8,128)(2,1)S(1)}, bf16[272,128]{1,0:T(8,128)(2,1)S(1)}, u32[]{:S(2)}, u32[]{:S(2)}) collective-permute-start(bf16[272,128]{1,0:T(8,128)(2,1)S(1)} %get-tuple-element.246), channel_id=1, source_target_pairs={{0,2},{1,3},{2,0},{3,1},{4,6},{5,7},{6,4},{7,5},{8,10},{9,11},{10,... | collective-permute-start | bytes 208904 | tf_op jit(solution)/shard_map/ppermute | solution.py:767
  28.2 8.2 %collective-permute-start.17 = (bf16[272,128]{1,0:T(8,128)(2,1)S(1)}, bf16[272,128]{1,0:T(8,128)(2,1)S(1)}, u32[]{:S(2)}, u32[]{:S(2)}) collective-permute-start(bf16[272,128]{1,0:T(8,128)(2,1)S(1)} %get-tuple-element.245), channel_id=1, source_target_pairs={{0,3},{1,0},{2,1},{3,2},{4,7},{5,4},{6,5},{7,6},{8,11},{9,8},{10,9... | collective-permute-start | bytes 208904 | tf_op jit(solution)/shard_map/ppermute | solution.py:767
  36.5 8.1 %collective-permute-start.18 = (f32[168,128]{1,0:T(8,128)S(1)}, f32[168,128]{1,0:T(8,128)S(1)}, u32[]{:S(2)}, u32[]{:S(2)}) collective-permute-start(f32[168,128]{1,0:T(8,128)S(1)} %get-tuple-element.111), channel_id=1, source_target_pairs={{0,1},{1,2},{2,3},{3,4},{4,5},{5,6},{6,7},{7,8},{8,9},{9,10},{10,1... | collective-permute-start | bytes 258056 | tf_op jit(solution)/shard_map/ppermute | solution.py:651
  37.8 6.7 %collective-permute-start.19 = (f32[168,128]{1,0:T(8,128)S(1)}, f32[168,128]{1,0:T(8,128)S(1)}, u32[]{:S(2)}, u32[]{:S(2)}) collective-permute-start(f32[168,128]{1,0:T(8,128)S(1)} %get-tuple-element.112), channel_id=1, source_target_pairs={{1,0},{2,1},{3,2},{4,3},{5,4},{6,5},{7,6},{8,7},{9,8},{10,9},{11,1... | collective-permute-start | bytes 258056 | tf_op jit(solution)/shard_map/ppermute | solution.py:655
  41.9 1.2 %collective-permute-start.20 = (f32[72,128]{1,0:T(8,128)S(1)}, f32[72,128]{1,0:T(8,128)S(1)}, u32[]{:S(2)}, u32[]{:S(2)}) collective-permute-start(f32[72,128]{1,0:T(8,128)S(1)} %get-tuple-element.115.own), channel_id=1, source_target_pairs={{0,4},{4,0},{8,12},{12,8},{16,20},{20,16},{24,28},{28,24},{1,5},{5... | collective-permute-start | bytes 110600 | tf_op jit(solution)/shard_map/ppermute | solution.py:732
  48.1 12.3 %all-to-all-start = ((f32[32,1,128]{2,1,0:T(1,128)}), f32[32,1,128]{2,1,0:T(1,128)S(1)}, u32[]{:S(2)}, u32[]{:S(2)}) async-start(f32[32,1,128]{2,1,0:T(1,128)} %get-tuple-element.119), calls=%async_computation | async-start | bytes 32768 | tf_op jit(solution)/shard_map/all_to_all | solution.py:790

commit v6 on v5

--- a/solution.py
+++ b/solution.py
@@ -385,10 +385,10 @@
 
 
 def sums_kernel(count, place, *refs):
-    del place
+    even = place[0] % 2 == 0
     own, own_gram, multi, start = refs[:4]
     arrived = refs[4 : 4 + count]
-    hyper, gram, low, high = refs[4 + count :]
+    hyper, gram, first_pack, second_pack = refs[4 + count :]
     rows = hyper.shape[0]
     total = own[...].astype(jnp.float32)
     grams = own_gram[...].astype(jnp.float32)
@@ -399,15 +399,15 @@
     half = gram.shape[0]
     gram[...] = grams[:half, :] + grams[half:, :]
     first, second = DEC * RIM_MULTI, DEC * RIM_MULTI + RIM
-    for pack, top in ((low, True), (high, False)):
-        for source, begin, size in (
-            (multi, 0, first),
-            (hyper, first, RIM),
-            (start, second, DEC * RIM_START),
-        ):
-            rows = source.shape[0]
-            at = 0 if top else rows - size
-            pack[begin : begin + size, :] = source[at : at + size, :]
+    for source, begin, size in (
+        (multi, 0, first),
+        (hyper, first, RIM),
+        (start, second, DEC * RIM_START),
+    ):
+        low = source[:size, :]
+        high = source[source.shape[0] - size :, :]
+        first_pack[begin : begin + size, :] = jnp.where(even, high, low)
+        second_pack[begin : begin + size, :] = jnp.where(even, low, high)
 
 
 def add_sums(place, hyper_part, gram_part, multi, start, arrived):
@@ -442,9 +442,12 @@
 
 
 def basis_kernel(
-    devices, taps, multi, hyper, start, before, after, hyper_w, multi_w, bound, basis, products,
-    natural, lifted, held,
+    devices, place, taps, multi, hyper, start, first_rows, second_rows, hyper_w, multi_w, bound,
+    basis, products, natural, lifted, held,
 ):
+    even = place[0] % 2 == 0
+    before = jnp.where(even, second_rows[...], first_rows[...])
+    after = jnp.where(even, first_rows[...], second_rows[...])
     fine = multi.shape[0]
     coarse = fine // DEC
     wide = coarse + 2 * RIM
@@ -517,18 +520,20 @@
         products[device] = block
 
 
-def make_basis(devices, taps, multi, hyper, start, before, after, hyper_w, multi_w, bound):
+def make_basis(
+    devices, place, taps, multi, hyper, start, first_rows, second_rows, hyper_w, multi_w, bound
+):
     fine, rank = multi.shape
     coarse = fine // DEC
     wide = coarse + 2 * RIM
-    arrays = (multi, hyper, start, before, after, hyper_w, multi_w, bound)
+    arrays = (multi, hyper, start, first_rows, second_rows, hyper_w, multi_w, bound)
     outs = [
         jax.ShapeDtypeStruct((ITERS + 2, DEC, coarse, rank), jnp.float32),
         pltpu.VMEM((devices, 1, rank), jnp.float32),
     ]
     return pl.pallas_call(
         functools.partial(basis_kernel, devices),
-        in_specs=[SMEM] + [whole(a.shape) for a in arrays],
+        in_specs=[SMEM, SMEM] + [whole(a.shape) for a in arrays],
         out_specs=[whole(o.shape) for o in outs],
         out_shape=outs,
         scratch_shapes=[
@@ -538,7 +543,7 @@
         ],
         compiler_params=params(),
         name="make_basis",
-    )(taps, *arrays)
+    )(place, taps, *arrays)
 
 
 def coefficients_kernel(products, bound, out, trusted):
@@ -776,16 +781,19 @@
     multi, band_gram, merged_gram = sum_arrived(
         place[None], band_factor, response, multi_part, multi_arrived
     )
-    hyper, gram, low, high = add_sums(
+    hyper, gram, first_pack, second_pack = add_sums(
         place[None], hyper_part, gram_part, multi, row_start, hyper_arrived
     )
     hyper_gram, multi_gram, hyper_w, multi_w, bound = make_operator(
         row, taps, band_gram, merged_gram, gram, exchanged(gram, 1)
     )
-    before_rows = to_next(high, BOTH, devices)
-    after_rows = to_previous(low, BOTH, devices)
+    first_rows = lax.ppermute(first_pack, BOTH, [(i, i ^ 1) for i in range(devices)])
+    second_rows = lax.ppermute(
+        second_pack, BOTH, [((i + 1) % devices, ((i ^ 1) + 1) % devices) for i in range(devices)]
+    )
     basis, products = make_basis(
-        devices, taps, multi, hyper, row_start, before_rows, after_rows, hyper_w, multi_w, bound
+        devices, place[None], taps, multi, hyper, row_start, first_rows, second_rows, hyper_w,
+        multi_w, bound,
     )
     products = lax.all_to_all(products, BOTH, 0, 0, tiled=True)
     coefficients, trusted = make_coefficients(products, bound)

time: 62.1 us -> 60.3 us (0.971)
  starting transfers between devices: 28 us -> 22.5 us
  waiting for transfers between devices: 14 us -> 17.8 us
    ppermute x2 -> x1, starting transfers between devices: 6.34 us -> 2.3 us  [to_previous(): lax.ppermute(values, axis, [((i + 1) % count, i) for i in range(count)])]
    ppermute x0 -> x2, waiting for transfers between devices: none -> 3.8 us  [the longest x1 3.79 us: body(): lax.ppermute(second_pack, BOTH, [((i + 1) % devices, ((i ^ 1) + 1) % devi...]
    all_to_all x1, starting transfers between devices: 5.21 us -> 2.54 us  [body(): products = lax.all_to_all(products, BOTH, 0, 0, tiled=True)]
    ppermute x0 -> x2, starting transfers between devices: none -> 2.48 us  [the longest x1 1.37 us: body(): lax.ppermute(first_pack, BOTH, [(i, i ^ 1) for i in range(devices)])]
    ppermute x2 -> x1, starting transfers between devices: 2.99 us -> 1.63 us  [to_next(): lax.ppermute(values, axis, [(i, (i + 1) % count) for i in range(count)])]
  transfers between devices with their start and end apart: 16 -> 16, of which waited for: 5 -> 6; matrix products, arithmetic and copies ran while one was open for 3% -> 3% of each run, Pallas kernels for 20% -> 20%
where the time goes in v6:
time: 60.3 us; the launch traced here: 60 us
  starting transfers between devices  22.5 us (37%)
  waiting for transfers between devices  17.8 us (30%)
  Pallas kernels  16.9 us (28%)
  local copies, waits for them, and re-layouts  1.09 us (2%)
  between operations  0.81 us (1%)
  other arithmetic  0.8 us (1%)
    ppermute x6, starting transfers between devices, exchange(): lax.ppermute(piece, 'col', [(i, (i + distance) % across) for i in range(a...  8.87 us
    all_to_all x1, waiting for transfers between devices, body(): products = lax.all_to_all(products, BOTH, 0, 0, tiled=True)  7.1 us
    ppermute x6, waiting for transfers between devices, exchange(): lax.ppermute(piece, 'col', [(i, (i + distance) % across) for i in range(a...  4.84 us
    ppermute x5, starting transfers between devices, exchanged(): lax.ppermute(values, 'row', [(i, i ^ distance) for i in range(along)])  4.64 us
    pallas_call x1, Pallas kernels, contract_hyper(): pl.pallas_call(functools.partial(hyper_kernel, share), in_specs=[SMEM, SM...  4.61 us
    ppermute x1, waiting for transfers between devices, body(): lax.ppermute(second_pack, BOTH, [((i + 1) % devices, ((i ^ 1) + 1) % devi...  3.79 us
    pallas_call x1, Pallas kernels, load(): pl.pallas_call(functools.partial(load_kernel, ranges), in_specs=[pl.Block...  3.74 us
    pallas_call x1, Pallas kernels, make_basis(): pl.pallas_call(functools.partial(basis_kernel, devices), in_specs=[SMEM,...  3.49 us
  transfers between devices with their start and end apart: 16, of which 6 were waited for; matrix products, arithmetic and copies ran while one was open for 3% of the time, Pallas kernels for 20%

profile of v6, /device:TPU:0, one launch (start us, length us, event | category | flops | bytes accessed | tf_op | source)
XLA Modules:
  0.0 60.0 jit_solution(8677238001017786447)
XLA Ops:
  0.6 0.5 collective-permute-start.6
  1.2 0.8 %select_reduce_fusion.taps = f32[17]{0:T(128)S(1)} fusion(f32[9]{0:T(128)} %param.18, s32[17]{0:T(128)S(1)} %iota_add_fusion, s32[9]{0:T(128)} %param.19), kind=kLoop, calls=%fused_computation.155 | loop fusion | flops 442 | bytes 208 | tf_op jit(solution)/shard_map/reduce_sum | solution.py:761
  2.0 0.7 %concatenate.36 = bf16[32,512]{1,0:T(8,128)(2,1)S(1)} pad(bf16[16,512]{1,0:T(8,128)(2,1)} %bitcast.165, bf16[]{:T(256)} %constant.54.clone.1), padding=0_16x0_0 | pad | bytes 49154 | tf_op jit(solution)/shard_map/concatenate | solution.py:741
  2.7 2.6 %collective-permute-start.7 = (bf16[32,512]{1,0:T(8,128)(2,1)S(1)}, bf16[32,512]{1,0:T(8,128)(2,1)S(1)}, u32[]{:S(2)}, u32[]{:S(2)}) collective-permute-start(bf16[32,512]{1,0:T(8,128)(2,1)S(1)} %pad_maximum_fusion.10.refs_0_), channel_id=1, source_target_pairs={{0,8},{4,12},{8,0},{12,4},{16,24},{20,28},{24,16},{28,20},{1,9},{5... | collective-permute-start | bytes 98312 | tf_op jit(solution)/shard_map/ppermute | solution.py:737
  5.3 1.5 %collective-permute-start.8 = (bf16[32,512]{1,0:T(8,128)(2,1)S(1)}, bf16[32,512]{1,0:T(8,128)(2,1)S(1)}, u32[]{:S(2)}, u32[]{:S(2)}) collective-permute-start(bf16[32,512]{1,0:T(8,128)(2,1)S(1)} %pad_maximum_fusion.10.refs_0_), channel_id=1, source_target_pairs={{0,16},{4,20},{8,24},{12,28},{16,0},{20,4},{24,8},{28,12},{1,17},{... | collective-permute-start | bytes 98312 | tf_op jit(solution)/shard_map/ppermute | solution.py:737
  6.8 0.1 fusion.117
  6.9 3.7 %load.1 = (bf16[2,2048,512]{2,1,0:T(8,128)(2,1)S(1)}, f32[96,128]{1,0:T(8,128)S(1)}, f32[2,96]{1,0:T(2,128)S(1)}, f32[512,128]{1,0:T(8,128)S(1)}, bf16[56,512,128]{2,1,0:T(8,128)(2,1)S(1)}) custom-call(bf16[2,2048,512]{2,1,0:T(8,128)(2,1)} %refs_0_, f32[96,128]{1,0:T(8,128)} %refs_1_.1, f32[2,96]{1,0:T(2,128)} %refs_2_.1, f32[512,128]{1,0:T(8,128)} %refs_3_.1, ...), custom_call_target="tpu_custom_call" | custom-call | bytes 23692800 | tf_op jit(solution)/shard_map/load/pallas_call | solution.py:80
  10.6 0.1 fusion.118
  10.8 0.8 %collective-permute-done.9.refs_3_ = bf16[32,512]{1,0:T(8,128)(2,1)S(1)} collective-permute-done((bf16[32,512]{1,0:T(8,128)(2,1)S(1)}, bf16[32,512]{1,0:T(8,128)(2,1)S(1)}, u32[]{:S(2)}, u32[]{:S(2)}) %collective-permute-start.9) | collective-permute-done | bytes 32800 | tf_op jit(solution)/shard_map/ppermute | solution.py:737
  11.7 1.6 %collective-permute-start.13 = (bf16[128,16]{1,0:T(8,128)(2,1)S(1)}, bf16[128,16]{1,0:T(8,128)(2,1)S(1)}, u32[]{:S(2)}, u32[]{:S(2)}) collective-permute-start(bf16[128,16]{1,0:T(8,128)(2,1)S(1)} %pad_maximum_fusion.11), channel_id=1, source_target_pairs={{0,1},{1,2},{2,3},{3,0},{4,5},{5,6},{6,7},{7,4},{8,9},{9,10},{10,1... | collective-permute-start | bytes 12296 | tf_op jit(solution)/shard_map/ppermute | solution.py:656
  13.3 2.3 %collective-permute-start.14 = (bf16[128,16]{1,0:T(8,128)(2,1)S(1)}, bf16[128,16]{1,0:T(8,128)(2,1)S(1)}, u32[]{:S(2)}, u32[]{:S(2)}) collective-permute-start(bf16[128,16]{1,0:T(8,128)(2,1)S(1)} %pad_maximum_fusion.12), channel_id=1, source_target_pairs={{1,0},{2,1},{3,2},{0,3},{5,4},{6,5},{7,6},{4,7},{9,8},{10,9},{11,1... | collective-permute-start | bytes 12296 | tf_op jit(solution)/shard_map/ppermute | solution.py:660
  15.6 1.8 %contract_multi.1 = (bf16[2048,128]{1,0:T(8,128)(2,1)S(1)}, f32[512,128]{1,0:T(8,128)S(1)}, bf16[56,512,128]{2,1,0:T(8,128)(2,1)S(1)}) custom-call(s32[1]{0:T(128)} %bitcast.62.place, f32[96,128]{1,0:T(8,128)S(1)} %get-tuple-element.98.band, f32[2,96]{1,0:T(2,128)S(1)} %get-tuple-element.99.response, ...), custom_call_target="tpu_custom_call", output_to_operand_aliasing={{2}: (5, {})} | custom-call | flops 536870912 | bytes 8388608 | tf_op jit(solution)/shard_map/contract_multi/pallas_call | solution.py:142
  17.5 2.4 %collective-permute-start.11 = (bf16[512,128]{1,0:T(8,128)(2,1)S(1)}, bf16[512,128]{1,0:T(8,128)(2,1)S(1)}, u32[]{:S(2)}, u32[]{:S(2)}) collective-permute-start(bf16[512,128]{1,0:T(8,128)(2,1)S(1)} %get-tuple-element.240), channel_id=1, source_target_pairs={{0,2},{1,3},{2,0},{3,1},{4,6},{5,7},{6,4},{7,5},{8,10},{9,11},{10,... | collective-permute-start | bytes 393224 | tf_op jit(solution)/shard_map/ppermute | solution.py:772
  19.9 1.5 %collective-permute-start.12 = (bf16[512,128]{1,0:T(8,128)(2,1)S(1)}, bf16[512,128]{1,0:T(8,128)(2,1)S(1)}, u32[]{:S(2)}, u32[]{:S(2)}) collective-permute-start(bf16[512,128]{1,0:T(8,128)(2,1)S(1)} %get-tuple-element.239), channel_id=1, source_target_pairs={{0,3},{1,0},{2,1},{3,2},{4,7},{5,4},{6,5},{7,6},{8,11},{9,8},{10,9... | collective-permute-start | bytes 393224 | tf_op jit(solution)/shard_map/ppermute | solution.py:772
  21.3 4.6 %contract_hyper.1 = (bf16[512,128]{1,0:T(8,128)(2,1)S(1)}, bf16[144,128]{1,0:T(8,128)(2,1)S(1)}) custom-call(s32[1]{0:T(128)} %bitcast.62.place, f32[17]{0:T(128)S(1)} %select_reduce_fusion.taps, f32[512,128]{1,0:T(8,128)S(1)} %get-tuple-element.105.columns, bf16[128,16]{1,0:T(8,128)(2,1)S(1)} %collective-permute-done.13.before, ...), custom_call_target="tpu_custom_call" | custom-call | tf_op jit(solution)/shard_map/contract_hyper/pallas_call | solution.py:227
  26.0 0.6 %collective-permute-start.15 = (bf16[272,128]{1,0:T(8,128)(2,1)S(1)}, bf16[272,128]{1,0:T(8,128)(2,1)S(1)}, u32[]{:S(2)}, u32[]{:S(2)}) collective-permute-start(bf16[272,128]{1,0:T(8,128)(2,1)S(1)} %get-tuple-element.247), channel_id=1, source_target_pairs={{0,1},{1,2},{2,3},{3,0},{4,5},{5,6},{6,7},{7,4},{8,9},{9,10},{10,1... | collective-permute-start | bytes 208904 | tf_op jit(solution)/shard_map/ppermute | solution.py:772
  26.6 1.5 %collective-permute-start.16 = (bf16[272,128]{1,0:T(8,128)(2,1)S(1)}, bf16[272,128]{1,0:T(8,128)(2,1)S(1)}, u32[]{:S(2)}, u32[]{:S(2)}) collective-permute-start(bf16[272,128]{1,0:T(8,128)(2,1)S(1)} %get-tuple-element.246), channel_id=1, source_target_pairs={{0,2},{1,3},{2,0},{3,1},{4,6},{5,7},{6,4},{7,5},{8,10},{9,11},{10,... | collective-permute-start | bytes 208904 | tf_op jit(solution)/shard_map/ppermute | solution.py:772
  28.2 2.8 %collective-permute-start.17 = (bf16[272,128]{1,0:T(8,128)(2,1)S(1)}, bf16[272,128]{1,0:T(8,128)(2,1)S(1)}, u32[]{:S(2)}, u32[]{:S(2)}) collective-permute-start(bf16[272,128]{1,0:T(8,128)(2,1)S(1)} %get-tuple-element.245), channel_id=1, source_target_pairs={{0,3},{1,0},{2,1},{3,2},{4,7},{5,4},{6,5},{7,6},{8,11},{9,8},{10,9... | collective-permute-start | bytes 208904 | tf_op jit(solution)/shard_map/ppermute | solution.py:772
  31.0 0.5 sum_arrived.1
  31.6 0.8 %collective-permute-done.15.refs_4_ = bf16[272,128]{1,0:T(8,128)(2,1)S(1)} collective-permute-done((bf16[272,128]{1,0:T(8,128)(2,1)S(1)}, bf16[272,128]{1,0:T(8,128)(2,1)S(1)}, u32[]{:S(2)}, u32[]{:S(2)}) %collective-permute-start.15) | collective-permute-done | bytes 69664 | tf_op jit(solution)/shard_map/ppermute | solution.py:772
  32.4 4.0 %collective-permute-done.16.refs_5_ = bf16[272,128]{1,0:T(8,128)(2,1)S(1)} collective-permute-done((bf16[272,128]{1,0:T(8,128)(2,1)S(1)}, bf16[272,128]{1,0:T(8,128)(2,1)S(1)}, u32[]{:S(2)}, u32[]{:S(2)}) %collective-permute-start.16) | collective-permute-done | bytes 69664 | tf_op jit(solution)/shard_map/ppermute | solution.py:772
  36.5 1.4 %collective-permute-start.18 = (f32[168,128]{1,0:T(8,128)S(1)}, f32[168,128]{1,0:T(8,128)S(1)}, u32[]{:S(2)}, u32[]{:S(2)}) collective-permute-start(f32[168,128]{1,0:T(8,128)S(1)} %get-tuple-element.111), channel_id=1, source_target_pairs={{0,1},{1,0},{2,3},{3,2},{4,5},{5,4},{6,7},{7,6},{8,9},{9,8},{10,11... | collective-permute-start | bytes 258056 | tf_op jit(solution)/shard_map/ppermute | solution.py:790
  37.8 1.1 %collective-permute-start.19 = (f32[168,128]{1,0:T(8,128)S(1)}, f32[168,128]{1,0:T(8,128)S(1)}, u32[]{:S(2)}, u32[]{:S(2)}) collective-permute-start(f32[168,128]{1,0:T(8,128)S(1)} %get-tuple-element.112), channel_id=1, source_target_pairs={{1,2},{2,1},{3,4},{4,3},{5,6},{6,5},{7,8},{8,7},{9,10},{10,9},{11,... | collective-permute-start | bytes 258056 | tf_op jit(solution)/shard_map/ppermute | solution.py:791
  39.0 1.2 %collective-permute-done.20.other = f32[72,128]{1,0:T(8,128)S(1)} collective-permute-done((f32[72,128]{1,0:T(8,128)S(1)}, f32[72,128]{1,0:T(8,128)S(1)}, u32[]{:S(2)}, u32[]{:S(2)}) %collective-permute-start.20) | collective-permute-done | bytes 36896 | tf_op jit(solution)/shard_map/ppermute | solution.py:737
  40.2 1.4 %make_operator.1 = (f32[128,128]{1,0:T(8,128)S(1)}, f32[128,128]{1,0:T(8,128)S(1)}, bf16[256,256]{1,0:T(8,128)(2,1)S(1)}, bf16[256,256]{1,0:T(8,128)(2,1)S(1)}, f32[8,128]{1,0:T(8,128)S(1)}) custom-call(s32[1]{0:T(128)} %bitcast.62.place, f32[17]{0:T(128)S(1)} %select_reduce_fusion.taps, f32[128,128]{1,0:T(8,128)S(1)} %get-tuple-element.113.band_gram, ...), custom_call_target="tpu_custom_call" | custom-call | bytes 67108864 | tf_op jit(solution)/shard_map/make_operator/pallas_call | solution.py:304
  41.6 3.8 %collective-permute-done.19.second_rows = f32[168,128]{1,0:T(8,128)S(1)} collective-permute-done((f32[168,128]{1,0:T(8,128)S(1)}, f32[168,128]{1,0:T(8,128)S(1)}, u32[]{:S(2)}, u32[]{:S(2)}) %collective-permute-start.19) | collective-permute-done | bytes 86048 | tf_op jit(solution)/shard_map/ppermute | solution.py:791
  45.4 3.5 %make_basis.1 = (f32[6,4,128,128]{3,2,1,0:T(8,128)S(1)}, f32[32,1,128]{2,1,0:T(1,128)}) custom-call(s32[1]{0:T(128)} %bitcast.60.place, f32[17]{0:T(128)S(1)} %select_reduce_fusion.taps, f32[512,128]{1,0:T(8,128)S(1)} %get-tuple-element.104.refs_2_.multi, f32[128,128]{1,0:T(8,128)S(1)} %get-tuple-element.110.hyper, ...), custom_call_target="tpu_custom_call" | custom-call | tf_op jit(solution)/shard_map/make_basis/pallas_call | solution.py:534
  48.9 2.5 %all-to-all-start = ((f32[32,1,128]{2,1,0:T(1,128)}), f32[32,1,128]{2,1,0:T(1,128)S(1)}, u32[]{:S(2)}, u32[]{:S(2)}) async-start(f32[32,1,128]{2,1,0:T(1,128)} %get-tuple-element.119), calls=%async_computation | async-start | bytes 32768 | tf_op jit(solution)/shard_map/all_to_all | solution.py:798
  51.4 7.1 %all-to-all-done.products = f32[32,1,128]{2,1,0:T(1,128)S(1)} async-done(((f32[32,1,128]{2,1,0:T(1,128)}), f32[32,1,128]{2,1,0:T(1,128)S(1)}, u32[]{:S(2)}, u32[]{:S(2)}) %all-to-all-start) | async-done | bytes 16416 | tf_op jit(solution)/shard_map/all_to_all | solution.py:798
  58.5 0.3 make_coefficients.1
  58.9 1.2 %conditional.1 = ((f32[512,128]{1,0:T(8,128)}, f32[512,128]{1,0:T(8,128)})) conditional(s32[]{:T(128)} %bitcast.63, (f32[6,4,128,128]{3,2,1,0:T(8,128)S(1)}, f32[17]{0:T(128)S(1)}, f32[128,128]{1,0:T(8,128)S(1)}, f32[512,128]{1,0:T(8,128)S(1)}, f32[128,128]{1,0:T(8,128)S(1)}, /*index=5*/f32[128,128]{1,0:T(8,128)S(1)}) %tuple.20, ...), branch_computations={%region_1.10_spmd, %region_10.11_spmd} | conditional | flops 257967104 | bytes 23068832 | solution.py:805
  59.1 0.9 %combine.1 = (f32[512,128]{1,0:T(8,128)}, f32[512,128]{1,0:T(8,128)}) custom-call(f32[16,128]{1,0:T(8,128)S(1)} %get-tuple-element.65.coefficients, f32[6,4,128,128]{3,2,1,0:T(8,128)S(1)} %get-tuple-element.66.basis), custom_call_target="tpu_custom_call" | custom-call | tf_op jit(solution)/shard_map/cond/branch_1_fun/combine/pallas_call | solution.py:645
  (24 shorter events, 0.4 us)
Async XLA Ops:
  0.6 2.1 %collective-permute-start.6 = (bf16[16,512]{1,0:T(8,128)(2,1)}, bf16[16,512]{1,0:T(8,128)(2,1)S(1)}, u32[]{:S(2)}, u32[]{:S(2)}) collective-permute-start(bf16[16,512]{1,0:T(8,128)(2,1)} %bitcast.164), channel_id=1, source_target_pairs={{0,4},{4,0},{8,12},{12,8},{16,20},{20,16},{24,28},{28,24},{1,5},{5... | collective-permute-start | bytes 49160 | tf_op jit(solution)/shard_map/ppermute | solution.py:737
  2.7 7.9 %collective-permute-start.7 = (bf16[32,512]{1,0:T(8,128)(2,1)S(1)}, bf16[32,512]{1,0:T(8,128)(2,1)S(1)}, u32[]{:S(2)}, u32[]{:S(2)}) collective-permute-start(bf16[32,512]{1,0:T(8,128)(2,1)S(1)} %pad_maximum_fusion.10.refs_0_), channel_id=1, source_target_pairs={{0,8},{4,12},{8,0},{12,4},{16,24},{20,28},{24,16},{28,20},{1,9},{5... | collective-permute-start | bytes 98312 | tf_op jit(solution)/shard_map/ppermute | solution.py:737
  5.3 5.5 %collective-permute-start.8 = (bf16[32,512]{1,0:T(8,128)(2,1)S(1)}, bf16[32,512]{1,0:T(8,128)(2,1)S(1)}, u32[]{:S(2)}, u32[]{:S(2)}) collective-permute-start(bf16[32,512]{1,0:T(8,128)(2,1)S(1)} %pad_maximum_fusion.10.refs_0_), channel_id=1, source_target_pairs={{0,16},{4,20},{8,24},{12,28},{16,0},{20,4},{24,8},{28,12},{1,17},{... | collective-permute-start | bytes 98312 | tf_op jit(solution)/shard_map/ppermute | solution.py:737
  6.8 4.8 %collective-permute-start.9 = (bf16[32,512]{1,0:T(8,128)(2,1)S(1)}, bf16[32,512]{1,0:T(8,128)(2,1)S(1)}, u32[]{:S(2)}, u32[]{:S(2)}) collective-permute-start(bf16[32,512]{1,0:T(8,128)(2,1)S(1)} %pad_maximum_fusion.10.refs_0_), channel_id=1, source_target_pairs={{0,24},{4,28},{8,16},{12,20},{16,8},{20,12},{24,0},{28,4},{1,25},{... | collective-permute-start | bytes 98312 | tf_op jit(solution)/shard_map/ppermute | solution.py:737
  11.7 9.6 %collective-permute-start.13 = (bf16[128,16]{1,0:T(8,128)(2,1)S(1)}, bf16[128,16]{1,0:T(8,128)(2,1)S(1)}, u32[]{:S(2)}, u32[]{:S(2)}) collective-permute-start(bf16[128,16]{1,0:T(8,128)(2,1)S(1)} %pad_maximum_fusion.11), channel_id=1, source_target_pairs={{0,1},{1,2},{2,3},{3,0},{4,5},{5,6},{6,7},{7,4},{8,9},{9,10},{10,1... | collective-permute-start | bytes 12296 | tf_op jit(solution)/shard_map/ppermute | solution.py:656
  13.3 8.0 %collective-permute-start.14 = (bf16[128,16]{1,0:T(8,128)(2,1)S(1)}, bf16[128,16]{1,0:T(8,128)(2,1)S(1)}, u32[]{:S(2)}, u32[]{:S(2)}) collective-permute-start(bf16[128,16]{1,0:T(8,128)(2,1)S(1)} %pad_maximum_fusion.12), channel_id=1, source_target_pairs={{1,0},{2,1},{3,2},{0,3},{5,4},{6,5},{7,6},{4,7},{9,8},{10,9},{11,1... | collective-permute-start | bytes 12296 | tf_op jit(solution)/shard_map/ppermute | solution.py:660
  17.5 10.7 %collective-permute-start.10 = (bf16[512,128]{1,0:T(8,128)(2,1)S(1)}, bf16[512,128]{1,0:T(8,128)(2,1)S(1)}, u32[]{:S(2)}, u32[]{:S(2)}) collective-permute-start(bf16[512,128]{1,0:T(8,128)(2,1)S(1)} %get-tuple-element.241), channel_id=1, source_target_pairs={{0,1},{1,2},{2,3},{3,0},{4,5},{5,6},{6,7},{7,4},{8,9},{9,10},{10,1... | collective-permute-start | bytes 393224 | tf_op jit(solution)/shard_map/ppermute | solution.py:772
  17.5 13.5 %collective-permute-start.11 = (bf16[512,128]{1,0:T(8,128)(2,1)S(1)}, bf16[512,128]{1,0:T(8,128)(2,1)S(1)}, u32[]{:S(2)}, u32[]{:S(2)}) collective-permute-start(bf16[512,128]{1,0:T(8,128)(2,1)S(1)} %get-tuple-element.240), channel_id=1, source_target_pairs={{0,2},{1,3},{2,0},{3,1},{4,6},{5,7},{6,4},{7,5},{8,10},{9,11},{10,... | collective-permute-start | bytes 393224 | tf_op jit(solution)/shard_map/ppermute | solution.py:772
  19.9 11.1 %collective-permute-start.12 = (bf16[512,128]{1,0:T(8,128)(2,1)S(1)}, bf16[512,128]{1,0:T(8,128)(2,1)S(1)}, u32[]{:S(2)}, u32[]{:S(2)}) collective-permute-start(bf16[512,128]{1,0:T(8,128)(2,1)S(1)} %get-tuple-element.239), channel_id=1, source_target_pairs={{0,3},{1,0},{2,1},{3,2},{4,7},{5,4},{6,5},{7,6},{8,11},{9,8},{10,9... | collective-permute-start | bytes 393224 | tf_op jit(solution)/shard_map/ppermute | solution.py:772
  26.0 6.3 %collective-permute-start.15 = (bf16[272,128]{1,0:T(8,128)(2,1)S(1)}, bf16[272,128]{1,0:T(8,128)(2,1)S(1)}, u32[]{:S(2)}, u32[]{:S(2)}) collective-permute-start(bf16[272,128]{1,0:T(8,128)(2,1)S(1)} %get-tuple-element.247), channel_id=1, source_target_pairs={{0,1},{1,2},{2,3},{3,0},{4,5},{5,6},{6,7},{7,4},{8,9},{9,10},{10,1... | collective-permute-start | bytes 208904 | tf_op jit(solution)/shard_map/ppermute | solution.py:772
  26.6 9.8 %collective-permute-start.16 = (bf16[272,128]{1,0:T(8,128)(2,1)S(1)}, bf16[272,128]{1,0:T(8,128)(2,1)S(1)}, u32[]{:S(2)}, u32[]{:S(2)}) collective-permute-start(bf16[272,128]{1,0:T(8,128)(2,1)S(1)} %get-tuple-element.246), channel_id=1, source_target_pairs={{0,2},{1,3},{2,0},{3,1},{4,6},{5,7},{6,4},{7,5},{8,10},{9,11},{10,... | collective-permute-start | bytes 208904 | tf_op jit(solution)/shard_map/ppermute | solution.py:772
  28.2 8.2 %collective-permute-start.17 = (bf16[272,128]{1,0:T(8,128)(2,1)S(1)}, bf16[272,128]{1,0:T(8,128)(2,1)S(1)}, u32[]{:S(2)}, u32[]{:S(2)}) collective-permute-start(bf16[272,128]{1,0:T(8,128)(2,1)S(1)} %get-tuple-element.245), channel_id=1, source_target_pairs={{0,3},{1,0},{2,1},{3,2},{4,7},{5,4},{6,5},{7,6},{8,11},{9,8},{10,9... | collective-permute-start | bytes 208904 | tf_op jit(solution)/shard_map/ppermute | solution.py:772
  36.5 5.1 %collective-permute-start.18 = (f32[168,128]{1,0:T(8,128)S(1)}, f32[168,128]{1,0:T(8,128)S(1)}, u32[]{:S(2)}, u32[]{:S(2)}) collective-permute-start(f32[168,128]{1,0:T(8,128)S(1)} %get-tuple-element.111), channel_id=1, source_target_pairs={{0,1},{1,0},{2,3},{3,2},{4,5},{5,4},{6,7},{7,6},{8,9},{9,8},{10,11... | collective-permute-start | bytes 258056 | tf_op jit(solution)/shard_map/ppermute | solution.py:790
  37.8 7.6 %collective-permute-start.19 = (f32[168,128]{1,0:T(8,128)S(1)}, f32[168,128]{1,0:T(8,128)S(1)}, u32[]{:S(2)}, u32[]{:S(2)}) collective-permute-start(f32[168,128]{1,0:T(8,128)S(1)} %get-tuple-element.112), channel_id=1, source_target_pairs={{1,2},{2,1},{3,4},{4,3},{5,6},{6,5},{7,8},{8,7},{9,10},{10,9},{11,... | collective-permute-start | bytes 258056 | tf_op jit(solution)/shard_map/ppermute | solution.py:791
  38.9 1.2 %collective-permute-start.20 = (f32[72,128]{1,0:T(8,128)S(1)}, f32[72,128]{1,0:T(8,128)S(1)}, u32[]{:S(2)}, u32[]{:S(2)}) collective-permute-start(f32[72,128]{1,0:T(8,128)S(1)} %get-tuple-element.115.own), channel_id=1, source_target_pairs={{0,4},{4,0},{8,12},{12,8},{16,20},{20,16},{24,28},{28,24},{1,5},{5... | collective-permute-start | bytes 110600 | tf_op jit(solution)/shard_map/ppermute | solution.py:737
  48.9 9.6 %all-to-all-start = ((f32[32,1,128]{2,1,0:T(1,128)}), f32[32,1,128]{2,1,0:T(1,128)S(1)}, u32[]{:S(2)}, u32[]{:S(2)}) async-start(f32[32,1,128]{2,1,0:T(1,128)} %get-tuple-element.119), calls=%async_computation | async-start | bytes 32768 | tf_op jit(solution)/shard_map/all_to_all | solution.py:798

commit v7 on v6

--- a/solution.py
+++ b/solution.py
@@ -787,10 +787,10 @@
     hyper_gram, multi_gram, hyper_w, multi_w, bound = make_operator(
         row, taps, band_gram, merged_gram, gram, exchanged(gram, 1)
     )
-    first_rows = lax.ppermute(first_pack, BOTH, [(i, i ^ 1) for i in range(devices)])
     second_rows = lax.ppermute(
         second_pack, BOTH, [((i + 1) % devices, ((i ^ 1) + 1) % devices) for i in range(devices)]
     )
+    first_rows = lax.ppermute(first_pack, BOTH, [(i, i ^ 1) for i in range(devices)])
     basis, products = make_basis(
         devices, place[None], taps, multi, hyper, row_start, first_rows, second_rows, hyper_w,
         multi_w, bound,

time: 60.3 us -> 60.3 us (level)
  no operation moved by 1% of the time
where the time goes in v7:
time: 60.3 us; the launch traced here: 60 us
  starting transfers between devices  22.5 us (37%)
  waiting for transfers between devices  17.8 us (30%)
  Pallas kernels  16.9 us (28%)
  local copies, waits for them, and re-layouts  1.09 us (2%)
  between operations  0.81 us (1%)
  other arithmetic  0.8 us (1%)
    ppermute x6, starting transfers between devices, exchange(): lax.ppermute(piece, 'col', [(i, (i + distance) % across) for i in range(a...  8.87 us
    all_to_all x1, waiting for transfers between devices, body(): products = lax.all_to_all(products, BOTH, 0, 0, tiled=True)  7.1 us
    ppermute x6, waiting for transfers between devices, exchange(): lax.ppermute(piece, 'col', [(i, (i + distance) % across) for i in range(a...  4.84 us
    ppermute x5, starting transfers between devices, exchanged(): lax.ppermute(values, 'row', [(i, i ^ distance) for i in range(along)])  4.64 us
    pallas_call x1, Pallas kernels, contract_hyper(): pl.pallas_call(functools.partial(hyper_kernel, share), in_specs=[SMEM, SM...  4.61 us
    ppermute x1, waiting for transfers between devices, body(): lax.ppermute(second_pack, BOTH, [((i + 1) % devices, ((i ^ 1) + 1) % devi...  3.79 us
    pallas_call x1, Pallas kernels, load(): pl.pallas_call(functools.partial(load_kernel, ranges), in_specs=[pl.Block...  3.74 us
    pallas_call x1, Pallas kernels, make_basis(): pl.pallas_call(functools.partial(basis_kernel, devices), in_specs=[SMEM,...  3.49 us
  transfers between devices with their start and end apart: 16, of which 6 were waited for; matrix products, arithmetic and copies ran while one was open for 3% of the time, Pallas kernels for 20%

profile of v7, /device:TPU:0, one launch (start us, length us, event | category | flops | bytes accessed | tf_op | source)
XLA Modules:
  0.0 60.0 jit_solution(8677238001017786447)
XLA Ops:
  0.6 0.5 collective-permute-start.6
  1.2 0.8 %select_reduce_fusion.taps = f32[17]{0:T(128)S(1)} fusion(f32[9]{0:T(128)} %param.18, s32[17]{0:T(128)S(1)} %iota_add_fusion, s32[9]{0:T(128)} %param.19), kind=kLoop, calls=%fused_computation.155 | loop fusion | flops 442 | bytes 208 | tf_op jit(solution)/shard_map/reduce_sum | solution.py:761
  2.0 0.7 %concatenate.36 = bf16[32,512]{1,0:T(8,128)(2,1)S(1)} pad(bf16[16,512]{1,0:T(8,128)(2,1)} %bitcast.165, bf16[]{:T(256)} %constant.54.clone.1), padding=0_16x0_0 | pad | bytes 49154 | tf_op jit(solution)/shard_map/concatenate | solution.py:741
  2.7 2.6 %collective-permute-start.7 = (bf16[32,512]{1,0:T(8,128)(2,1)S(1)}, bf16[32,512]{1,0:T(8,128)(2,1)S(1)}, u32[]{:S(2)}, u32[]{:S(2)}) collective-permute-start(bf16[32,512]{1,0:T(8,128)(2,1)S(1)} %pad_maximum_fusion.10.refs_0_), channel_id=1, source_target_pairs={{0,8},{4,12},{8,0},{12,4},{16,24},{20,28},{24,16},{28,20},{1,9},{5... | collective-permute-start | bytes 98312 | tf_op jit(solution)/shard_map/ppermute | solution.py:737
  5.3 1.5 %collective-permute-start.8 = (bf16[32,512]{1,0:T(8,128)(2,1)S(1)}, bf16[32,512]{1,0:T(8,128)(2,1)S(1)}, u32[]{:S(2)}, u32[]{:S(2)}) collective-permute-start(bf16[32,512]{1,0:T(8,128)(2,1)S(1)} %pad_maximum_fusion.10.refs_0_), channel_id=1, source_target_pairs={{0,16},{4,20},{8,24},{12,28},{16,0},{20,4},{24,8},{28,12},{1,17},{... | collective-permute-start | bytes 98312 | tf_op jit(solution)/shard_map/ppermute | solution.py:737
  6.8 0.1 fusion.117
  6.9 3.7 %load.1 = (bf16[2,2048,512]{2,1,0:T(8,128)(2,1)S(1)}, f32[96,128]{1,0:T(8,128)S(1)}, f32[2,96]{1,0:T(2,128)S(1)}, f32[512,128]{1,0:T(8,128)S(1)}, bf16[56,512,128]{2,1,0:T(8,128)(2,1)S(1)}) custom-call(bf16[2,2048,512]{2,1,0:T(8,128)(2,1)} %refs_0_, f32[96,128]{1,0:T(8,128)} %refs_1_.1, f32[2,96]{1,0:T(2,128)} %refs_2_.1, f32[512,128]{1,0:T(8,128)} %refs_3_.1, ...), custom_call_target="tpu_custom_call" | custom-call | bytes 23692800 | tf_op jit(solution)/shard_map/load/pallas_call | solution.py:80
  10.6 0.1 fusion.118
  10.8 0.8 %collective-permute-done.9.refs_3_ = bf16[32,512]{1,0:T(8,128)(2,1)S(1)} collective-permute-done((bf16[32,512]{1,0:T(8,128)(2,1)S(1)}, bf16[32,512]{1,0:T(8,128)(2,1)S(1)}, u32[]{:S(2)}, u32[]{:S(2)}) %collective-permute-start.9) | collective-permute-done | bytes 32800 | tf_op jit(solution)/shard_map/ppermute | solution.py:737
  11.7 1.6 %collective-permute-start.13 = (bf16[128,16]{1,0:T(8,128)(2,1)S(1)}, bf16[128,16]{1,0:T(8,128)(2,1)S(1)}, u32[]{:S(2)}, u32[]{:S(2)}) collective-permute-start(bf16[128,16]{1,0:T(8,128)(2,1)S(1)} %pad_maximum_fusion.11), channel_id=1, source_target_pairs={{0,1},{1,2},{2,3},{3,0},{4,5},{5,6},{6,7},{7,4},{8,9},{9,10},{10,1... | collective-permute-start | bytes 12296 | tf_op jit(solution)/shard_map/ppermute | solution.py:656
  13.3 2.3 %collective-permute-start.14 = (bf16[128,16]{1,0:T(8,128)(2,1)S(1)}, bf16[128,16]{1,0:T(8,128)(2,1)S(1)}, u32[]{:S(2)}, u32[]{:S(2)}) collective-permute-start(bf16[128,16]{1,0:T(8,128)(2,1)S(1)} %pad_maximum_fusion.12), channel_id=1, source_target_pairs={{1,0},{2,1},{3,2},{0,3},{5,4},{6,5},{7,6},{4,7},{9,8},{10,9},{11,1... | collective-permute-start | bytes 12296 | tf_op jit(solution)/shard_map/ppermute | solution.py:660
  15.6 1.8 %contract_multi.1 = (bf16[2048,128]{1,0:T(8,128)(2,1)S(1)}, f32[512,128]{1,0:T(8,128)S(1)}, bf16[56,512,128]{2,1,0:T(8,128)(2,1)S(1)}) custom-call(s32[1]{0:T(128)} %bitcast.62.place, f32[96,128]{1,0:T(8,128)S(1)} %get-tuple-element.98.band, f32[2,96]{1,0:T(2,128)S(1)} %get-tuple-element.99.response, ...), custom_call_target="tpu_custom_call", output_to_operand_aliasing={{2}: (5, {})} | custom-call | flops 536870912 | bytes 8388608 | tf_op jit(solution)/shard_map/contract_multi/pallas_call | solution.py:142
  17.5 2.4 %collective-permute-start.11 = (bf16[512,128]{1,0:T(8,128)(2,1)S(1)}, bf16[512,128]{1,0:T(8,128)(2,1)S(1)}, u32[]{:S(2)}, u32[]{:S(2)}) collective-permute-start(bf16[512,128]{1,0:T(8,128)(2,1)S(1)} %get-tuple-element.240), channel_id=1, source_target_pairs={{0,2},{1,3},{2,0},{3,1},{4,6},{5,7},{6,4},{7,5},{8,10},{9,11},{10,... | collective-permute-start | bytes 393224 | tf_op jit(solution)/shard_map/ppermute | solution.py:772
  19.9 1.5 %collective-permute-start.12 = (bf16[512,128]{1,0:T(8,128)(2,1)S(1)}, bf16[512,128]{1,0:T(8,128)(2,1)S(1)}, u32[]{:S(2)}, u32[]{:S(2)}) collective-permute-start(bf16[512,128]{1,0:T(8,128)(2,1)S(1)} %get-tuple-element.239), channel_id=1, source_target_pairs={{0,3},{1,0},{2,1},{3,2},{4,7},{5,4},{6,5},{7,6},{8,11},{9,8},{10,9... | collective-permute-start | bytes 393224 | tf_op jit(solution)/shard_map/ppermute | solution.py:772
  21.3 4.6 %contract_hyper.1 = (bf16[512,128]{1,0:T(8,128)(2,1)S(1)}, bf16[144,128]{1,0:T(8,128)(2,1)S(1)}) custom-call(s32[1]{0:T(128)} %bitcast.62.place, f32[17]{0:T(128)S(1)} %select_reduce_fusion.taps, f32[512,128]{1,0:T(8,128)S(1)} %get-tuple-element.105.columns, bf16[128,16]{1,0:T(8,128)(2,1)S(1)} %collective-permute-done.13.before, ...), custom_call_target="tpu_custom_call" | custom-call | tf_op jit(solution)/shard_map/contract_hyper/pallas_call | solution.py:227
  26.0 0.6 %collective-permute-start.15 = (bf16[272,128]{1,0:T(8,128)(2,1)S(1)}, bf16[272,128]{1,0:T(8,128)(2,1)S(1)}, u32[]{:S(2)}, u32[]{:S(2)}) collective-permute-start(bf16[272,128]{1,0:T(8,128)(2,1)S(1)} %get-tuple-element.247), channel_id=1, source_target_pairs={{0,1},{1,2},{2,3},{3,0},{4,5},{5,6},{6,7},{7,4},{8,9},{9,10},{10,1... | collective-permute-start | bytes 208904 | tf_op jit(solution)/shard_map/ppermute | solution.py:772
  26.6 1.5 %collective-permute-start.16 = (bf16[272,128]{1,0:T(8,128)(2,1)S(1)}, bf16[272,128]{1,0:T(8,128)(2,1)S(1)}, u32[]{:S(2)}, u32[]{:S(2)}) collective-permute-start(bf16[272,128]{1,0:T(8,128)(2,1)S(1)} %get-tuple-element.246), channel_id=1, source_target_pairs={{0,2},{1,3},{2,0},{3,1},{4,6},{5,7},{6,4},{7,5},{8,10},{9,11},{10,... | collective-permute-start | bytes 208904 | tf_op jit(solution)/shard_map/ppermute | solution.py:772
  28.2 2.8 %collective-permute-start.17 = (bf16[272,128]{1,0:T(8,128)(2,1)S(1)}, bf16[272,128]{1,0:T(8,128)(2,1)S(1)}, u32[]{:S(2)}, u32[]{:S(2)}) collective-permute-start(bf16[272,128]{1,0:T(8,128)(2,1)S(1)} %get-tuple-element.245), channel_id=1, source_target_pairs={{0,3},{1,0},{2,1},{3,2},{4,7},{5,4},{6,5},{7,6},{8,11},{9,8},{10,9... | collective-permute-start | bytes 208904 | tf_op jit(solution)/shard_map/ppermute | solution.py:772
  31.0 0.5 sum_arrived.1
  31.6 0.8 %collective-permute-done.15.refs_4_ = bf16[272,128]{1,0:T(8,128)(2,1)S(1)} collective-permute-done((bf16[272,128]{1,0:T(8,128)(2,1)S(1)}, bf16[272,128]{1,0:T(8,128)(2,1)S(1)}, u32[]{:S(2)}, u32[]{:S(2)}) %collective-permute-start.15) | collective-permute-done | bytes 69664 | tf_op jit(solution)/shard_map/ppermute | solution.py:772
  32.4 4.0 %collective-permute-done.16.refs_5_ = bf16[272,128]{1,0:T(8,128)(2,1)S(1)} collective-permute-done((bf16[272,128]{1,0:T(8,128)(2,1)S(1)}, bf16[272,128]{1,0:T(8,128)(2,1)S(1)}, u32[]{:S(2)}, u32[]{:S(2)}) %collective-permute-start.16) | collective-permute-done | bytes 69664 | tf_op jit(solution)/shard_map/ppermute | solution.py:772
  36.5 1.4 %collective-permute-start.18 = (f32[168,128]{1,0:T(8,128)S(1)}, f32[168,128]{1,0:T(8,128)S(1)}, u32[]{:S(2)}, u32[]{:S(2)}) collective-permute-start(f32[168,128]{1,0:T(8,128)S(1)} %get-tuple-element.111), channel_id=1, source_target_pairs={{0,1},{1,0},{2,3},{3,2},{4,5},{5,4},{6,7},{7,6},{8,9},{9,8},{10,11... | collective-permute-start | bytes 258056 | tf_op jit(solution)/shard_map/ppermute | solution.py:793
  37.8 1.1 %collective-permute-start.19 = (f32[168,128]{1,0:T(8,128)S(1)}, f32[168,128]{1,0:T(8,128)S(1)}, u32[]{:S(2)}, u32[]{:S(2)}) collective-permute-start(f32[168,128]{1,0:T(8,128)S(1)} %get-tuple-element.112), channel_id=1, source_target_pairs={{1,2},{2,1},{3,4},{4,3},{5,6},{6,5},{7,8},{8,7},{9,10},{10,9},{11,... | collective-permute-start | bytes 258056 | tf_op jit(solution)/shard_map/ppermute | solution.py:790
  39.0 1.2 %collective-permute-done.20.other = f32[72,128]{1,0:T(8,128)S(1)} collective-permute-done((f32[72,128]{1,0:T(8,128)S(1)}, f32[72,128]{1,0:T(8,128)S(1)}, u32[]{:S(2)}, u32[]{:S(2)}) %collective-permute-start.20) | collective-permute-done | bytes 36896 | tf_op jit(solution)/shard_map/ppermute | solution.py:737
  40.2 1.4 %make_operator.1 = (f32[128,128]{1,0:T(8,128)S(1)}, f32[128,128]{1,0:T(8,128)S(1)}, bf16[256,256]{1,0:T(8,128)(2,1)S(1)}, bf16[256,256]{1,0:T(8,128)(2,1)S(1)}, f32[8,128]{1,0:T(8,128)S(1)}) custom-call(s32[1]{0:T(128)} %bitcast.62.place, f32[17]{0:T(128)S(1)} %select_reduce_fusion.taps, f32[128,128]{1,0:T(8,128)S(1)} %get-tuple-element.113.band_gram, ...), custom_call_target="tpu_custom_call" | custom-call | bytes 67108864 | tf_op jit(solution)/shard_map/make_operator/pallas_call | solution.py:304
  41.6 3.8 %collective-permute-done.19.second_rows = f32[168,128]{1,0:T(8,128)S(1)} collective-permute-done((f32[168,128]{1,0:T(8,128)S(1)}, f32[168,128]{1,0:T(8,128)S(1)}, u32[]{:S(2)}, u32[]{:S(2)}) %collective-permute-start.19) | collective-permute-done | bytes 86048 | tf_op jit(solution)/shard_map/ppermute | solution.py:790
  45.4 3.5 %make_basis.1 = (f32[6,4,128,128]{3,2,1,0:T(8,128)S(1)}, f32[32,1,128]{2,1,0:T(1,128)}) custom-call(s32[1]{0:T(128)} %bitcast.60.place, f32[17]{0:T(128)S(1)} %select_reduce_fusion.taps, f32[512,128]{1,0:T(8,128)S(1)} %get-tuple-element.104.refs_2_.multi, f32[128,128]{1,0:T(8,128)S(1)} %get-tuple-element.110.hyper, ...), custom_call_target="tpu_custom_call" | custom-call | tf_op jit(solution)/shard_map/make_basis/pallas_call | solution.py:534
  48.9 2.5 %all-to-all-start = ((f32[32,1,128]{2,1,0:T(1,128)}), f32[32,1,128]{2,1,0:T(1,128)S(1)}, u32[]{:S(2)}, u32[]{:S(2)}) async-start(f32[32,1,128]{2,1,0:T(1,128)} %get-tuple-element.119), calls=%async_computation | async-start | bytes 32768 | tf_op jit(solution)/shard_map/all_to_all | solution.py:798
  51.4 7.1 %all-to-all-done.products = f32[32,1,128]{2,1,0:T(1,128)S(1)} async-done(((f32[32,1,128]{2,1,0:T(1,128)}), f32[32,1,128]{2,1,0:T(1,128)S(1)}, u32[]{:S(2)}, u32[]{:S(2)}) %all-to-all-start) | async-done | bytes 16416 | tf_op jit(solution)/shard_map/all_to_all | solution.py:798
  58.5 0.3 make_coefficients.1
  58.9 1.2 %conditional.1 = ((f32[512,128]{1,0:T(8,128)}, f32[512,128]{1,0:T(8,128)})) conditional(s32[]{:T(128)} %bitcast.63, (f32[6,4,128,128]{3,2,1,0:T(8,128)S(1)}, f32[17]{0:T(128)S(1)}, f32[128,128]{1,0:T(8,128)S(1)}, f32[512,128]{1,0:T(8,128)S(1)}, f32[128,128]{1,0:T(8,128)S(1)}, /*index=5*/f32[128,128]{1,0:T(8,128)S(1)}) %tuple.20, ...), branch_computations={%region_1.10_spmd, %region_10.11_spmd} | conditional | flops 257967104 | bytes 23068832 | solution.py:805
  59.1 0.9 %combine.1 = (f32[512,128]{1,0:T(8,128)}, f32[512,128]{1,0:T(8,128)}) custom-call(f32[16,128]{1,0:T(8,128)S(1)} %get-tuple-element.65.coefficients, f32[6,4,128,128]{3,2,1,0:T(8,128)S(1)} %get-tuple-element.66.basis), custom_call_target="tpu_custom_call" | custom-call | tf_op jit(solution)/shard_map/cond/branch_1_fun/combine/pallas_call | solution.py:645
  (24 shorter events, 0.4 us)
Async XLA Ops:
  0.6 2.1 %collective-permute-start.6 = (bf16[16,512]{1,0:T(8,128)(2,1)}, bf16[16,512]{1,0:T(8,128)(2,1)S(1)}, u32[]{:S(2)}, u32[]{:S(2)}) collective-permute-start(bf16[16,512]{1,0:T(8,128)(2,1)} %bitcast.164), channel_id=1, source_target_pairs={{0,4},{4,0},{8,12},{12,8},{16,20},{20,16},{24,28},{28,24},{1,5},{5... | collective-permute-start | bytes 49160 | tf_op jit(solution)/shard_map/ppermute | solution.py:737
  2.7 7.9 %collective-permute-start.7 = (bf16[32,512]{1,0:T(8,128)(2,1)S(1)}, bf16[32,512]{1,0:T(8,128)(2,1)S(1)}, u32[]{:S(2)}, u32[]{:S(2)}) collective-permute-start(bf16[32,512]{1,0:T(8,128)(2,1)S(1)} %pad_maximum_fusion.10.refs_0_), channel_id=1, source_target_pairs={{0,8},{4,12},{8,0},{12,4},{16,24},{20,28},{24,16},{28,20},{1,9},{5... | collective-permute-start | bytes 98312 | tf_op jit(solution)/shard_map/ppermute | solution.py:737
  5.3 5.5 %collective-permute-start.8 = (bf16[32,512]{1,0:T(8,128)(2,1)S(1)}, bf16[32,512]{1,0:T(8,128)(2,1)S(1)}, u32[]{:S(2)}, u32[]{:S(2)}) collective-permute-start(bf16[32,512]{1,0:T(8,128)(2,1)S(1)} %pad_maximum_fusion.10.refs_0_), channel_id=1, source_target_pairs={{0,16},{4,20},{8,24},{12,28},{16,0},{20,4},{24,8},{28,12},{1,17},{... | collective-permute-start | bytes 98312 | tf_op jit(solution)/shard_map/ppermute | solution.py:737
  6.8 4.8 %collective-permute-start.9 = (bf16[32,512]{1,0:T(8,128)(2,1)S(1)}, bf16[32,512]{1,0:T(8,128)(2,1)S(1)}, u32[]{:S(2)}, u32[]{:S(2)}) collective-permute-start(bf16[32,512]{1,0:T(8,128)(2,1)S(1)} %pad_maximum_fusion.10.refs_0_), channel_id=1, source_target_pairs={{0,24},{4,28},{8,16},{12,20},{16,8},{20,12},{24,0},{28,4},{1,25},{... | collective-permute-start | bytes 98312 | tf_op jit(solution)/shard_map/ppermute | solution.py:737
  11.7 9.6 %collective-permute-start.13 = (bf16[128,16]{1,0:T(8,128)(2,1)S(1)}, bf16[128,16]{1,0:T(8,128)(2,1)S(1)}, u32[]{:S(2)}, u32[]{:S(2)}) collective-permute-start(bf16[128,16]{1,0:T(8,128)(2,1)S(1)} %pad_maximum_fusion.11), channel_id=1, source_target_pairs={{0,1},{1,2},{2,3},{3,0},{4,5},{5,6},{6,7},{7,4},{8,9},{9,10},{10,1... | collective-permute-start | bytes 12296 | tf_op jit(solution)/shard_map/ppermute | solution.py:656
  13.3 8.0 %collective-permute-start.14 = (bf16[128,16]{1,0:T(8,128)(2,1)S(1)}, bf16[128,16]{1,0:T(8,128)(2,1)S(1)}, u32[]{:S(2)}, u32[]{:S(2)}) collective-permute-start(bf16[128,16]{1,0:T(8,128)(2,1)S(1)} %pad_maximum_fusion.12), channel_id=1, source_target_pairs={{1,0},{2,1},{3,2},{0,3},{5,4},{6,5},{7,6},{4,7},{9,8},{10,9},{11,1... | collective-permute-start | bytes 12296 | tf_op jit(solution)/shard_map/ppermute | solution.py:660
  17.5 10.7 %collective-permute-start.10 = (bf16[512,128]{1,0:T(8,128)(2,1)S(1)}, bf16[512,128]{1,0:T(8,128)(2,1)S(1)}, u32[]{:S(2)}, u32[]{:S(2)}) collective-permute-start(bf16[512,128]{1,0:T(8,128)(2,1)S(1)} %get-tuple-element.241), channel_id=1, source_target_pairs={{0,1},{1,2},{2,3},{3,0},{4,5},{5,6},{6,7},{7,4},{8,9},{9,10},{10,1... | collective-permute-start | bytes 393224 | tf_op jit(solution)/shard_map/ppermute | solution.py:772
  17.5 13.5 %collective-permute-start.11 = (bf16[512,128]{1,0:T(8,128)(2,1)S(1)}, bf16[512,128]{1,0:T(8,128)(2,1)S(1)}, u32[]{:S(2)}, u32[]{:S(2)}) collective-permute-start(bf16[512,128]{1,0:T(8,128)(2,1)S(1)} %get-tuple-element.240), channel_id=1, source_target_pairs={{0,2},{1,3},{2,0},{3,1},{4,6},{5,7},{6,4},{7,5},{8,10},{9,11},{10,... | collective-permute-start | bytes 393224 | tf_op jit(solution)/shard_map/ppermute | solution.py:772
  19.9 11.1 %collective-permute-start.12 = (bf16[512,128]{1,0:T(8,128)(2,1)S(1)}, bf16[512,128]{1,0:T(8,128)(2,1)S(1)}, u32[]{:S(2)}, u32[]{:S(2)}) collective-permute-start(bf16[512,128]{1,0:T(8,128)(2,1)S(1)} %get-tuple-element.239), channel_id=1, source_target_pairs={{0,3},{1,0},{2,1},{3,2},{4,7},{5,4},{6,5},{7,6},{8,11},{9,8},{10,9... | collective-permute-start | bytes 393224 | tf_op jit(solution)/shard_map/ppermute | solution.py:772
  26.0 6.3 %collective-permute-start.15 = (bf16[272,128]{1,0:T(8,128)(2,1)S(1)}, bf16[272,128]{1,0:T(8,128)(2,1)S(1)}, u32[]{:S(2)}, u32[]{:S(2)}) collective-permute-start(bf16[272,128]{1,0:T(8,128)(2,1)S(1)} %get-tuple-element.247), channel_id=1, source_target_pairs={{0,1},{1,2},{2,3},{3,0},{4,5},{5,6},{6,7},{7,4},{8,9},{9,10},{10,1... | collective-permute-start | bytes 208904 | tf_op jit(solution)/shard_map/ppermute | solution.py:772
  26.6 9.8 %collective-permute-start.16 = (bf16[272,128]{1,0:T(8,128)(2,1)S(1)}, bf16[272,128]{1,0:T(8,128)(2,1)S(1)}, u32[]{:S(2)}, u32[]{:S(2)}) collective-permute-start(bf16[272,128]{1,0:T(8,128)(2,1)S(1)} %get-tuple-element.246), channel_id=1, source_target_pairs={{0,2},{1,3},{2,0},{3,1},{4,6},{5,7},{6,4},{7,5},{8,10},{9,11},{10,... | collective-permute-start | bytes 208904 | tf_op jit(solution)/shard_map/ppermute | solution.py:772
  28.2 8.2 %collective-permute-start.17 = (bf16[272,128]{1,0:T(8,128)(2,1)S(1)}, bf16[272,128]{1,0:T(8,128)(2,1)S(1)}, u32[]{:S(2)}, u32[]{:S(2)}) collective-permute-start(bf16[272,128]{1,0:T(8,128)(2,1)S(1)} %get-tuple-element.245), channel_id=1, source_target_pairs={{0,3},{1,0},{2,1},{3,2},{4,7},{5,4},{6,5},{7,6},{8,11},{9,8},{10,9... | collective-permute-start | bytes 208904 | tf_op jit(solution)/shard_map/ppermute | solution.py:772
  36.5 5.1 %collective-permute-start.18 = (f32[168,128]{1,0:T(8,128)S(1)}, f32[168,128]{1,0:T(8,128)S(1)}, u32[]{:S(2)}, u32[]{:S(2)}) collective-permute-start(f32[168,128]{1,0:T(8,128)S(1)} %get-tuple-element.111), channel_id=1, source_target_pairs={{0,1},{1,0},{2,3},{3,2},{4,5},{5,4},{6,7},{7,6},{8,9},{9,8},{10,11... | collective-permute-start | bytes 258056 | tf_op jit(solution)/shard_map/ppermute | solution.py:793
  37.8 7.6 %collective-permute-start.19 = (f32[168,128]{1,0:T(8,128)S(1)}, f32[168,128]{1,0:T(8,128)S(1)}, u32[]{:S(2)}, u32[]{:S(2)}) collective-permute-start(f32[168,128]{1,0:T(8,128)S(1)} %get-tuple-element.112), channel_id=1, source_target_pairs={{1,2},{2,1},{3,4},{4,3},{5,6},{6,5},{7,8},{8,7},{9,10},{10,9},{11,... | collective-permute-start | bytes 258056 | tf_op jit(solution)/shard_map/ppermute | solution.py:790
  38.9 1.2 %collective-permute-start.20 = (f32[72,128]{1,0:T(8,128)S(1)}, f32[72,128]{1,0:T(8,128)S(1)}, u32[]{:S(2)}, u32[]{:S(2)}) collective-permute-start(f32[72,128]{1,0:T(8,128)S(1)} %get-tuple-element.115.own), channel_id=1, source_target_pairs={{0,4},{4,0},{8,12},{12,8},{16,20},{20,16},{24,28},{28,24},{1,5},{5... | collective-permute-start | bytes 110600 | tf_op jit(solution)/shard_map/ppermute | solution.py:737
  48.9 9.6 %all-to-all-start = ((f32[32,1,128]{2,1,0:T(1,128)}), f32[32,1,128]{2,1,0:T(1,128)S(1)}, u32[]{:S(2)}, u32[]{:S(2)}) async-start(f32[32,1,128]{2,1,0:T(1,128)} %get-tuple-element.119), calls=%async_computation | async-start | bytes 32768 | tf_op jit(solution)/shard_map/all_to_all | solution.py:798
